TPU v7x, 32 devices: a whole 2x2x4 slice. The times are simulated.
32 devices in a mesh: grp: 2 (over y), pb: 4 (over z), ea: 2 (over x), ma: 2 (over core).
Axes of the slice: x: 2, y: 2, z: 4, core: 2. Of those that a mesh axis runs over, the one named last changes fastest.
Arguments:
- table: bfloat16 [2, 4, 4, 60, 1024], P(None, 'pb', 'ea', 'ma'), may hold values from -1.5 to 1.5
- r_el: int32 [4, 3], P('ea'), may hold values from -6 to 6
- r_ph: int32 [4, 3], replicated, may hold values from -6 to 6
- k_coords: int32 [8, 3], P('grp'), parts along dimension 0, may hold values from 0 to 47
- q_coords: int32 [192, 3], P(('grp', 'pb')), parts along dimension 0, may hold values from 0 to 47
- u_k: bfloat16 [2, 8, 32, 32], P(None, ('grp', 'ea')), parts along dimension 1, may hold values from -0.75 to 0.75
- u_kq: bfloat16 [2, 192, 4, 32, 32], P(None, ('grp', 'pb', 'ma'), 'ea'), parts along dimension 1, may hold values from -0.75 to 0.75
- modes_q: bfloat16 [2, 192, 60, 60], P(None, ('grp', 'pb', 'ma')), parts along dimension 1, may hold values from -0.5 to 0.5
- weights_q: float32 [192, 60], P(('grp', 'pb', 'ma')), parts along dimension 0, may hold values from 0.2 to 6
Outputs:
- coupling_sq: bfloat16 [192, 4, 60, 1024], P(('grp', 'pb', 'ma'), 'ea'), parts along dimension 0
- kernel: float32 [8, 1024], P(('grp', 'ea')), parts along dimension 0
There are 2 independent parts, one for each index of `grp`. A program takes and returns all parts, laid end to end along the dimension named above; an argument that names none is the same for every part. Nothing has to cross between parts.
All inputs are finite; a program needn't handle non-finite values.
Results may differ from a plain program's by a relative error of at most 0.0084.
Values may be sent and summed in bfloat16 or wider, within the bound.
No kernel may reach another device: no remote copies, remote signals or barrier semaphores. Data moves between devices by JAX's collectives and lax.ppermute only.
A program may use at most 128 MiB of HBM per device.

v0:
```python
import math

import jax
import jax.numpy as jnp
from jax import lax
from jax.sharding import PartitionSpec as P

GRID = 48


def phase_pair(coords, vectors):
    turns = jnp.mod(jnp.sum(coords[:, None, :] * vectors[None, :, :], axis=-1), GRID)
    angles = turns.astype(jnp.float32) * (2.0 * math.pi / GRID)
    return (jnp.cos(angles), jnp.sin(angles))


def rotation_block(cos_part, sin_part):
    return jnp.stack([jnp.stack([cos_part, -sin_part], 1), jnp.stack([sin_part, cos_part], 1)], 0)


def body(table, r_el, r_ph, k_coords, q_coords, u_k, u_kq, modes_q, weights_q):
    k_rows = u_k.shape[1]
    q_rows = u_kq.shape[1]
    width = u_k.shape[2]
    half_modes = table.shape[3]
    modes_all = 2 * half_modes
    pairs = table.shape[4]
    full_table, full_vectors = (
        lax.all_gather(table, "ea", axis=2, tiled=True),
        lax.all_gather(r_el, "ea", axis=0, tiled=True),
    )
    own_k = lax.dynamic_slice_in_dim(k_coords, lax.axis_index("ea") * k_rows, k_rows, 0)
    electron = rotation_block(*phase_pair(own_k, full_vectors)).astype(jnp.bfloat16)
    by_k = jnp.einsum(
        "dkce,cpemx->kdpmx", electron, full_table, preferred_element_type=jnp.float32
    ).astype(jnp.bfloat16)
    all_modes = lax.all_gather(by_k, "ma", axis=3, tiled=True)
    every_row = lax.all_gather(all_modes, "pb", axis=2, tiled=True)
    own_coords = lax.dynamic_slice_in_dim(q_coords, lax.axis_index("ma") * q_rows, q_rows, 0)
    phonon = rotation_block(*phase_pair(own_coords, r_ph)).astype(jnp.bfloat16)
    summed = jnp.einsum(
        "dqcp,kcpmx->dqkmx", phonon, every_row, preferred_element_type=jnp.float32
    ).astype(jnp.bfloat16)
    shaped = summed.reshape(2, q_rows, k_rows, modes_all, width, width)
    right_block = jnp.stack([jnp.stack([u_k[0], u_k[1]], 2), jnp.stack([-u_k[1], u_k[0]], 2)], 0)
    right = jnp.einsum(
        "cqkamn,cknds->dqkams", shaped, right_block, preferred_element_type=jnp.float32
    ).astype(jnp.bfloat16)
    flipped = jnp.swapaxes(u_kq, -1, -2)
    left_block = jnp.stack(
        [jnp.stack([flipped[0], flipped[1]], 3), jnp.stack([-flipped[1], flipped[0]], 3)], 0
    )
    band = jnp.einsum(
        "dqkrcm,cqkams->dqkars", left_block, right, preferred_element_type=jnp.float32
    ).astype(jnp.bfloat16)
    band = band.reshape(2, q_rows, k_rows, modes_all, pairs)
    mode_block = jnp.stack(
        [jnp.stack([modes_q[0], modes_q[1]], 2), jnp.stack([-modes_q[1], modes_q[0]], 2)], 0
    )
    coupling = jnp.einsum(
        "cqkax,cqadv->dqkvx", band, mode_block, preferred_element_type=jnp.float32
    )
    squared = coupling[0] * coupling[0] + coupling[1] * coupling[1]
    weighted = jnp.sum(weights_q[:, None, :, None] * squared, axis=(0, 2))
    total_weighted = lax.psum(weighted, ("pb", "ma"))
    kernel = total_weighted / (q_rows * lax.axis_size("pb") * lax.axis_size("ma") * modes_all)
    return (squared.astype(jnp.bfloat16), kernel)


def solution(mesh):
    return jax.shard_map(
        body,
        mesh=mesh,
        in_specs=(
            P(None, "pb", "ea", "ma", None),
            P("ea", None),
            P(),
            P("grp", None),
            P(("grp", "pb"), None),
            P(None, ("grp", "ea"), None, None),
            P(None, ("grp", "pb", "ma"), "ea", None, None),
            P(None, ("grp", "pb", "ma"), None, None),
            P(("grp", "pb", "ma"), None),
        ),
        out_specs=(P(("grp", "pb", "ma"), "ea", None, None), P(("grp", "ea"), None)),
        check_vma=False,
    )
```

profile of v0, /device:TPU:0, one launch (start us, length us, event | category | flops | bytes accessed | tf_op | source)
XLA Modules:
  0.0 180.5 jit_solution(977138418767455567)
XLA Ops:
  7.2 0.0 copy-start
  7.2 0.0 all-gather.3.cloned.1.call-start
  7.2 0.7 constant_dynamic-slice_fusion
  7.9 0.1 copy.70
  8.0 5.4 %all-gather = s32[2,2,3]{2,1,0:T(2,128)S(1)} all-gather(s32[1,2,3]{2,1,0:T(2,128)} %bitcast.159), channel_id=1, replica_groups=mesh['grp'=2,'pb'=4,'ea'=2,'ma'=2] {'ea'}, dimensions={0}, use_global_device_ids=true | all-gather | bytes 72 | tf_op jit(solution)/shard_map/all_gather | solution.py:30
  13.4 0.1 copy.71
  13.5 0.1 multiply_reduce_fusion.2
  13.6 0.1 negate_convert_fusion.1
  13.7 1.1 copy.76
  14.8 7.5 %all_gather.13 = bf16[2,1,4,30,1024]{4,0,3,1,2:T(2,128)(2,1)S(1)} all-gather(bf16[2,1,2,30,1024]{4,0,3,1,2:T(2,128)(2,1)S(1)} %copy.76), channel_id=1, replica_groups=mesh['grp'=2,'pb'=4,'ea'=2,'ma'=2] {'ea'}, dimensions={2}, use_global_device_ids=true | all-gather | bytes 737280 | tf_op jit(solution)/shard_map/all_gather | solution.py:29
  22.3 0.6 fusion.21
  22.9 2.2 %all_gather.14 = bf16[2,2,1,60,1024]{4,0,3,1,2:T(2,128)(2,1)S(1)} all-gather(bf16[2,2,1,30,1024]{4,0,3,1,2:T(2,128)(2,1)S(1)} %fusion.21), channel_id=1, replica_groups=mesh['grp'=2,'pb'=4,'ea'=2,'ma'=2] {'ma'}, dimensions={3}, use_global_device_ids=true | all-gather | bytes 737280 | tf_op jit(solution)/shard_map/all_gather | solution.py:37
  25.1 1.3 copy.78
  26.4 0.0 all-gather.3.cloned.1.call-update
  26.4 0.8 copy.69
  27.2 0.7 fusion.50
  27.9 0.1 copy.112
  28.0 0.1 copy.111
  28.1 1.2 copy.82
  29.3 1.7 fusion.49
  31.1 0.4 copy.110
  31.4 0.4 copy.109
  31.8 0.0 copy-done
  31.8 0.1 constant_dynamic-slice_fusion.1
  31.9 0.1 multiply_reduce_fusion.1
  32.0 0.1 negate_convert_fusion
  32.2 0.2 maximum_bitcast_fusion.6
  32.4 0.2 maximum_bitcast_fusion.4
  32.5 39.0 %all-gather.3.cloned.1.call-done = bf16[2,2,4,60,1024]{4,1,3,0,2:T(2,128)(2,1)} async-done(((bf16[2,2,1,60,1024]{4,1,3,0,2:T(2,128)(2,1)}), bf16[2,2,4,60,1024]{4,1,3,0,2:T(2,128)(2,1)}) %all-gather.3.cloned.1.call-update) | async-done | bytes 1966096 | tf_op jit(solution)/shard_map/all_gather | solution.py:38
  71.6 8.2 %bitcast_convert_fusion.2 = bf16[2,12,2,60,1024]{4,1,3,2,0:T(8,128)(2,1)} fusion(bf16[2,2,4,60,1024]{4,1,3,0,2:T(2,128)(2,1)} %all-gather.3.cloned.1.call-done, bf16[1,12,2,4]{1,3,2,0:T(4,128)(2,1)S(1)} %get-tuple-element.26, bf16[1,12,2,4]{1,3,2,0:T(4,128)(2,1)S(1)} %get-tuple-element.25), kind=kOutput, calls=%fused_computation.2 | convolution fusion | flops 50135808 | bytes 7864704 | tf_op jit(solution)/shard_map/dqcp,kcpmx->dqkmx/dot_general | solution.py:41
  79.7 15.9 %copy.80 = bf16[2,12,2,60,1024]{3,4,2,1,0:T(8,128)(2,1)} copy(bf16[2,12,2,60,1024]{4,1,3,2,0:T(8,128)(2,1)} %bitcast_convert_fusion.2) | data formatting | bytes 11796480 | tf_op jit(solution)/shard_map/convert_element_type | solution.py:43
  95.6 9.1 %fusion = bf16[2,12,2,60,32,32,1]{3,5,4,1,0,2,6:T(8,128)(2,1)} fusion(bf16[2,12,2,60,32,32,1]{3,5,4,2,1,0,6:T(8,128)(2,1)} %bitcast.151, bf16[1,2,32,2,32]{2,4,0,3,1:T(8,128)(2,1)S(1)} %get-tuple-element.21, bf16[1,2,32,2,32]{2,4,0,3,1:T(8,128)(2,1)S(1)} %get-tuple-element.20), kind=kOutput, calls=%fused_computation.3 | convolution fusion | flops 380469248 | bytes 11812864 | tf_op jit(solution)/shard_map/cqkamn,cknds->dqkams/dot_general | solution.py:46
  104.8 14.1 %fusion.1 = bf16[2,12,2,60,32,32]{3,4,0,5,2,1:T(8,128)(2,1)} fusion(bf16[2,12,2,60,32,32,1]{3,5,4,1,0,2,6:T(8,128)(2,1)} %fusion, bf16[1,12,2,32,2,32]{5,3,4,0,2,1:T(8,128)(2,1)S(1)} %get-tuple-element.17, bf16[1,12,2,32,2,32]{5,3,4,0,2,1:T(8,128)(2,1)S(1)} %get-tuple-element.16), kind=kOutput, calls=%fused_computation.4 | convolution fusion | flops 380829696 | bytes 11993088 | tf_op jit(solution)/shard_map/dqkrcm,cqkams->dqkars/dot_general | solution.py:53
  118.9 13.6 %copy.85 = bf16[2,12,2,60,32,32]{3,5,4,2,1,0:T(8,128)(2,1)} copy(bf16[2,12,2,60,32,32]{3,4,0,5,2,1:T(8,128)(2,1)} %fusion.1) | data formatting | bytes 11796480 | tf_op jit(solution)/shard_map/convert_element_type | solution.py:55
  132.5 13.3 %fusion.14 = f32[2,12,2,60,1024]{4,3,2,0,1:T(8,128)} fusion(bf16[2,12,2,60,1024,1]{3,4,2,1,0,5:T(8,128)(2,1)} %bitcast.150, bf16[1,12,60,2,60]{2,4,0,3,1:T(8,128)(2,1)S(1)} %get-tuple-element.15, bf16[1,12,60,2,60]{2,4,0,3,1:T(8,128)(2,1)S(1)} %get-tuple-element.14), kind=kOutput, calls=%fused_computation.16 | convolution fusion | flops 708480000 | bytes 18040320 | tf_op jit(solution)/shard_map/cqkax,cqadv->dqkvx/dot_general | solution.py:60
  145.8 0.0 copy-start.2
  145.8 0.0 copy-start.3
  145.8 0.0 copy-start.1
  145.8 6.6 %fusion.19 = bf16[12,2,60,1024]{3,2,1,0:T(8,128)(2,1)S(1)} fusion(f32[2,12,2,60,1024]{4,3,2,0,1:T(8,128)} %fusion.14), kind=kLoop, calls=%fused_computation.19 | loop fusion | flops 5898240 | bytes 14745600 | tf_op jit(solution)/shard_map/convert_element_type | solution.py:67
  152.3 4.6 %copy.87 = bf16[12,2,60,1024]{3,1,2,0:T(2,128)(2,1)} copy(bf16[12,2,60,1024]{3,2,1,0:T(8,128)(2,1)S(1)} %fusion.19) | data formatting | bytes 5898240
  157.0 0.0 copy-done.2
  157.0 0.0 copy-done.3
  157.0 1.1 multiply_reduce_fusion
  158.1 14.9 %psum.7 = f32[2,1024]{1,0:T(2,128)S(1)} all-reduce(f32[2,1024]{1,0:T(2,128)S(1)} %multiply_reduce_fusion), channel_id=1, replica_groups=mesh['grp'=2,'pb'=4,'ea'=2,'ma'=2] {'pb','ma'}, use_global_device_ids=true, to_apply=%region_3.4 | all-reduce | flops 2048 | bytes 16384 | tf_op jit(solution)/shard_map/psum | solution.py:65
  173.0 0.6 broadcast_multiply_fusion
  173.6 0.0 copy-done.1
  (7 shorter events, 0.1 us)
Async XLA Ops:
  7.2 24.7 %copy-start = (s32[24,3]{0,1:T(4,128)S(1)}, s32[24,3]{0,1:T(4,128)}, u32[]{:S(2)}) copy-start(s32[24,3]{0,1:T(4,128)} %param.13) | copy-start | bytes 868
  7.2 64.4 %all-gather.3.cloned.1.call-start = ((), (), s32[]{:S(2)}) async-start(), calls=%async_computation | async-start | bytes 2457600 | tf_op jit(solution)/shard_map/all_gather | solution.py:38
  145.8 11.2 %copy-start.2 = (f32[2,12,2,60,1024]{4,3,2,0,1:T(8,128)S(1)}, f32[2,12,2,60,1024]{4,3,2,0,1:T(8,128)}, u32[]{:S(2)}) copy-start(f32[2,12,2,60,1024]{4,3,2,0,1:T(8,128)} %fusion.14) | copy-start | bytes 35389444
  145.8 11.2 %copy-start.3 = (f32[12,60]{1,0:T(8,128)S(1)}, f32[12,60]{1,0:T(8,128)}, u32[]{:S(2)}) copy-start(f32[12,60]{1,0:T(8,128)} %param.17) | copy-start | bytes 8644
  145.8 27.8 %copy-start.1 = (s32[24,3]{0,1:T(4,128)S(1)}, s32[24,3]{0,1:T(4,128)}, u32[]{:S(2)}) copy-start(s32[24,3]{0,1:T(4,128)} %param.13) | copy-start | bytes 868
Sparse Core Ops, SparseCore 0:
  26.5 45.0 all-gather.2
where the time goes:
time: 181 us; the launch traced here: 180 us
  matrix products  45.3 us (25%)
  local copies, waits for them, and re-layouts  43 us (24%)
  waiting for transfers between devices  39 us (22%)
  blocking collectives  30 us (17%)
  between operations  14.2 us (8%)
  other arithmetic  8.99 us (5%)
    all_gather x1, waiting for transfers between devices, body(): every_row = lax.all_gather(all_modes, 'pb', axis=2, tiled=True)  39 us
    convert_element_type x1, local copies, waits for them, and re-layouts, body(): summed = jnp.einsum('dqcp,kcpmx->dqkmx', phonon, every_row, preferred_ele...  15.9 us
    psum x1, blocking collectives, body(): total_weighted = lax.psum(weighted, ('pb', 'ma'))  14.9 us
    dot_general x1, matrix products, body(): jnp.einsum('dqkrcm,cqkams->dqkars', left_block, right, preferred_element_...  14.1 us
    convert_element_type x1, local copies, waits for them, and re-layouts, body(): band = jnp.einsum('dqkrcm,cqkams->dqkars', left_block, right, preferred_e...  13.6 us
    dot_general x1, matrix products, body(): jnp.einsum('cqkax,cqadv->dqkvx', band, mode_block, preferred_element_type...  13.3 us
    dot_general x1, matrix products, body(): jnp.einsum('cqkamn,cknds->dqkams', shaped, right_block, preferred_element...  9.11 us
    unnamed x17, local copies, waits for them, and re-layouts  8.81 us
  transfers between devices with their start and end apart: 1, of which 1 were waited for; matrix products, arithmetic and copies ran while one was open for 3% of the time, Pallas kernels for 0%

commit v1 on v0

v1 whole, which is shorter than its diff:
```python
import functools
import math

import jax
import jax.numpy as jnp
from jax import lax
from jax.experimental import pallas as pl
from jax.experimental.pallas import tpu as pltpu
from jax.sharding import PartitionSpec as P

GRID = 48
MIB = 1 << 20
NT = (((1,), (1,)), ((), ()))
F32 = jnp.float32
BF16 = jnp.bfloat16
MODE_PAD = 32
BRANCH_PAD = 64
SMEM = pl.BlockSpec(memory_space=pltpu.SMEM)
VMEM = pl.BlockSpec(memory_space=pltpu.VMEM)


def wrap(turns):
    turns = lax.rem(turns, GRID)
    return jnp.where(turns < 0, turns + GRID, turns)


def phases(turns):
    angles = turns.astype(F32) * (2.0 * math.pi / GRID)
    return jnp.cos(angles).astype(BF16).astype(F32), jnp.sin(angles).astype(BF16).astype(F32)


def electron_kernel(n_k, n_src, rows_e, half, place_ref, k_ref, *refs):
    vectors, tables, outs = refs[:n_src], refs[n_src : 2 * n_src], refs[2 * n_src :]
    turns = []
    for k in range(n_k):
        for s in range(n_src):
            for e in range(rows_e):
                row = place_ref[0] * n_k + k
                t = sum(k_ref[row, d] * vectors[s][e, d] for d in range(3))
                turns.append(jnp.full((1, 128), wrap(t), jnp.int32))
    cos, sin = phases(jnp.concatenate(turns, 0))
    wide = half * rows_e
    at = lax.broadcasted_iota(jnp.int32, (MODE_PAD, 2 * wide), 0)
    lane = lax.broadcasted_iota(jnp.int32, (MODE_PAD, 2 * wide), 1)
    imag = lane >= wide
    rest = jnp.where(imag, lane - wide, lane)
    own = rest - at * rows_e
    rows = []
    for k in range(n_k):
        for out in range(2):
            columns = []
            for s in range(n_src):
                value = jnp.zeros((MODE_PAD, 2 * wide), F32)
                for e in range(rows_e):
                    i = (k * n_src + s) * rows_e + e
                    c, d = cos[i : i + 1, : 2 * wide], sin[i : i + 1, : 2 * wide]
                    here = jnp.where(imag, c, d) if out else jnp.where(imag, -d, c)
                    value = jnp.where(own == e, here, value)
                columns.append(value)
            rows.append(jnp.concatenate(columns, 1))
    factor = jnp.concatenate(rows, 0).astype(BF16)
    data = jnp.concatenate(
        [t[c, 0].reshape(wide, t.shape[-1]) for t in tables for c in range(2)], 0
    )
    total = jnp.dot(factor, data, preferred_element_type=F32).astype(BF16)
    for k in range(n_k):
        outs[k][...] = total[k * 2 * MODE_PAD : (k + 1) * 2 * MODE_PAD]


def rotation_kernel(masks, place_ref, r_ref, q_ref, u_k_ref, u_kq_ref, left_ref, kron_ref):
    _, q_rows, n_k, width, _ = u_kq_ref.shape
    lanes = lax.broadcasted_iota(jnp.int32, (1, q_rows * width), 1) // width
    first = place_ref[2] * q_rows
    coords = []
    for d in range(3):
        line = jnp.zeros((1, q_rows * width), jnp.int32)
        for q in range(q_rows):
            line = jnp.where(lanes == q, q_ref[first + q, d], line)
        coords.append(line)
    turns = []
    for mask in masks:
        p = place_ref[1] ^ mask
        turns.append(wrap(sum(coords[d] * r_ref[p, d] for d in range(3))))
    cos, sin = phases(jnp.concatenate(turns, 0))
    row = lax.broadcasted_iota(jnp.int32, (8 * width, 8 * width), 0)
    lane = lax.broadcasted_iota(jnp.int32, (8 * width, 8 * width), 1)
    same = row % 8 == lane // width
    for k in range(n_k):
        ur, ui = (
            jnp.concatenate([u_kq_ref[c, q, k].astype(F32) for q in range(q_rows)], 1)
            for c in range(2)
        )
        parts = []
        for i in range(len(masks)):
            c, s = cos[i : i + 1], sin[i : i + 1]
            parts += [c * ur + s * ui, s * ur - c * ui]
        left_ref[k] = jnp.concatenate(parts, 0).T.astype(BF16)
        for c in range(2):
            u = u_k_ref[c, k].astype(F32).T
            u = jnp.concatenate([u] * 8, 1)
            u = jnp.broadcast_to(u[:, None, :], (width, 8, 8 * width)).reshape(8 * width, 8 * width)
            kron_ref[k, :, c * 8 * width : (c + 1) * 8 * width] = jnp.where(same, u, 0.0).astype(BF16)


def mode_kernel(half, place_ref, modes_ref, weights_ref, mix_ref, column_ref):
    _, q_rows, modes, _ = modes_ref.shape
    first = place_ref[2] == 0
    rows = jnp.zeros((MODE_PAD - half, 2 * BRANCH_PAD), F32)
    gap = jnp.zeros((half, BRANCH_PAD - modes), F32)
    for q in range(q_rows):
        dr, di = modes_ref[0, q].astype(F32), modes_ref[1, q].astype(F32)
        parts = []
        for h in range(2):
            r, i = (jnp.where(first ^ (h == 1), d[:half], d[half:]) for d in (dr, di))
            parts += [jnp.concatenate([r, gap, i, gap], 1), rows]
            parts += [jnp.concatenate([-i, gap, r, gap], 1), rows]
        mix_ref[q] = jnp.concatenate(parts, 0).T.astype(BF16)
    w = weights_ref[...]
    w = jnp.concatenate([w, jnp.zeros((q_rows, 128 - modes), F32)], 1)
    w = jnp.concatenate([w, jnp.zeros((128 - q_rows, 128), F32)], 0).T
    for q in range(q_rows):
        column_ref[q] = w[:BRANCH_PAD, q : q + 1]


def coupling_kernel(n_p, k, width, q_step, modes, count, *refs):
    own, sib = refs[:n_p], refs[n_p : 2 * n_p]
    a_ref, l_ref, d_ref, w_ref = refs[2 * n_p : 2 * n_p + 4]
    out_ref, mean_ref, x2, zs, acc = refs[-5:]
    step = pl.program_id(0)
    q_all = l_ref.shape[1] // width
    pitch = width + 8
    unroll = 4

    @pl.when(step == 0)
    def _():
        acc[...] = jnp.zeros_like(acc)
        a_mat = a_ref[0]
        for p in range(n_p):
            for t in range(width // 16):
                parts = []
                for u in range(2):
                    lanes = pl.ds((2 * t + u) * 8 * width, 8 * width)
                    ys = []
                    for ref in (own[p], sib[p]):
                        y = ref[:, lanes]
                        h = y.shape[0] // 2
                        ys.append((y, jnp.concatenate([-y[h:], y[:h]], 0)))
                    y0 = jnp.concatenate([ys[0][0], ys[1][0]], 0)
                    y1 = jnp.concatenate([ys[0][1], ys[1][1]], 0)
                    rhs = jnp.concatenate(
                        [jnp.concatenate([y0, y1], 1), jnp.concatenate([y1, -y0], 1)], 0
                    )
                    parts.append(lax.dot_general(a_mat, rhs, NT, preferred_element_type=F32))
                for n in range(width):
                    both = jnp.concatenate([part[n * 8 : n * 8 + 8] for part in parts], 0).astype(BF16)
                    for c in range(2):
                        row = (p * 2 + c) * width + t * 16
                        x2[row : row + 16, n * 128 : (n + 1) * 128] = both[:, c * 128 : (c + 1) * 128]

        def columns(i, carry):
            start = pl.multiple_of(i * unroll * 128, unroll * 128)
            z = jnp.dot(l_ref[0], x2[:, pl.ds(start, unroll * 128)], preferred_element_type=F32)
            for u in range(unroll):
                zs[pl.ds(unroll * i + u, q_all * width, stride=pitch), :] = z[:, u * 128 : (u + 1) * 128]
            return carry

        lax.fori_loop(0, width // unroll, columns, 0)

    rows = width * pitch
    total = acc[...]
    for u in range(q_step):
        q = step * q_step + u
        z = zs[pl.ds(pl.multiple_of(q * rows, rows), rows), :]
        z = z.reshape(width, pitch, 128)[:, :width].reshape(width * width, 128).astype(BF16)
        res = lax.dot_general(d_ref[u], z, NT, preferred_element_type=F32)
        sq = res[:BRANCH_PAD] * res[:BRANCH_PAD] + res[BRANCH_PAD:] * res[BRANCH_PAD:]
        out_ref[u, 0] = sq[:modes].astype(BF16)
        weighted = sq * w_ref[u]
        for r in range(BRANCH_PAD // 8):
            total = total + weighted[r * 8 : r * 8 + 8]
    acc[...] = total

    @pl.when(step == pl.num_programs(0) - 1)
    def _():
        mean = jnp.sum(total, 0, keepdims=True) / count
        if k == 0:
            mean_ref[...] = jnp.broadcast_to(mean, mean_ref.shape)
        else:
            mean_ref[...] = refs[2 * n_p + 4][...]
            mean_ref[k : k + 1] = mean


def body(table, r_el, r_ph, k_coords, q_coords, u_k, u_kq, modes_q, weights_q):
    n_ea, n_pb, n_ma = lax.axis_size("ea"), lax.axis_size("pb"), lax.axis_size("ma")
    ea, pb, ma = lax.axis_index("ea"), lax.axis_index("pb"), lax.axis_index("ma")
    k_rows, q_rows, width = u_k.shape[1], u_kq.shape[1], u_k.shape[2]
    rows_e, half, pairs = table.shape[2], table.shape[3], table.shape[4]
    modes = n_ma * half
    place = jnp.stack([ea, pb, ma]).astype(jnp.int32)
    shift = lambda n, s: [(i, (i + s) % n) for i in range(n)]
    flip = lambda n, s: [(i, i ^ s) for i in range(n)]

    table = jnp.transpose(table, (0, 1, 3, 2, 4))
    tables = [table] + [lax.ppermute(table, "ea", shift(n_ea, s)) for s in range(1, n_ea)]
    vectors = [r_el] + [lax.ppermute(r_el, "ea", shift(n_ea, s)) for s in range(1, n_ea)]

    masks = [0]
    distance = n_pb // 2
    while distance:
        masks += [m ^ distance for m in masks]
        distance //= 2

    left, kron = pl.pallas_call(
        functools.partial(rotation_kernel, masks),
        out_shape=[
            jax.ShapeDtypeStruct((k_rows, q_rows * width, n_pb * 2 * width), BF16),
            jax.ShapeDtypeStruct((k_rows, 8 * width, 16 * width), BF16),
        ],
        in_specs=[SMEM, SMEM, SMEM, VMEM, VMEM],
        out_specs=[VMEM, VMEM],
        cost_estimate=pl.CostEstimate(flops=1 << 20, bytes_accessed=4 * MIB, transcendentals=0),
        compiler_params=pltpu.CompilerParams(vmem_limit_bytes=24 * MIB),
        name="rotations",
    )(place, r_ph, q_coords, u_k, u_kq)

    by_k = pl.pallas_call(
        functools.partial(electron_kernel, k_rows, n_ea, rows_e, half),
        out_shape=[jax.ShapeDtypeStruct((2 * MODE_PAD, pairs), BF16)] * k_rows,
        in_specs=[SMEM] * (2 + n_ea) + [VMEM] * n_ea,
        out_specs=[VMEM] * k_rows,
        compiler_params=pltpu.CompilerParams(vmem_limit_bytes=16 * MIB),
        name="electron_sum",
    )(place, k_coords, *vectors, *tables)

    mix, weights = pl.pallas_call(
        functools.partial(mode_kernel, half),
        out_shape=[
            jax.ShapeDtypeStruct((q_rows, 2 * BRANCH_PAD, n_ma * 2 * MODE_PAD), BF16),
            jax.ShapeDtypeStruct((q_rows, BRANCH_PAD, 1), F32),
        ],
        in_specs=[SMEM, VMEM, VMEM],
        out_specs=[VMEM, VMEM],
        cost_estimate=pl.CostEstimate(flops=1 << 20, bytes_accessed=4 * MIB, transcendentals=0),
        compiler_params=pltpu.CompilerParams(vmem_limit_bytes=16 * MIB),
        name="mode_rotation",
    )(place, modes_q, weights_q)

    swap = flip(n_ma, 1)
    blocks = [[y] for y in by_k]
    distance = n_pb // 2
    while distance:
        for held in blocks:
            held += [lax.ppermute(y, "pb", flip(n_pb, distance)) for y in held]
        distance //= 2

    q_step = q_rows // 2 if q_rows % 2 == 0 else q_rows
    out = mean = None
    for k in range(k_rows):
        own = blocks[k]
        sib = [lax.ppermute(y, "ma", swap) for y in own]
        operands = [*own, *sib, kron, left, mix, weights]
        in_specs = (
            [VMEM] * (2 * n_pb)
            + [
                pl.BlockSpec((1, 8 * width, 16 * width), functools.partial(lambda k, i: (k, 0, 0), k)),
                pl.BlockSpec(
                    (1, q_rows * width, n_pb * 2 * width), functools.partial(lambda k, i: (k, 0, 0), k)
                ),
                pl.BlockSpec((q_step, 2 * BRANCH_PAD, n_ma * 2 * MODE_PAD), lambda i: (i, 0, 0)),
                pl.BlockSpec((q_step, BRANCH_PAD, 1), lambda i: (i, 0, 0)),
            ]
        )
        aliases = {}
        if k:
            in_specs += [VMEM, pl.BlockSpec(memory_space=pl.ANY)]
            aliases = {len(operands) + 1: 0}
            operands += [mean, out]
        out, mean = pl.pallas_call(
            functools.partial(
                coupling_kernel, n_pb, k, width, q_step, modes, q_rows * n_pb * n_ma * modes
            ),
            grid=(q_rows // q_step,),
            out_shape=[
                jax.ShapeDtypeStruct((q_rows, k_rows, modes, pairs), BF16),
                jax.ShapeDtypeStruct((k_rows, pairs), F32),
            ],
            in_specs=in_specs,
            out_specs=[
                pl.BlockSpec((q_step, 1, modes, pairs), functools.partial(lambda k, i: (i, k, 0, 0), k)),
                pl.BlockSpec((k_rows, pairs), lambda i: (0, 0)),
            ],
            scratch_shapes=[
                pltpu.VMEM((n_pb * 2 * width, width * 128), BF16),
                pltpu.VMEM((q_rows * width * (width + 8), 128), F32),
                pltpu.VMEM((8, pairs), F32),
            ],
            input_output_aliases=aliases,
            compiler_params=pltpu.CompilerParams(vmem_limit_bytes=(16 + 2 * n_pb) * MIB),
            name="coupling",
        )(*operands)
    mean = mean + lax.ppermute(mean, "ma", swap)
    distance = 1
    while distance < n_pb:
        mean = mean + lax.ppermute(mean, "pb", flip(n_pb, distance))
        distance *= 2
    return (out, mean)


def solution(mesh):
    return jax.shard_map(
        body,
        mesh=mesh,
        in_specs=(
            P(None, "pb", "ea", "ma", None),
            P("ea", None),
            P(),
            P("grp", None),
            P(("grp", "pb"), None),
            P(None, ("grp", "ea"), None, None),
            P(None, ("grp", "pb", "ma"), "ea", None, None),
            P(None, ("grp", "pb", "ma"), None, None),
            P(("grp", "pb", "ma"), None),
        ),
        out_specs=(P(("grp", "pb", "ma"), "ea", None, None), P(("grp", "ea"), None)),
        check_vma=False,
    )
```

time: 181 us -> 65.1 us (0.36)
  matrix products: 45.3 us -> 0 us
  local copies, waits for them, and re-layouts: 43 us -> 11.9 us
  blocking collectives: 30 us -> 0 us
  waiting for transfers between devices: 39 us -> 22.8 us
  starting transfers between devices: 0.04 us -> 15 us
  Pallas kernels: 0 us -> 13.5 us
  between operations: 14.2 us -> 0.76 us
  other arithmetic: 8.99 us -> 0.69 us
    dot_general x5 -> x0, matrix products: 45.3 us -> none  [the longest x1 14.1 us: body(): jnp.einsum('dqkrcm,cqkams->dqkars', left_block, right, preferred_element_...]
    all_gather x1 -> x0, waiting for transfers between devices: 39 us -> none  [body(): every_row = lax.all_gather(all_modes, 'pb', axis=2, tiled=True)]
    convert_element_type x2 -> x0, local copies, waits for them, and re-layouts: 29.5 us -> none  [the longest x1 15.9 us: body(): summed = jnp.einsum('dqcp,kcpmx->dqkmx', phonon, every_row, preferred_ele...]
    ppermute x0 -> x19, waiting for transfers between devices: none -> 22.8 us  [the longest x6 13.5 us: body(): held += [lax.ppermute(y, 'pb', flip(n_pb, distance)) for y in held]]
    all_gather x3 -> x0, blocking collectives: 15.1 us -> none  [the longest x1 7.5 us: body(): lax.all_gather(table, 'ea', axis=2, tiled=True)]
    ppermute x0 -> x19, starting transfers between devices: none -> 15 us  [the longest x6 5.56 us: body(): held += [lax.ppermute(y, 'pb', flip(n_pb, distance)) for y in held]]
    psum x1 -> x0, blocking collectives: 14.9 us -> none  [body(): total_weighted = lax.psum(weighted, ('pb', 'ma'))]
    pallas_call x0 -> x5, Pallas kernels: none -> 13.5 us  [the longest x2 9.94 us: body(): pl.pallas_call(functools.partial(coupling_kernel, n_pb, k, width, q_step,...]
  transfers between devices with their start and end apart: 1 -> 19, of which waited for: 1 -> 7; matrix products, arithmetic and copies ran while one was open for 3% -> 10% of each run, Pallas kernels for 0% -> 12%
where the time goes in v1:
time: 65.1 us; the launch traced here: 64.6 us
  waiting for transfers between devices  22.8 us (35%)
  starting transfers between devices  15 us (23%)
  Pallas kernels  13.5 us (21%)
  local copies, waits for them, and re-layouts  11.9 us (18%)
  between operations  0.76 us (1%)
  other arithmetic  0.69 us (1%)
    ppermute x6, waiting for transfers between devices, body(): held += [lax.ppermute(y, 'pb', flip(n_pb, distance)) for y in held]  13.5 us
    unnamed x17, local copies, waits for them, and re-layouts  11.9 us
    pallas_call x2, Pallas kernels, body(): pl.pallas_call(functools.partial(coupling_kernel, n_pb, k, width, q_step,...  9.94 us
    ppermute x1, waiting for transfers between devices, body(): lax.ppermute(r_el, 'ea', shift(n_ea, s))  6.07 us
    ppermute x6, starting transfers between devices, body(): held += [lax.ppermute(y, 'pb', flip(n_pb, distance)) for y in held]  5.56 us
    ppermute x2, starting transfers between devices, body(): mean = mean + lax.ppermute(mean, 'pb', flip(n_pb, distance))  4.27 us
    ppermute x1, starting transfers between devices, body(): lax.ppermute(table, 'ea', shift(n_ea, s))  3 us
    ppermute x2, waiting for transfers between devices, body(): mean = mean + lax.ppermute(mean, 'pb', flip(n_pb, distance))  2.4 us
  transfers between devices with their start and end apart: 19, of which 7 were waited for; matrix products, arithmetic and copies ran while one was open for 10% of the time, Pallas kernels for 12%

profile of v1, /device:TPU:0, one launch (start us, length us, event | category | flops | bytes accessed | tf_op | source)
XLA Modules:
  0.0 64.6 jit_solution(16977141486865527782)
XLA Ops:
  0.6 3.0 %collective-permute-start.1 = (bf16[2,1,30,2,1024]{4,3,2,1,0:T(2,128)(2,1)}, bf16[2,1,30,2,1024]{4,3,2,1,0:T(2,128)(2,1)S(1)}, u32[]{:S(2)}, u32[]{:S(2)}) collective-permute-start(bf16[2,1,30,2,1024]{4,3,2,1,0:T(2,128)(2,1)} %bitcast.4), channel_id=1, source_target_pairs={{0,2},{2,0},{1,3},{3,1},{4,6},{6,4},{5,7},{7,5},{8,10},{10,8},{9,1... | collective-permute-start | bytes 737288 | tf_op jit(solution)/shard_map/ppermute | solution.py:204
  3.6 0.1 collective-permute-start
  3.7 0.1 pad_add_fusion.place_ref
  3.8 6.1 %collective-permute-done.refs_1_ = s32[2,3]{1,0:T(2,128)S(1)} collective-permute-done((s32[2,3]{1,0:T(2,128)}, s32[2,3]{1,0:T(2,128)S(1)}, u32[]{:S(2)}, u32[]{:S(2)}) %collective-permute-start) | collective-permute-done | bytes 56 | tf_op jit(solution)/shard_map/ppermute | solution.py:205
  9.9 0.0 collective-permute-done.1.refs_3_
  9.9 0.0 copy-start.1
  9.9 0.9 %copy-done.1 = bf16[2,1,2,30,1024]{4,2,3,1,0:T(2,128)(2,1)S(1)} copy-done((bf16[2,1,2,30,1024]{4,2,3,1,0:T(2,128)(2,1)S(1)}, bf16[2,1,2,30,1024]{4,2,3,1,0:T(2,128)(2,1)}, u32[]{:S(2)}) %copy-start.1) | copy-done | bytes 245784
  10.8 0.0 copy-start.4
  10.8 0.7 %copy-done.4 = s32[4,3]{1,0:T(4,128)S(1)} copy-done((s32[4,3]{1,0:T(4,128)S(1)}, s32[4,3]{1,0:T(4,128)}, u32[]{:S(2)}) %copy-start.4) | copy-done | bytes 72
  11.5 0.0 copy-start.6
  11.5 0.7 %copy-done.6 = s32[2,3]{1,0:T(2,128)S(1)} copy-done((s32[2,3]{1,0:T(2,128)S(1)}, s32[2,3]{1,0:T(2,128)}, u32[]{:S(2)}) %copy-start.6) | copy-done | bytes 48
  12.2 1.0 %electron_sum.1 = (bf16[64,1024]{1,0:T(8,128)(2,1)S(1)}, bf16[64,1024]{1,0:T(8,128)(2,1)S(1)}) custom-call(s32[3]{0:T(128)S(1)} %pad_add_fusion.place_ref, s32[4,3]{1,0:T(4,128)S(1)} %copy-done.4, s32[2,3]{1,0:T(2,128)S(1)} %copy-done.6, s32[2,3]{1,0:T(2,128)S(1)} %collective-permute-done.refs_1_, bf16[2,1,30,2,1024]{4,3,2,1,0:T(2,128)(2,1)S(1)} %bitcast.5, ...), custom_call_target="tpu_custom_call" | custom-call | tf_op jit(solution)/shard_map/electron_sum/pallas_call | solution.py:226
  13.1 2.9 %collective-permute-start.9 = (bf16[64,1024]{1,0:T(8,128)(2,1)S(1)}, bf16[64,1024]{1,0:T(8,128)(2,1)S(1)}, u32[]{:S(2)}, u32[]{:S(2)}) collective-permute-start(bf16[64,1024]{1,0:T(8,128)(2,1)S(1)} %get-tuple-element.17.refs_0_), channel_id=1, source_target_pairs={{0,8},{4,12},{8,0},{12,4},{1,9},{5,13},{9,1},{13,5},{2,10},{6,14},... | collective-permute-start | bytes 393224 | tf_op jit(solution)/shard_map/ppermute | solution.py:253
  16.0 0.1 collective-permute-start.2
  16.1 1.8 %collective-permute-start.10 = (bf16[64,1024]{1,0:T(8,128)(2,1)S(1)}, bf16[64,1024]{1,0:T(8,128)(2,1)S(1)}, u32[]{:S(2)}, u32[]{:S(2)}) collective-permute-start(bf16[64,1024]{1,0:T(8,128)(2,1)S(1)} %get-tuple-element.17.refs_0_), channel_id=1, source_target_pairs={{0,4},{4,0},{8,12},{12,8},{1,5},{5,1},{9,13},{13,9},{2,6},{6,2},{1... | collective-permute-start | bytes 393224 | tf_op jit(solution)/shard_map/ppermute | solution.py:253
  17.9 0.2 collective-permute-start.3
  18.2 7.4 %collective-permute-done.9.refs_1_ = bf16[64,1024]{1,0:T(8,128)(2,1)S(1)} collective-permute-done((bf16[64,1024]{1,0:T(8,128)(2,1)S(1)}, bf16[64,1024]{1,0:T(8,128)(2,1)S(1)}, u32[]{:S(2)}, u32[]{:S(2)}) %collective-permute-start.9) | collective-permute-done | bytes 131104 | tf_op jit(solution)/shard_map/ppermute | solution.py:253
  25.6 0.0 collective-permute-start.11
  25.6 0.0 collective-permute-start.12
  25.6 1.7 %collective-permute-done.2.refs_1_ = bf16[64,1024]{1,0:T(8,128)(2,1)S(1)} collective-permute-done((bf16[64,1024]{1,0:T(8,128)(2,1)S(1)}, bf16[64,1024]{1,0:T(8,128)(2,1)S(1)}, u32[]{:S(2)}, u32[]{:S(2)}) %collective-permute-start.2) | collective-permute-done | bytes 131104 | tf_op jit(solution)/shard_map/ppermute | solution.py:253
  27.3 0.5 collective-permute-start.4
  27.8 0.0 collective-permute-done.10.refs_2_
  27.8 0.0 collective-permute-start.14
  27.8 0.0 collective-permute-done.3.refs_2_
  27.8 0.5 collective-permute-start.13
  28.3 3.5 %collective-permute-done.11.refs_3_ = bf16[64,1024]{1,0:T(8,128)(2,1)S(1)} collective-permute-done((bf16[64,1024]{1,0:T(8,128)(2,1)S(1)}, bf16[64,1024]{1,0:T(8,128)(2,1)S(1)}, u32[]{:S(2)}, u32[]{:S(2)}) %collective-permute-start.11) | collective-permute-done | bytes 131104 | tf_op jit(solution)/shard_map/ppermute | solution.py:253
  31.8 0.0 collective-permute-start.15
  31.8 0.0 collective-permute-done.12.refs_4_
  31.8 0.5 collective-permute-start.5
  32.3 0.9 %collective-permute-done.4.refs_3_ = bf16[64,1024]{1,0:T(8,128)(2,1)S(1)} collective-permute-done((bf16[64,1024]{1,0:T(8,128)(2,1)S(1)}, bf16[64,1024]{1,0:T(8,128)(2,1)S(1)}, u32[]{:S(2)}, u32[]{:S(2)}) %collective-permute-start.4) | collective-permute-done | bytes 131104 | tf_op jit(solution)/shard_map/ppermute | solution.py:253
  33.2 0.0 collective-permute-start.6
  33.2 0.0 collective-permute-done.14.refs_6_
  33.2 0.5 collective-permute-start.7
  33.7 0.0 collective-permute-done.13.refs_5_
  33.7 0.1 collective-permute-start.8
  33.8 0.8 %copy.12.q_ref = s32[24,3]{1,0:T(8,128)S(1)} copy(s32[24,3]{0,1:T(4,128)} %param.13) | data formatting | bytes 576 | tf_op args[4]
  34.6 1.1 %copy.13.modes_ref = bf16[2,12,60,60]{3,2,1,0:T(8,128)(2,1)S(1)} copy(bf16[2,12,60,60]{3,0,2,1:T(2,128)(2,1)} %param.16) | data formatting | bytes 345600 | tf_op args[7]
  35.6 0.0 copy-start.3
  35.6 0.7 %copy-done.3 = f32[12,60]{1,0:T(8,128)S(1)} copy-done((f32[12,60]{1,0:T(8,128)S(1)}, f32[12,60]{1,0:T(8,128)}, u32[]{:S(2)}) %copy-start.3) | copy-done | bytes 2904
  36.3 1.2 %mode_rotation.1 = (bf16[12,128,128]{2,1,0:T(8,128)(2,1)S(1)}, f32[12,64,1]{2,1,0:T(8,128)S(1)}) custom-call(s32[3]{0:T(128)S(1)} %pad_add_fusion.place_ref, bf16[2,12,60,60]{3,2,1,0:T(8,128)(2,1)S(1)} %copy.13.modes_ref, f32[12,60]{1,0:T(8,128)S(1)} %copy-done.3), custom_call_target="tpu_custom_call" | custom-call | flops 1048576 | bytes 4194304 | tf_op jit(solution)/shard_map/mode_rotation/pallas_call | solution.py:235
  37.5 0.0 copy-start
  37.5 1.0 %copy-done = bf16[2,12,2,32,32]{4,3,2,1,0:T(8,128)(2,1)S(1)} copy-done((bf16[2,12,2,32,32]{4,3,2,1,0:T(8,128)(2,1)S(1)}, bf16[2,12,2,32,32]{4,3,2,1,0:T(8,128)(2,1)}, u32[]{:S(2)}) %copy-start) | copy-done | bytes 98328
  38.5 0.0 copy-start.2
  38.5 0.8 %copy-done.2 = bf16[2,2,32,32]{3,2,1,0:T(8,128)(2,1)S(1)} copy-done((bf16[2,2,32,32]{3,2,1,0:T(8,128)(2,1)S(1)}, bf16[2,2,32,32]{3,2,1,0:T(8,128)(2,1)}, u32[]{:S(2)}) %copy-start.2) | copy-done | bytes 8216
  39.3 0.0 copy-start.5
  39.3 0.7 %copy-done.5 = s32[4,3]{1,0:T(4,128)S(1)} copy-done((s32[4,3]{1,0:T(4,128)S(1)}, s32[4,3]{1,0:T(4,128)}, u32[]{:S(2)}) %copy-start.5) | copy-done | bytes 72
  39.9 1.4 %rotations.1 = (bf16[2,384,256]{2,1,0:T(8,128)(2,1)S(1)}, bf16[2,256,512]{2,1,0:T(8,128)(2,1)S(1)}) custom-call(s32[3]{0:T(128)S(1)} %pad_add_fusion.place_ref, s32[4,3]{1,0:T(4,128)S(1)} %copy-done.5, s32[24,3]{1,0:T(8,128)S(1)} %copy.12.q_ref, bf16[2,2,32,32]{3,2,1,0:T(8,128)(2,1)S(1)} %copy-done.2, bf16[2,12,2,32,32]{4,3,2,1,0:T(8,128)(2,1)S(1)} %copy-done), custom_call_target="tpu_custom_call" | custom-call | flops 1048576 | bytes 4194304 | tf_op jit(solution)/shard_map/rotations/pallas_call | solution.py:213
  41.3 0.0 collective-permute-done.15.refs_7_
  41.4 5.0 %coupling.2 = (bf16[12,2,60,1024]{3,2,1,0:T(8,128)(2,1)S(1)}, f32[2,1024]{1,0:T(2,128)S(1)}) custom-call(bf16[64,1024]{1,0:T(8,128)(2,1)S(1)} %get-tuple-element.17.refs_0_, bf16[64,1024]{1,0:T(8,128)(2,1)S(1)} %collective-permute-done.9.refs_1_, bf16[64,1024]{1,0:T(8,128)(2,1)S(1)} %collective-permute-done.10.refs_2_, ...), custom_call_target="tpu_custom_call" | custom-call | tf_op jit(solution)/shard_map/coupling/pallas_call | solution.py:278
  46.3 0.0 collective-permute-done.5.refs_4_
  46.3 0.0 collective-permute-done.7.refs_6_
  46.4 0.0 collective-permute-done.6.refs_5_
  46.4 0.0 collective-permute-done.8.refs_7_
  46.4 5.0 %coupling.3 = (bf16[12,2,60,1024]{3,2,1,0:T(8,128)(2,1)S(1)}, f32[2,1024]{1,0:T(2,128)S(1)}) custom-call(bf16[64,1024]{1,0:T(8,128)(2,1)S(1)} %get-tuple-element.12.refs_0_, bf16[64,1024]{1,0:T(8,128)(2,1)S(1)} %collective-permute-done.2.refs_1_, bf16[64,1024]{1,0:T(8,128)(2,1)S(1)} %collective-permute-done.3.refs_2_, ...), custom_call_target="tpu_custom_call", output_to_operand_aliasing={{0}: (13, {})} | custom-call | tf_op jit(solution)/shard_map/coupling/pallas_call | solution.py:278
  51.4 0.5 collective-permute-start.16
  51.9 0.8 %collective-permute-done.16 = f32[2,1024]{1,0:T(2,128)S(1)} collective-permute-done((f32[2,1024]{1,0:T(2,128)S(1)}, f32[2,1024]{1,0:T(2,128)S(1)}, u32[]{:S(2)}, u32[]{:S(2)}) %collective-permute-start.16) | collective-permute-done | bytes 8224 | tf_op jit(solution)/shard_map/ppermute | solution.py:301
  52.7 1.2 %collective-permute-start.17 = (f32[2,1024]{1,0:T(2,128)S(1)}, f32[2,1024]{1,0:T(2,128)S(1)}, u32[]{:S(2)}, u32[]{:S(2)}) collective-permute-start(f32[2,1024]{1,0:T(2,128)S(1)} %add.9), channel_id=1, source_target_pairs={{0,4},{4,0},{8,12},{12,8},{1,5},{5,1},{9,13},{13,9},{2,6},{6,2},{1... | collective-permute-start | bytes 24584 | tf_op jit(solution)/shard_map/ppermute | solution.py:304
  53.9 2.4 %collective-permute-done.17 = f32[2,1024]{1,0:T(2,128)S(1)} collective-permute-done((f32[2,1024]{1,0:T(2,128)S(1)}, f32[2,1024]{1,0:T(2,128)S(1)}, u32[]{:S(2)}, u32[]{:S(2)}) %collective-permute-start.17) | collective-permute-done | bytes 8224 | tf_op jit(solution)/shard_map/ppermute | solution.py:304
  56.4 3.0 %collective-permute-start.18 = (f32[2,1024]{1,0:T(2,128)S(1)}, f32[2,1024]{1,0:T(2,128)S(1)}, u32[]{:S(2)}, u32[]{:S(2)}) collective-permute-start(f32[2,1024]{1,0:T(2,128)S(1)} %add.10), channel_id=1, source_target_pairs={{0,8},{4,12},{8,0},{12,4},{1,9},{5,13},{9,1},{13,5},{2,10},{6,14},... | collective-permute-start | bytes 24584 | tf_op jit(solution)/shard_map/ppermute | solution.py:304
  59.4 4.6 %copy.14 = bf16[12,2,60,1024]{3,1,2,0:T(2,128)(2,1)} copy(bf16[12,2,60,1024]{3,2,1,0:T(8,128)(2,1)S(1)} %get-tuple-element.22) | data formatting | bytes 5898240
  64.0 0.0 collective-permute-done.18
  64.0 0.6 add.11
  (2 shorter events, 0.0 us)
Async XLA Ops:
  0.6 9.2 %collective-permute-start.1 = (bf16[2,1,30,2,1024]{4,3,2,1,0:T(2,128)(2,1)}, bf16[2,1,30,2,1024]{4,3,2,1,0:T(2,128)(2,1)S(1)}, u32[]{:S(2)}, u32[]{:S(2)}) collective-permute-start(bf16[2,1,30,2,1024]{4,3,2,1,0:T(2,128)(2,1)} %bitcast.4), channel_id=1, source_target_pairs={{0,2},{2,0},{1,3},{3,1},{4,6},{6,4},{5,7},{7,5},{8,10},{10,8},{9,1... | collective-permute-start | bytes 737288 | tf_op jit(solution)/shard_map/ppermute | solution.py:204
  3.6 6.2 %collective-permute-start = (s32[2,3]{1,0:T(2,128)}, s32[2,3]{1,0:T(2,128)S(1)}, u32[]{:S(2)}, u32[]{:S(2)}) collective-permute-start(s32[2,3]{1,0:T(2,128)} %refs_0_.1), channel_id=1, source_target_pairs={{0,2},{2,0},{1,3},{3,1},{4,6},{6,4},{5,7},{7,5},{8,10},{10,8},{9,1... | collective-permute-start | bytes 80 | tf_op jit(solution)/shard_map/ppermute | solution.py:205
  9.9 0.9 %copy-start.1 = (bf16[2,1,2,30,1024]{4,2,3,1,0:T(2,128)(2,1)S(1)}, bf16[2,1,2,30,1024]{4,2,3,1,0:T(2,128)(2,1)}, u32[]{:S(2)}) copy-start(bf16[2,1,2,30,1024]{4,2,3,1,0:T(2,128)(2,1)} %param.9) | copy-start | bytes 737284
  10.8 0.7 %copy-start.4 = (s32[4,3]{1,0:T(4,128)S(1)}, s32[4,3]{1,0:T(4,128)}, u32[]{:S(2)}) copy-start(s32[4,3]{1,0:T(4,128)} %k_ref.1) | copy-start | bytes 148
  11.5 0.7 %copy-start.6 = (s32[2,3]{1,0:T(2,128)S(1)}, s32[2,3]{1,0:T(2,128)}, u32[]{:S(2)}) copy-start(s32[2,3]{1,0:T(2,128)} %refs_0_.1) | copy-start | bytes 76
  13.1 12.4 %collective-permute-start.9 = (bf16[64,1024]{1,0:T(8,128)(2,1)S(1)}, bf16[64,1024]{1,0:T(8,128)(2,1)S(1)}, u32[]{:S(2)}, u32[]{:S(2)}) collective-permute-start(bf16[64,1024]{1,0:T(8,128)(2,1)S(1)} %get-tuple-element.17.refs_0_), channel_id=1, source_target_pairs={{0,8},{4,12},{8,0},{12,4},{1,9},{5,13},{9,1},{13,5},{2,10},{6,14},... | collective-permute-start | bytes 393224 | tf_op jit(solution)/shard_map/ppermute | solution.py:253
  16.0 11.2 %collective-permute-start.2 = (bf16[64,1024]{1,0:T(8,128)(2,1)S(1)}, bf16[64,1024]{1,0:T(8,128)(2,1)S(1)}, u32[]{:S(2)}, u32[]{:S(2)}) collective-permute-start(bf16[64,1024]{1,0:T(8,128)(2,1)S(1)} %get-tuple-element.12.refs_0_), channel_id=1, source_target_pairs={{0,8},{4,12},{8,0},{12,4},{1,9},{5,13},{9,1},{13,5},{2,10},{6,14},... | collective-permute-start | bytes 393224 | tf_op jit(solution)/shard_map/ppermute | solution.py:253
  16.1 11.7 %collective-permute-start.10 = (bf16[64,1024]{1,0:T(8,128)(2,1)S(1)}, bf16[64,1024]{1,0:T(8,128)(2,1)S(1)}, u32[]{:S(2)}, u32[]{:S(2)}) collective-permute-start(bf16[64,1024]{1,0:T(8,128)(2,1)S(1)} %get-tuple-element.17.refs_0_), channel_id=1, source_target_pairs={{0,4},{4,0},{8,12},{12,8},{1,5},{5,1},{9,13},{13,9},{2,6},{6,2},{1... | collective-permute-start | bytes 393224 | tf_op jit(solution)/shard_map/ppermute | solution.py:253
  17.9 9.9 %collective-permute-start.3 = (bf16[64,1024]{1,0:T(8,128)(2,1)S(1)}, bf16[64,1024]{1,0:T(8,128)(2,1)S(1)}, u32[]{:S(2)}, u32[]{:S(2)}) collective-permute-start(bf16[64,1024]{1,0:T(8,128)(2,1)S(1)} %get-tuple-element.12.refs_0_), channel_id=1, source_target_pairs={{0,4},{4,0},{8,12},{12,8},{1,5},{5,1},{9,13},{13,9},{2,6},{6,2},{1... | collective-permute-start | bytes 393224 | tf_op jit(solution)/shard_map/ppermute | solution.py:253
  25.6 6.2 %collective-permute-start.11 = (bf16[64,1024]{1,0:T(8,128)(2,1)S(1)}, bf16[64,1024]{1,0:T(8,128)(2,1)S(1)}, u32[]{:S(2)}, u32[]{:S(2)}) collective-permute-start(bf16[64,1024]{1,0:T(8,128)(2,1)S(1)} %collective-permute-done.9.refs_1_), channel_id=1, source_target_pairs={{0,4},{4,0},{8,12},{12,8},{1,5},{5,1},{9,13},{13,9},{2,6},{6,2},{1... | collective-permute-start | bytes 393224 | tf_op jit(solution)/shard_map/ppermute | solution.py:253
  25.6 6.2 %collective-permute-start.12 = (bf16[64,1024]{1,0:T(8,128)(2,1)S(1)}, bf16[64,1024]{1,0:T(8,128)(2,1)S(1)}, u32[]{:S(2)}, u32[]{:S(2)}) collective-permute-start(bf16[64,1024]{1,0:T(8,128)(2,1)S(1)} %get-tuple-element.17.refs_0_), channel_id=1, source_target_pairs={{0,1},{1,0},{2,3},{3,2},{4,5},{5,4},{6,7},{7,6},{8,9},{9,8},{10,11... | collective-permute-start | bytes 393224 | tf_op jit(solution)/shard_map/ppermute | solution.py:260
  27.3 5.9 %collective-permute-start.4 = (bf16[64,1024]{1,0:T(8,128)(2,1)S(1)}, bf16[64,1024]{1,0:T(8,128)(2,1)S(1)}, u32[]{:S(2)}, u32[]{:S(2)}) collective-permute-start(bf16[64,1024]{1,0:T(8,128)(2,1)S(1)} %collective-permute-done.2.refs_1_), channel_id=1, source_target_pairs={{0,4},{4,0},{8,12},{12,8},{1,5},{5,1},{9,13},{13,9},{2,6},{6,2},{1... | collective-permute-start | bytes 393224 | tf_op jit(solution)/shard_map/ppermute | solution.py:253
  27.8 5.4 %collective-permute-start.14 = (bf16[64,1024]{1,0:T(8,128)(2,1)S(1)}, bf16[64,1024]{1,0:T(8,128)(2,1)S(1)}, u32[]{:S(2)}, u32[]{:S(2)}) collective-permute-start(bf16[64,1024]{1,0:T(8,128)(2,1)S(1)} %collective-permute-done.10.refs_2_), channel_id=1, source_target_pairs={{0,1},{1,0},{2,3},{3,2},{4,5},{5,4},{6,7},{7,6},{8,9},{9,8},{10,11... | collective-permute-start | bytes 393224 | tf_op jit(solution)/shard_map/ppermute | solution.py:260
  27.8 5.9 %collective-permute-start.13 = (bf16[64,1024]{1,0:T(8,128)(2,1)S(1)}, bf16[64,1024]{1,0:T(8,128)(2,1)S(1)}, u32[]{:S(2)}, u32[]{:S(2)}) collective-permute-start(bf16[64,1024]{1,0:T(8,128)(2,1)S(1)} %collective-permute-done.9.refs_1_), channel_id=1, source_target_pairs={{0,1},{1,0},{2,3},{3,2},{4,5},{5,4},{6,7},{7,6},{8,9},{9,8},{10,11... | collective-permute-start | bytes 393224 | tf_op jit(solution)/shard_map/ppermute | solution.py:260
  31.8 9.5 %collective-permute-start.15 = (bf16[64,1024]{1,0:T(8,128)(2,1)S(1)}, bf16[64,1024]{1,0:T(8,128)(2,1)S(1)}, u32[]{:S(2)}, u32[]{:S(2)}) collective-permute-start(bf16[64,1024]{1,0:T(8,128)(2,1)S(1)} %collective-permute-done.11.refs_3_), channel_id=1, source_target_pairs={{0,1},{1,0},{2,3},{3,2},{4,5},{5,4},{6,7},{7,6},{8,9},{9,8},{10,11... | collective-permute-start | bytes 393224 | tf_op jit(solution)/shard_map/ppermute | solution.py:260
  31.8 14.5 %collective-permute-start.5 = (bf16[64,1024]{1,0:T(8,128)(2,1)S(1)}, bf16[64,1024]{1,0:T(8,128)(2,1)S(1)}, u32[]{:S(2)}, u32[]{:S(2)}) collective-permute-start(bf16[64,1024]{1,0:T(8,128)(2,1)S(1)} %get-tuple-element.12.refs_0_), channel_id=1, source_target_pairs={{0,1},{1,0},{2,3},{3,2},{4,5},{5,4},{6,7},{7,6},{8,9},{9,8},{10,11... | collective-permute-start | bytes 393224 | tf_op jit(solution)/shard_map/ppermute | solution.py:260
  33.2 13.2 %collective-permute-start.6 = (bf16[64,1024]{1,0:T(8,128)(2,1)S(1)}, bf16[64,1024]{1,0:T(8,128)(2,1)S(1)}, u32[]{:S(2)}, u32[]{:S(2)}) collective-permute-start(bf16[64,1024]{1,0:T(8,128)(2,1)S(1)} %collective-permute-done.2.refs_1_), channel_id=1, source_target_pairs={{0,1},{1,0},{2,3},{3,2},{4,5},{5,4},{6,7},{7,6},{8,9},{9,8},{10,11... | collective-permute-start | bytes 393224 | tf_op jit(solution)/shard_map/ppermute | solution.py:260
  33.2 13.1 %collective-permute-start.7 = (bf16[64,1024]{1,0:T(8,128)(2,1)S(1)}, bf16[64,1024]{1,0:T(8,128)(2,1)S(1)}, u32[]{:S(2)}, u32[]{:S(2)}) collective-permute-start(bf16[64,1024]{1,0:T(8,128)(2,1)S(1)} %collective-permute-done.3.refs_2_), channel_id=1, source_target_pairs={{0,1},{1,0},{2,3},{3,2},{4,5},{5,4},{6,7},{7,6},{8,9},{9,8},{10,11... | collective-permute-start | bytes 393224 | tf_op jit(solution)/shard_map/ppermute | solution.py:260
  33.7 12.6 %collective-permute-start.8 = (bf16[64,1024]{1,0:T(8,128)(2,1)S(1)}, bf16[64,1024]{1,0:T(8,128)(2,1)S(1)}, u32[]{:S(2)}, u32[]{:S(2)}) collective-permute-start(bf16[64,1024]{1,0:T(8,128)(2,1)S(1)} %collective-permute-done.4.refs_3_), channel_id=1, source_target_pairs={{0,1},{1,0},{2,3},{3,2},{4,5},{5,4},{6,7},{7,6},{8,9},{9,8},{10,11... | collective-permute-start | bytes 393224 | tf_op jit(solution)/shard_map/ppermute | solution.py:260
  35.6 0.7 %copy-start.3 = (f32[12,60]{1,0:T(8,128)S(1)}, f32[12,60]{1,0:T(8,128)}, u32[]{:S(2)}) copy-start(f32[12,60]{1,0:T(8,128)} %weights_ref.1) | copy-start | bytes 8644
  37.5 1.0 %copy-start = (bf16[2,12,2,32,32]{4,3,2,1,0:T(8,128)(2,1)S(1)}, bf16[2,12,2,32,32]{4,3,2,1,0:T(8,128)(2,1)}, u32[]{:S(2)}) copy-start(bf16[2,12,2,32,32]{4,3,2,1,0:T(8,128)(2,1)} %u_kq_ref.1) | copy-start | bytes 294916
  38.5 0.8 %copy-start.2 = (bf16[2,2,32,32]{3,2,1,0:T(8,128)(2,1)S(1)}, bf16[2,2,32,32]{3,2,1,0:T(8,128)(2,1)}, u32[]{:S(2)}) copy-start(bf16[2,2,32,32]{3,2,1,0:T(8,128)(2,1)} %u_k_ref.1) | copy-start | bytes 24580
  39.3 0.7 %copy-start.5 = (s32[4,3]{1,0:T(4,128)S(1)}, s32[4,3]{1,0:T(4,128)}, u32[]{:S(2)}) copy-start(s32[4,3]{1,0:T(4,128)} %r_ref.1) | copy-start | bytes 148
  51.4 1.3 %collective-permute-start.16 = (f32[2,1024]{1,0:T(2,128)S(1)}, f32[2,1024]{1,0:T(2,128)S(1)}, u32[]{:S(2)}, u32[]{:S(2)}) collective-permute-start(f32[2,1024]{1,0:T(2,128)S(1)} %get-tuple-element.21), channel_id=1, source_target_pairs={{0,1},{1,0},{2,3},{3,2},{4,5},{5,4},{6,7},{7,6},{8,9},{9,8},{10,11... | collective-permute-start | bytes 24584 | tf_op jit(solution)/shard_map/ppermute | solution.py:301
  52.7 3.7 %collective-permute-start.17 = (f32[2,1024]{1,0:T(2,128)S(1)}, f32[2,1024]{1,0:T(2,128)S(1)}, u32[]{:S(2)}, u32[]{:S(2)}) collective-permute-start(f32[2,1024]{1,0:T(2,128)S(1)} %add.9), channel_id=1, source_target_pairs={{0,4},{4,0},{8,12},{12,8},{1,5},{5,1},{9,13},{13,9},{2,6},{6,2},{1... | collective-permute-start | bytes 24584 | tf_op jit(solution)/shard_map/ppermute | solution.py:304
  56.4 7.7 %collective-permute-start.18 = (f32[2,1024]{1,0:T(2,128)S(1)}, f32[2,1024]{1,0:T(2,128)S(1)}, u32[]{:S(2)}, u32[]{:S(2)}) collective-permute-start(f32[2,1024]{1,0:T(2,128)S(1)} %add.10), channel_id=1, source_target_pairs={{0,8},{4,12},{8,0},{12,4},{1,9},{5,13},{9,1},{13,5},{2,10},{6,14},... | collective-permute-start | bytes 24584 | tf_op jit(solution)/shard_map/ppermute | solution.py:304

commit v2 on v1

v2 whole, which is shorter than its diff:
```python
import functools
import math

import jax
import jax.numpy as jnp
from jax import lax
from jax.experimental import pallas as pl
from jax.experimental.pallas import tpu as pltpu
from jax.sharding import PartitionSpec as P

GRID = 48
MIB = 1 << 20
NT = (((1,), (1,)), ((), ()))
F32 = jnp.float32
BF16 = jnp.bfloat16
MODE_PAD = 32
BRANCH_PAD = 64
SMEM = pl.BlockSpec(memory_space=pltpu.SMEM)
VMEM = pl.BlockSpec(memory_space=pltpu.VMEM)
HBM = pl.BlockSpec(memory_space=pltpu.HBM)


def cost(us):
    return pl.CostEstimate(flops=us * 1_000_000_000, bytes_accessed=us * 3_000_000, transcendentals=0)


def wrap(turns):
    turns = lax.rem(turns, GRID)
    return jnp.where(turns < 0, turns + GRID, turns)


def phases(turns):
    angles = turns.astype(F32) * (2.0 * math.pi / GRID)
    return jnp.cos(angles).astype(BF16).astype(F32), jnp.sin(angles).astype(BF16).astype(F32)


def phase_kernel(n_k, n_ea, rows_e, half, coords_ref, factor_ref):
    here, core = lax.axis_index("ea"), lax.axis_index("ma")
    turns = []
    for s in range(n_ea):
        for i in range(n_k):
            row = lax.rem(here + s, n_ea) * n_k + lax.rem(core + i, n_k)
            for e in range(rows_e):
                t = sum(coords_ref[row, d] * coords_ref[n_ea * n_k + e, d] for d in range(3))
                turns.append(jnp.full((1, 128), wrap(t), jnp.int32))
    cos, sin = phases(jnp.concatenate(turns, 0))
    wide = half * rows_e
    at = lax.broadcasted_iota(jnp.int32, (MODE_PAD, 2 * wide), 0)
    lane = lax.broadcasted_iota(jnp.int32, (MODE_PAD, 2 * wide), 1)
    imag = lane >= wide
    own = jnp.where(imag, lane - wide, lane) - at * rows_e
    rows = []
    for i in range(n_ea * n_k):
        for out in range(2):
            value = jnp.zeros((MODE_PAD, 2 * wide), F32)
            for e in range(rows_e):
                j = i * rows_e + e
                c, d = cos[j : j + 1, : 2 * wide], sin[j : j + 1, : 2 * wide]
                value = jnp.where(own == e, jnp.where(imag, c, d) if out else jnp.where(imag, -d, c), value)
            rows.append(value)
    factor_ref[...] = jnp.concatenate(rows, 0).astype(BF16)


def electron_kernel(factor_ref, table_ref, *outs):
    _, _, half, rows_e, pairs = table_ref.shape
    data = jnp.concatenate([table_ref[c, 0].reshape(half * rows_e, pairs) for c in range(2)], 0)
    total = jnp.dot(factor_ref[...], data, preferred_element_type=F32)
    for i, out in enumerate(outs):
        out[...] = total[i * 2 * MODE_PAD : (i + 1) * 2 * MODE_PAD].astype(out.dtype)


def rotation_kernel(masks, r_ref, q_ref, u_k_ref, u_kq_ref, left_ref, kron_ref):
    _, q_rows, n_k, width, _ = u_kq_ref.shape
    lanes = lax.broadcasted_iota(jnp.int32, (1, q_rows * width), 1) // width
    first = lax.axis_index("ma") * q_rows
    coords = []
    for d in range(3):
        line = jnp.zeros((1, q_rows * width), jnp.int32)
        for q in range(q_rows):
            line = jnp.where(lanes == q, q_ref[d, first + q], line)
        coords.append(line)
    turns = []
    for mask in masks:
        p = lax.axis_index("pb") ^ mask
        turns.append(wrap(sum(coords[d] * r_ref[p, d] for d in range(3))))
    cos, sin = phases(jnp.concatenate(turns, 0))
    row = lax.broadcasted_iota(jnp.int32, (8 * width, 8 * width), 0)
    lane = lax.broadcasted_iota(jnp.int32, (8 * width, 8 * width), 1)
    same = row % 8 == lane // width
    for k in range(n_k):
        at = lax.rem(lax.axis_index("ma") + k, n_k)
        ur, ui = (
            jnp.concatenate([u_kq_ref[c, q, at].astype(F32) for q in range(q_rows)], 1)
            for c in range(2)
        )
        parts = []
        for i in range(len(masks)):
            c, s = cos[i : i + 1], sin[i : i + 1]
            parts += [c * ur + s * ui, s * ur - c * ui]
        left_ref[k] = jnp.concatenate(parts, 0).T.astype(BF16)
        for c in range(2):
            u = u_k_ref[c, at].astype(F32).T
            u = jnp.concatenate([u] * 8, 1)
            u = jnp.broadcast_to(u[:, None, :], (width, 8, 8 * width)).reshape(8 * width, 8 * width)
            kron_ref[k, :, c * 8 * width : (c + 1) * 8 * width] = jnp.where(same, u, 0.0).astype(BF16)


def mode_kernel(half, modes_ref, weights_ref, mix_ref, column_ref):
    _, q_rows, modes, _ = modes_ref.shape
    first = lax.axis_index("ma") == 0
    rows = jnp.zeros((MODE_PAD - half, 2 * BRANCH_PAD), F32)
    gap = jnp.zeros((half, BRANCH_PAD - modes), F32)
    for q in range(q_rows):
        dr, di = modes_ref[0, q].astype(F32), modes_ref[1, q].astype(F32)
        parts = []
        for h in range(2):
            r, i = (jnp.where(first ^ (h == 1), d[:half], d[half:]) for d in (dr, di))
            parts += [jnp.concatenate([r, gap, i, gap], 1), rows]
            parts += [jnp.concatenate([-i, gap, r, gap], 1), rows]
        mix_ref[q] = jnp.concatenate(parts, 0).T.astype(BF16)
    w = weights_ref[...]
    w = jnp.concatenate([w, jnp.zeros((q_rows, 128 - modes), F32)], 1)
    w = jnp.concatenate([w, jnp.zeros((128 - q_rows, 128), F32)], 0).T
    for q in range(q_rows):
        column_ref[q] = w[:BRANCH_PAD, q : q + 1]


def lift(a_mat, y_refs, x_ref, first_row, width):
    quarter = MODE_PAD
    for t in range(width // 16):
        parts = []
        for u in range(2):
            lanes = slice((2 * t + u) * 8 * width, (2 * t + u + 1) * 8 * width)
            p = [ref[i * quarter : (i + 1) * quarter, lanes] for ref in y_refs for i in range(2)]
            y = jnp.concatenate(p, 0)
            turned = jnp.concatenate([-p[1], p[0], -p[3], p[2]], 0)
            rhs = jnp.concatenate(
                [jnp.concatenate([y, turned], 1), jnp.concatenate([turned, -y], 1)], 0
            )
            parts.append(lax.dot_general(a_mat, rhs, NT, preferred_element_type=F32))
        for n in range(width):
            both = jnp.concatenate([part[n * 8 : n * 8 + 8] for part in parts], 0).astype(BF16)
            for c in range(2):
                row = first_row + c * width + t * 16
                x_ref[row : row + 16, n * 128 : (n + 1) * 128] = both[:, c * 128 : (c + 1) * 128]


def lift_kernel(k, width, a_ref, *refs):
    for i in range(0, len(refs) - 1, 2):
        lift(a_ref[k], refs[i : i + 2], refs[-1], i * width, width)


def coupling_kernel(
    k, width, modes, count, early_ref, y0_ref, y1_ref, a_ref, l_ref, d_ref, w_ref, out_ref, mean_ref, late, zs
):
    q_rows = l_ref.shape[1] // width
    pitch = width + 8
    unroll = width if l_ref.shape[2] <= 512 else 4
    lift(a_ref[k], (y0_ref, y1_ref), late, 0, width)

    def columns(i):
        start = i * unroll * 128
        if not isinstance(start, int):
            start = pl.multiple_of(start, unroll * 128)
        lanes = pl.ds(start, unroll * 128)
        x = jnp.concatenate([early_ref[:, lanes], late[:, lanes]], 0)
        z = jnp.dot(l_ref[k], x, preferred_element_type=F32)
        for u in range(unroll):
            zs[pl.ds(unroll * i + u, q_rows * width, stride=pitch), :] = z[:, u * 128 : (u + 1) * 128]

    if unroll == width:
        columns(0)
    else:
        pl.loop(0, width // unroll)(columns)

    rows = width * pitch
    total = jnp.zeros((8, width * width), F32)
    for q in range(q_rows):
        z = zs[q * rows : (q + 1) * rows, :].reshape(width, pitch, 128)[:, :width]
        z = z.reshape(width * width, 128).astype(BF16)
        res = lax.dot_general(d_ref[q], z, NT, preferred_element_type=F32)
        sq = res[:BRANCH_PAD] * res[:BRANCH_PAD] + res[BRANCH_PAD:] * res[BRANCH_PAD:]
        out_ref[q] = sq[:modes].astype(BF16)
        weighted = sq * w_ref[q]
        for r in range(BRANCH_PAD // 8):
            total = total + weighted[r * 8 : r * 8 + 8]
    mean_ref[...] = jnp.sum(total, 0, keepdims=True) / count


def order_kernel(first_ref, second_ref, *refs):
    out_ref = refs[-1]
    first = lax.axis_index("ma") == 0
    for q in range(out_ref.shape[0]):
        mine, other = first_ref[q], second_ref[q]
        both = jnp.stack([jnp.where(first, mine, other), jnp.where(first, other, mine)])
        out_ref[q] = jnp.swapaxes(both, 0, 1)


def body(table, r_el, r_ph, k_coords, q_coords, u_k, u_kq, modes_q, weights_q):
    n_ea, n_pb, n_ma = lax.axis_size("ea"), lax.axis_size("pb"), lax.axis_size("ma")
    k_rows, q_rows, width = u_k.shape[1], u_kq.shape[1], u_k.shape[2]
    rows_e, half, pairs = table.shape[2], table.shape[3], table.shape[4]
    modes = n_ma * half
    shift = lambda n, s: [(i, (i + s) % n) for i in range(n)]
    flip = lambda n, s: [(i, i ^ s) for i in range(n)]

    table = jnp.transpose(table, (0, 1, 3, 2, 4))
    n_parts = n_ea * k_rows
    factor = pl.pallas_call(
        functools.partial(phase_kernel, k_rows, n_ea, rows_e, half),
        out_shape=jax.ShapeDtypeStruct((n_parts * 2 * MODE_PAD, 2 * half * rows_e), BF16),
        in_specs=[SMEM],
        out_specs=VMEM,
        cost_estimate=cost(2),
        compiler_params=pltpu.CompilerParams(vmem_limit_bytes=16 * MIB),
        name="electron_phases",
    )(jnp.concatenate([k_coords, r_el]))
    parts = pl.pallas_call(
        electron_kernel,
        out_shape=[
            jax.ShapeDtypeStruct((2 * MODE_PAD, pairs), F32 if i < k_rows else BF16)
            for i in range(n_parts)
        ],
        in_specs=[VMEM, VMEM],
        out_specs=[VMEM] * n_parts,
        cost_estimate=cost(2),
        compiler_params=pltpu.CompilerParams(vmem_limit_bytes=16 * MIB),
        name="electron_sum",
    )(factor, table)
    mine, other = [parts[0]], [lax.ppermute(parts[1], "ma", flip(n_ma, 1))]
    for s in range(1, n_ea):
        cross = [
            (e * n_ma + c, (e + s) % n_ea * n_ma + (c ^ 1)) for e in range(n_ea) for c in range(n_ma)
        ]
        mine.append(lax.ppermute(parts[s * k_rows], "ea", shift(n_ea, s)))
        other.append(lax.ppermute(parts[s * k_rows + 1], ("ea", "ma"), cross))

    masks = [0]
    distance = n_pb // 2
    while distance:
        masks += [m ^ distance for m in masks]
        distance //= 2

    left, kron = pl.pallas_call(
        functools.partial(rotation_kernel, masks),
        out_shape=[
            jax.ShapeDtypeStruct((k_rows, q_rows * width, n_pb * 2 * width), BF16),
            jax.ShapeDtypeStruct((k_rows, 8 * width, 16 * width), BF16),
        ],
        in_specs=[SMEM, SMEM, VMEM, VMEM],
        out_specs=[VMEM, VMEM],
        cost_estimate=cost(2),
        compiler_params=pltpu.CompilerParams(vmem_limit_bytes=24 * MIB),
        name="rotations",
    )(r_ph, q_coords.T, u_k, u_kq)

    mix, weights = pl.pallas_call(
        functools.partial(mode_kernel, half),
        out_shape=[
            jax.ShapeDtypeStruct((q_rows, 2 * BRANCH_PAD, n_ma * 2 * MODE_PAD), BF16),
            jax.ShapeDtypeStruct((q_rows, BRANCH_PAD, 1), F32),
        ],
        in_specs=[VMEM, VMEM],
        out_specs=[VMEM, VMEM],
        cost_estimate=cost(2),
        compiler_params=pltpu.CompilerParams(vmem_limit_bytes=16 * MIB),
        name="mode_rotation",
    )(modes_q, weights_q)

    mine[0], left, kron = lax.optimization_barrier((mine[0], left, kron))
    by_k = [sum(y.astype(F32) for y in part).astype(BF16) for part in (mine, other)]

    swap = flip(n_ma, 1)
    halves = [[y] for y in by_k]
    distance = n_pb // 2
    while distance:
        for half_blocks in halves:
            half_blocks += [lax.ppermute(y, "pb", flip(n_pb, distance)) for y in half_blocks]
        distance //= 2
    held = [y for pair in zip(*halves) for y in pair]
    swapped = [lax.ppermute(y, "ma", swap) for y in held]
    swapped = [swapped[i ^ 1] for i in range(len(swapped))]

    results = []
    for k, blocks in enumerate((held, swapped)):
        early = pl.pallas_call(
            functools.partial(lift_kernel, k, width),
            out_shape=jax.ShapeDtypeStruct(((n_pb - 1) * 2 * width, width * 128), BF16),
            in_specs=[VMEM] * (2 * n_pb - 1),
            out_specs=VMEM,
            cost_estimate=cost(1),
            compiler_params=pltpu.CompilerParams(vmem_limit_bytes=(4 + n_pb) * MIB),
            name="lift",
        )(kron, *blocks[:-2])
        results.append(
            pl.pallas_call(
                functools.partial(
                    coupling_kernel, k, width, modes, q_rows * n_pb * n_ma * modes
                ),
                out_shape=[
                    jax.ShapeDtypeStruct((q_rows, modes, pairs), BF16),
                    jax.ShapeDtypeStruct((1, pairs), F32),
                ],
                in_specs=[VMEM] * 7,
                out_specs=[VMEM, VMEM],
                scratch_shapes=[
                    pltpu.VMEM((2 * width, width * 128), BF16),
                    pltpu.VMEM((q_rows * width * (width + 8), 128), F32),
                ],
                cost_estimate=cost(4),
                compiler_params=pltpu.CompilerParams(vmem_limit_bytes=(14 + n_pb) * MIB),
                name="coupling",
            )(early, *blocks[-2:], kron, left, mix, weights)
        )
    (first, mean), (second, rest) = results
    core = lax.axis_index("ma")
    mean = jnp.where(core == 0, jnp.concatenate([mean, rest]), jnp.concatenate([rest, mean]))

    pieces = 2 if q_rows % 2 == 0 else 1
    out = None
    for i in range(pieces):
        block = (q_rows // pieces, modes, pairs)
        at = functools.partial(lambda i, j: (i, 0, 0), i)
        operands = [first, second] + ([] if out is None else [out])
        out = pl.pallas_call(
            order_kernel,
            grid=(1,),
            out_shape=jax.ShapeDtypeStruct((q_rows, modes, k_rows, pairs), BF16),
            in_specs=[pl.BlockSpec(block, at)] * 2 + [pl.BlockSpec(memory_space=pl.ANY)] * (i > 0),
            out_specs=pl.BlockSpec(
                (q_rows // pieces, modes, k_rows, pairs),
                functools.partial(lambda i, j: (i, 0, 0, 0), i),
            ),
            input_output_aliases={2: 0} if i else {},
            cost_estimate=cost(2),
            compiler_params=pltpu.CompilerParams(vmem_limit_bytes=16 * MIB),
            name="order",
        )(*operands)
    out = jnp.transpose(out, (0, 2, 1, 3))
    mean = mean + lax.ppermute(mean, "ma", swap)
    distance = 1
    while distance < n_pb:
        mean = mean + lax.ppermute(mean, "pb", flip(n_pb, distance))
        distance *= 2
    return (out, mean)


def solution(mesh):
    return jax.shard_map(
        body,
        mesh=mesh,
        in_specs=(
            P(None, "pb", "ea", "ma", None),
            P("ea", None),
            P(),
            P("grp", None),
            P(("grp", "pb"), None),
            P(None, ("grp", "ea"), None, None),
            P(None, ("grp", "pb", "ma"), "ea", None, None),
            P(None, ("grp", "pb", "ma"), None, None),
            P(("grp", "pb", "ma"), None),
        ),
        out_specs=(P(("grp", "pb", "ma"), "ea", None, None), P(("grp", "ea"), None)),
        check_vma=False,
    )
```

time: 65.1 us -> 46.5 us (0.71)
  local copies, waits for them, and re-layouts: 11.9 us -> 0.32 us
  waiting for transfers between devices: 22.8 us -> 14.9 us
  starting transfers between devices: 15 us -> 15.8 us
  other arithmetic: 0.69 us -> 1.43 us
    unnamed x17 -> x15, local copies, waits for them, and re-layouts: 11.9 us -> 0.32 us
    ppermute x16 -> x17, waiting for transfers between devices: 19.6 us -> 11.4 us  [the longest x6 8.94 us: body(): lax.ppermute(y, 'pb', flip(n_pb, distance))]
    ppermute x16 -> x17, starting transfers between devices: 10.2 us -> 12.5 us  [the longest x6 7.82 us: body(): lax.ppermute(y, 'pb', flip(n_pb, distance))]
    ppermute x2, starting transfers between devices: 4.27 us -> 2.69 us  [body(): mean = mean + lax.ppermute(mean, 'pb', flip(n_pb, distance))]
    concatenate x0 -> x1, other arithmetic: none -> 0.71 us  [body(): jnp.concatenate([k_coords, r_el])]
    pallas_call x3 -> x8, Pallas kernels: 10.9 us -> 11.2 us  [the longest x2 5.22 us: body(): pl.pallas_call(functools.partial(coupling_kernel, k, width, modes, q_rows...]
  transfers between devices with their start and end apart: 19 -> 20, of which waited for: 7 -> 9; matrix products, arithmetic and copies ran while one was open for 10% -> 0% of each run, Pallas kernels for 12% -> 20%
where the time goes in v2:
time: 46.5 us; the launch traced here: 46.4 us
  starting transfers between devices  15.8 us (34%)
  waiting for transfers between devices  14.9 us (32%)
  Pallas kernels  13.1 us (28%)
  other arithmetic  1.43 us (3%)
  between operations  0.83 us (2%)
    ppermute x6, waiting for transfers between devices, body(): lax.ppermute(y, 'pb', flip(n_pb, distance))  8.94 us
    ppermute x6, starting transfers between devices, body(): lax.ppermute(y, 'pb', flip(n_pb, distance))  7.82 us
    pallas_call x2, Pallas kernels, body(): pl.pallas_call(functools.partial(coupling_kernel, k, width, modes, q_rows...  5.22 us
    ppermute x1, starting transfers between devices, body(): mine.append(lax.ppermute(parts[s * k_rows], 'ea', shift(n_ea, s)))  3 us
    pallas_call x2, Pallas kernels, body(): pl.pallas_call(order_kernel, grid=(1,), out_shape=jax.ShapeDtypeStruct((q...  2.97 us
    ppermute x2, starting transfers between devices, body(): mean = mean + lax.ppermute(mean, 'pb', flip(n_pb, distance))  2.69 us
    ppermute x2, waiting for transfers between devices, body(): mean = mean + lax.ppermute(mean, 'pb', flip(n_pb, distance))  2.66 us
    ppermute x1, waiting for transfers between devices, body(): mine.append(lax.ppermute(parts[s * k_rows], 'ea', shift(n_ea, s)))  2.42 us
  transfers between devices with their start and end apart: 20, of which 9 were waited for; matrix products, arithmetic and copies ran while one was open for 0% of the time, Pallas kernels for 20%

profile of v2, /device:TPU:0, one launch (start us, length us, event | category | flops | bytes accessed | tf_op | source)
XLA Modules:
  0.0 46.4 jit_solution(11690046723762957935)
XLA Ops:
  0.6 0.7 %pad_add_fusion.coords_ref = s32[6,3]{1,0:T(8,128)S(1)} fusion(s32[2,3]{1,0:T(2,128)} %param.10, s32[4,3]{1,0:T(4,128)} %param.12), kind=kLoop, calls=%fused_computation.3 | loop fusion | flops 18 | bytes 144 | tf_op jit(solution)/shard_map/concatenate | solution.py:217
  1.3 0.0 copy-start.1
  1.3 0.7 %electron_phases.1.factor_ref = bf16[256,120]{1,0:T(8,128)(2,1)S(1)} custom-call(s32[6,3]{1,0:T(8,128)S(1)} %pad_add_fusion.coords_ref), custom_call_target="tpu_custom_call" | custom-call | flops 2000000000 | bytes 6000000 | tf_op jit(solution)/shard_map/electron_phases/pallas_call | solution.py:209
  2.1 0.2 copy-done.1
  2.3 0.0 copy-start
  2.3 0.3 electron_sum.1
  2.6 3.0 %collective-permute-start = (bf16[64,1024]{1,0:T(8,128)(2,1)S(1)}, bf16[64,1024]{1,0:T(8,128)(2,1)S(1)}, u32[]{:S(2)}, u32[]{:S(2)}) collective-permute-start(bf16[64,1024]{1,0:T(8,128)(2,1)S(1)} %get-tuple-element.22), channel_id=1, source_target_pairs={{0,2},{2,0},{1,3},{3,1},{4,6},{6,4},{5,7},{7,5},{8,10},{10,8},{9,1... | collective-permute-start | bytes 393224 | tf_op jit(solution)/shard_map/ppermute | solution.py:235
  5.6 0.0 collective-permute-start.2
  5.6 0.2 collective-permute-start.1
  5.8 0.0 copy-done
  5.8 0.0 copy-done.2
  5.8 0.0 copy-done.4
  5.8 0.0 copy-done.5
  5.8 0.0 copy-start.6
  5.8 1.3 %rotations.1 = (bf16[2,384,256]{2,1,0:T(8,128)(2,1)S(1)}, bf16[2,256,512]{2,1,0:T(8,128)(2,1)S(1)}) custom-call(s32[4,3]{1,0:T(4,128)S(1)} %copy-done.4, s32[3,24]{1,0:T(4,128)S(1)} %bitcast.4, bf16[2,2,32,32]{3,2,1,0:T(8,128)(2,1)S(1)} %copy-done.2, bf16[2,12,2,32,32]{4,3,2,1,0:T(8,128)(2,1)S(1)} %copy-done), custom_call_target="tpu_custom_call" | custom-call | flops 2000000000 | bytes 6000000 | tf_op jit(solution)/shard_map/rotations/pallas_call | solution.py:244
  7.1 0.0 copy-start.3
  7.1 2.4 %collective-permute-done = bf16[64,1024]{1,0:T(8,128)(2,1)S(1)} collective-permute-done((bf16[64,1024]{1,0:T(8,128)(2,1)S(1)}, bf16[64,1024]{1,0:T(8,128)(2,1)S(1)}, u32[]{:S(2)}, u32[]{:S(2)}) %collective-permute-start) | collective-permute-done | bytes 131104 | tf_op jit(solution)/shard_map/ppermute | solution.py:235
  9.6 2.2 %collective-permute-start.5 = (bf16[64,1024]{1,0:T(8,128)(2,1)S(1)}, bf16[64,1024]{1,0:T(8,128)(2,1)S(1)}, u32[]{:S(2)}, u32[]{:S(2)}) collective-permute-start(bf16[64,1024]{1,0:T(8,128)(2,1)S(1)} %add_convert_fusion.1.refs_0_), channel_id=1, source_target_pairs={{0,4},{4,0},{8,12},{12,8},{1,5},{5,1},{9,13},{13,9},{2,6},{6,2},{1... | collective-permute-start | bytes 393224 | tf_op jit(solution)/shard_map/ppermute | solution.py:278
  11.8 2.6 %collective-permute-start.3 = (bf16[64,1024]{1,0:T(8,128)(2,1)S(1)}, bf16[64,1024]{1,0:T(8,128)(2,1)S(1)}, u32[]{:S(2)}, u32[]{:S(2)}) collective-permute-start(bf16[64,1024]{1,0:T(8,128)(2,1)S(1)} %add_convert_fusion.1.refs_0_), channel_id=1, source_target_pairs={{0,8},{4,12},{8,0},{12,4},{1,9},{5,13},{9,1},{13,5},{2,10},{6,14},... | collective-permute-start | bytes 393224 | tf_op jit(solution)/shard_map/ppermute | solution.py:278
  14.4 0.0 collective-permute-done.2
  14.4 0.0 collective-permute-done.1
  14.4 0.5 %collective-permute-start.6 = (bf16[64,1024]{1,0:T(8,128)(2,1)S(1)}, bf16[64,1024]{1,0:T(8,128)(2,1)S(1)}, u32[]{:S(2)}, u32[]{:S(2)}) collective-permute-start(bf16[64,1024]{1,0:T(8,128)(2,1)S(1)} %add_convert_fusion.refs_1_), channel_id=1, source_target_pairs={{0,4},{4,0},{8,12},{12,8},{1,5},{5,1},{9,13},{13,9},{2,6},{6,2},{1... | collective-permute-start | bytes 393224 | tf_op jit(solution)/shard_map/ppermute | solution.py:278
  14.9 0.7 %collective-permute-start.4 = (bf16[64,1024]{1,0:T(8,128)(2,1)S(1)}, bf16[64,1024]{1,0:T(8,128)(2,1)S(1)}, u32[]{:S(2)}, u32[]{:S(2)}) collective-permute-start(bf16[64,1024]{1,0:T(8,128)(2,1)S(1)} %add_convert_fusion.refs_1_), channel_id=1, source_target_pairs={{0,8},{4,12},{8,0},{12,4},{1,9},{5,13},{9,1},{13,5},{2,10},{6,14},... | collective-permute-start | bytes 393224 | tf_op jit(solution)/shard_map/ppermute | solution.py:278
  15.6 0.0 copy-done.6
  15.6 0.1 copy.12.modes_ref
  15.7 0.1 collective-permute-start.10
  15.8 3.9 %collective-permute-done.5.refs_4_ = bf16[64,1024]{1,0:T(8,128)(2,1)S(1)} collective-permute-done((bf16[64,1024]{1,0:T(8,128)(2,1)S(1)}, bf16[64,1024]{1,0:T(8,128)(2,1)S(1)}, u32[]{:S(2)}, u32[]{:S(2)}) %collective-permute-start.5) | collective-permute-done | bytes 131104 | tf_op jit(solution)/shard_map/ppermute | solution.py:278
  19.8 0.0 collective-permute-start.9
  19.8 0.0 collective-permute-done.3.refs_2_
  19.8 0.5 %collective-permute-start.14 = (bf16[64,1024]{1,0:T(8,128)(2,1)S(1)}, bf16[64,1024]{1,0:T(8,128)(2,1)S(1)}, u32[]{:S(2)}, u32[]{:S(2)}) collective-permute-start(bf16[64,1024]{1,0:T(8,128)(2,1)S(1)} %collective-permute-done.5.refs_4_), channel_id=1, source_target_pairs={{0,1},{1,0},{2,3},{3,2},{4,5},{5,4},{6,7},{7,6},{8,9},{9,8},{10,11... | collective-permute-start | bytes 393224 | tf_op jit(solution)/shard_map/ppermute | solution.py:281
  20.3 1.6 %collective-permute-done.6.refs_5_ = bf16[64,1024]{1,0:T(8,128)(2,1)S(1)} collective-permute-done((bf16[64,1024]{1,0:T(8,128)(2,1)S(1)}, bf16[64,1024]{1,0:T(8,128)(2,1)S(1)}, u32[]{:S(2)}, u32[]{:S(2)}) %collective-permute-start.6) | collective-permute-done | bytes 131104 | tf_op jit(solution)/shard_map/ppermute | solution.py:278
  21.9 1.5 %collective-permute-start.7 = (bf16[64,1024]{1,0:T(8,128)(2,1)S(1)}, bf16[64,1024]{1,0:T(8,128)(2,1)S(1)}, u32[]{:S(2)}, u32[]{:S(2)}) collective-permute-start(bf16[64,1024]{1,0:T(8,128)(2,1)S(1)} %collective-permute-done.3.refs_2_), channel_id=1, source_target_pairs={{0,4},{4,0},{8,12},{12,8},{1,5},{5,1},{9,13},{13,9},{2,6},{6,2},{1... | collective-permute-start | bytes 393224 | tf_op jit(solution)/shard_map/ppermute | solution.py:278
  23.3 1.4 %collective-permute-done.4.refs_3_ = bf16[64,1024]{1,0:T(8,128)(2,1)S(1)} collective-permute-done((bf16[64,1024]{1,0:T(8,128)(2,1)S(1)}, bf16[64,1024]{1,0:T(8,128)(2,1)S(1)}, u32[]{:S(2)}, u32[]{:S(2)}) %collective-permute-start.4) | collective-permute-done | bytes 131104 | tf_op jit(solution)/shard_map/ppermute | solution.py:278
  24.7 0.3 collective-permute-start.8
  25.0 0.0 copy-done.3
  25.0 0.6 %mode_rotation.1 = (bf16[12,128,128]{2,1,0:T(8,128)(2,1)S(1)}, f32[12,64,1]{2,1,0:T(8,128)S(1)}) custom-call(bf16[2,12,60,60]{3,2,1,0:T(8,128)(2,1)S(1)} %copy.12.modes_ref, f32[12,60]{1,0:T(8,128)S(1)} %copy-done.3), custom_call_target="tpu_custom_call" | custom-call | flops 2000000000 | bytes 6000000 | tf_op jit(solution)/shard_map/mode_rotation/pallas_call | solution.py:257
  25.6 1.0 %lift.2.early_ref = bf16[192,4096]{1,0:T(8,128)(2,1)S(1)} custom-call(bf16[2,256,512]{2,1,0:T(8,128)(2,1)S(1)} %get-tuple-element.20.a_ref, bf16[64,1024]{1,0:T(8,128)(2,1)S(1)} %add_convert_fusion.1.refs_0_, bf16[64,1024]{1,0:T(8,128)(2,1)S(1)} %add_convert_fusion.refs_1_, bf16[64,1024]{1,0:T(8,128)(2,1)S(1)} %collective-permute-done.3.refs_2_, ...), custom_call_target="tpu_custom_call" | custom-call | flops 1000000000 | bytes 3000000 | tf_op jit(solution)/shard_map/lift/pallas_call | solution.py:286
  26.7 0.0 collective-permute-done.10.refs_1_
  26.7 0.1 collective-permute-start.12
  26.8 0.0 collective-permute-done.9.refs_0_
  26.8 0.5 %collective-permute-start.13 = (bf16[64,1024]{1,0:T(8,128)(2,1)S(1)}, bf16[64,1024]{1,0:T(8,128)(2,1)S(1)}, u32[]{:S(2)}, u32[]{:S(2)}) collective-permute-start(bf16[64,1024]{1,0:T(8,128)(2,1)S(1)} %collective-permute-done.6.refs_5_), channel_id=1, source_target_pairs={{0,1},{1,0},{2,3},{3,2},{4,5},{5,4},{6,7},{7,6},{8,9},{9,8},{10,11... | collective-permute-start | bytes 393224 | tf_op jit(solution)/shard_map/ppermute | solution.py:281
  27.3 0.0 collective-permute-done.14.refs_5_
  27.3 0.1 collective-permute-start.11
  27.3 0.2 collective-permute-done.7.y0_ref
  27.5 0.2 collective-permute-start.16
  27.8 1.9 %collective-permute-done.8.y1_ref = bf16[64,1024]{1,0:T(8,128)(2,1)S(1)} collective-permute-done((bf16[64,1024]{1,0:T(8,128)(2,1)S(1)}, bf16[64,1024]{1,0:T(8,128)(2,1)S(1)}, u32[]{:S(2)}, u32[]{:S(2)}) %collective-permute-start.8) | collective-permute-done | bytes 131104 | tf_op jit(solution)/shard_map/ppermute | solution.py:278
  29.6 0.0 collective-permute-start.15
  29.6 2.6 %coupling.2 = (bf16[12,60,1024]{2,1,0:T(8,128)(2,1)S(1)}, f32[1,1024]{1,0:T(1,128)S(1)}) custom-call(bf16[192,4096]{1,0:T(8,128)(2,1)S(1)} %lift.2.early_ref, bf16[64,1024]{1,0:T(8,128)(2,1)S(1)} %collective-permute-done.7.y0_ref, bf16[64,1024]{1,0:T(8,128)(2,1)S(1)} %collective-permute-done.8.y1_ref, bf16[2,256,512]{2,1,0:T(8,128)(2,1)S(1)} %get-tuple-element.20.a_ref, ...), custom_call_target="tpu_custom_call" | custom-call | flops 4000000000 | bytes 12000000 | tf_op jit(solution)/shard_map/coupling/pallas_call | solution.py:296
  32.3 0.0 collective-permute-done.12.refs_3_
  32.3 0.0 collective-permute-done.13.refs_4_
  32.3 0.0 collective-permute-done.11.refs_2_
  32.3 1.0 %lift.3.early_ref = bf16[192,4096]{1,0:T(8,128)(2,1)S(1)} custom-call(bf16[2,256,512]{2,1,0:T(8,128)(2,1)S(1)} %get-tuple-element.20.a_ref, bf16[64,1024]{1,0:T(8,128)(2,1)S(1)} %collective-permute-done.9.refs_0_, bf16[64,1024]{1,0:T(8,128)(2,1)S(1)} %collective-permute-done.10.refs_1_, bf16[64,1024]{1,0:T(8,128)(2,1)S(1)} %collective-permute-done.11.refs_2_, ...), custom_call_target="tpu_custom_call" | custom-call | flops 1000000000 | bytes 3000000 | tf_op jit(solution)/shard_map/lift/pallas_call | solution.py:286
  33.3 0.0 collective-permute-done.16.y1_ref
  33.3 0.0 collective-permute-done.15.y0_ref
  33.3 2.6 %coupling.3 = (bf16[12,60,1024]{2,1,0:T(8,128)(2,1)S(1)}, f32[1,1024]{1,0:T(1,128)S(1)}) custom-call(bf16[192,4096]{1,0:T(8,128)(2,1)S(1)} %lift.3.early_ref, bf16[64,1024]{1,0:T(8,128)(2,1)S(1)} %collective-permute-done.15.y0_ref, bf16[64,1024]{1,0:T(8,128)(2,1)S(1)} %collective-permute-done.16.y1_ref, bf16[2,256,512]{2,1,0:T(8,128)(2,1)S(1)} %get-tuple-element.20.a_ref, ...), custom_call_target="tpu_custom_call" | custom-call | flops 4000000000 | bytes 12000000 | tf_op jit(solution)/shard_map/coupling/pallas_call | solution.py:296
  36.0 0.6 %collective-permute-start.17 = (f32[2,1024]{1,0:T(2,128)S(1)}, f32[2,1024]{1,0:T(2,128)S(1)}, u32[]{:S(2)}, u32[]{:S(2)}) collective-permute-start(f32[2,1024]{1,0:T(2,128)S(1)} %maximum_select_fusion), channel_id=1, source_target_pairs={{0,1},{1,0},{2,3},{3,2},{4,5},{5,4},{6,7},{7,6},{8,9},{9,8},{10,11... | collective-permute-start | bytes 24584 | tf_op jit(solution)/shard_map/ppermute | solution.py:340
  36.5 0.8 %collective-permute-done.17 = f32[2,1024]{1,0:T(2,128)S(1)} collective-permute-done((f32[2,1024]{1,0:T(2,128)S(1)}, f32[2,1024]{1,0:T(2,128)S(1)}, u32[]{:S(2)}, u32[]{:S(2)}) %collective-permute-start.17) | collective-permute-done | bytes 8224 | tf_op jit(solution)/shard_map/ppermute | solution.py:340
  37.4 0.8 %collective-permute-start.18 = (f32[2,1024]{1,0:T(2,128)S(1)}, f32[2,1024]{1,0:T(2,128)S(1)}, u32[]{:S(2)}, u32[]{:S(2)}) collective-permute-start(f32[2,1024]{1,0:T(2,128)S(1)} %fusion), channel_id=1, source_target_pairs={{0,4},{4,0},{8,12},{12,8},{1,5},{5,1},{9,13},{13,9},{2,6},{6,2},{1... | collective-permute-start | bytes 24584 | tf_op jit(solution)/shard_map/ppermute | solution.py:343
  38.2 1.5 %order.2.refs_0_ = bf16[12,60,2,1024]{3,2,1,0:T(2,128)(2,1)} custom-call(bf16[12,60,1024]{2,1,0:T(8,128)(2,1)S(1)} %get-tuple-element.28.first_ref, bf16[12,60,1024]{2,1,0:T(8,128)(2,1)S(1)} %get-tuple-element.29.second_ref), custom_call_target="tpu_custom_call" | custom-call | flops 2000000000 | bytes 6000000 | tf_op jit(solution)/shard_map/order/pallas_call | solution.py:325
  39.6 1.5 %collective-permute-done.18 = f32[2,1024]{1,0:T(2,128)S(1)} collective-permute-done((f32[2,1024]{1,0:T(2,128)S(1)}, f32[2,1024]{1,0:T(2,128)S(1)}, u32[]{:S(2)}, u32[]{:S(2)}) %collective-permute-start.18) | collective-permute-done | bytes 8224 | tf_op jit(solution)/shard_map/ppermute | solution.py:343
  41.1 1.9 %collective-permute-start.19 = (f32[2,1024]{1,0:T(2,128)S(1)}, f32[2,1024]{1,0:T(2,128)S(1)}, u32[]{:S(2)}, u32[]{:S(2)}) collective-permute-start(f32[2,1024]{1,0:T(2,128)S(1)} %fusion.1), channel_id=1, source_target_pairs={{0,8},{4,12},{8,0},{12,4},{1,9},{5,13},{9,1},{13,5},{2,10},{6,14},... | collective-permute-start | bytes 24584 | tf_op jit(solution)/shard_map/ppermute | solution.py:343
  43.1 1.5 %order.3 = bf16[12,60,2,1024]{3,2,1,0:T(2,128)(2,1)} custom-call(bf16[12,60,1024]{2,1,0:T(8,128)(2,1)S(1)} %get-tuple-element.28.first_ref, bf16[12,60,1024]{2,1,0:T(8,128)(2,1)S(1)} %get-tuple-element.29.second_ref, bf16[12,60,2,1024]{3,2,1,0:T(2,128)(2,1)} %order.2.refs_0_), custom_call_target="tpu_custom_call", output_to_operand_aliasing={{}: (2, {})} | custom-call | flops 2000000000 | bytes 6000000 | tf_op jit(solution)/shard_map/order/pallas_call | solution.py:325
  44.6 1.2 %collective-permute-done.19 = f32[2,1024]{1,0:T(2,128)S(1)} collective-permute-done((f32[2,1024]{1,0:T(2,128)S(1)}, f32[2,1024]{1,0:T(2,128)S(1)}, u32[]{:S(2)}, u32[]{:S(2)}) %collective-permute-start.19) | collective-permute-done | bytes 8224 | tf_op jit(solution)/shard_map/ppermute | solution.py:343
  45.8 0.6 %add.19 = f32[2,1024]{1,0:T(2,128)} add(f32[2,1024]{1,0:T(2,128)S(1)} %fusion.1, f32[2,1024]{1,0:T(2,128)S(1)} %collective-permute-done.19) | non-fusion elementwise | flops 2048 | bytes 24576 | tf_op jit(solution)/shard_map/add | solution.py:343
  (8 shorter events, 0.1 us)
Async XLA Ops:
  1.3 0.9 %copy-start.1 = (bf16[2,1,2,30,1024]{4,2,3,1,0:T(2,128)(2,1)S(1)}, bf16[2,1,2,30,1024]{4,2,3,1,0:T(2,128)(2,1)}, u32[]{:S(2)}) copy-start(bf16[2,1,2,30,1024]{4,2,3,1,0:T(2,128)(2,1)} %param.9) | copy-start | bytes 737284
  2.3 3.5 %copy-start = (bf16[2,12,2,32,32]{4,3,2,1,0:T(8,128)(2,1)S(1)}, bf16[2,12,2,32,32]{4,3,2,1,0:T(8,128)(2,1)}, u32[]{:S(2)}) copy-start(bf16[2,12,2,32,32]{4,3,2,1,0:T(8,128)(2,1)} %u_kq_ref.1) | copy-start | bytes 294916
  2.3 3.5 %copy-start.2 = (bf16[2,2,32,32]{3,2,1,0:T(8,128)(2,1)S(1)}, bf16[2,2,32,32]{3,2,1,0:T(8,128)(2,1)}, u32[]{:S(2)}) copy-start(bf16[2,2,32,32]{3,2,1,0:T(8,128)(2,1)} %u_k_ref.1) | copy-start | bytes 24580
  2.3 3.5 %copy-start.4 = (s32[4,3]{1,0:T(4,128)S(1)}, s32[4,3]{1,0:T(4,128)}, u32[]{:S(2)}) copy-start(s32[4,3]{1,0:T(4,128)} %r_ref.1) | copy-start | bytes 148
  2.3 3.5 %copy-start.5 = (s32[24,3]{0,1:T(4,128)S(1)}, s32[24,3]{0,1:T(4,128)}, u32[]{:S(2)}) copy-start(s32[24,3]{0,1:T(4,128)} %param.13) | copy-start | bytes 868
  2.6 6.9 %collective-permute-start = (bf16[64,1024]{1,0:T(8,128)(2,1)S(1)}, bf16[64,1024]{1,0:T(8,128)(2,1)S(1)}, u32[]{:S(2)}, u32[]{:S(2)}) collective-permute-start(bf16[64,1024]{1,0:T(8,128)(2,1)S(1)} %get-tuple-element.22), channel_id=1, source_target_pairs={{0,2},{2,0},{1,3},{3,1},{4,6},{6,4},{5,7},{7,5},{8,10},{10,8},{9,1... | collective-permute-start | bytes 393224 | tf_op jit(solution)/shard_map/ppermute | solution.py:235
  5.6 8.8 %collective-permute-start.2 = (bf16[64,1024]{1,0:T(8,128)(2,1)S(1)}, bf16[64,1024]{1,0:T(8,128)(2,1)S(1)}, u32[]{:S(2)}, u32[]{:S(2)}) collective-permute-start(bf16[64,1024]{1,0:T(8,128)(2,1)S(1)} %get-tuple-element.24), channel_id=1, source_target_pairs={{0,3},{1,2},{2,1},{3,0},{4,7},{5,6},{6,5},{7,4},{8,11},{9,10},{10,... | collective-permute-start | bytes 393224 | tf_op jit(solution)/shard_map/ppermute | solution.py:236
  5.6 8.8 %collective-permute-start.1 = (f32[64,1024]{1,0:T(8,128)S(1)}, f32[64,1024]{1,0:T(8,128)S(1)}, u32[]{:S(2)}, u32[]{:S(2)}) collective-permute-start(f32[64,1024]{1,0:T(8,128)S(1)} %get-tuple-element.23), channel_id=1, source_target_pairs={{0,1},{1,0},{2,3},{3,2},{4,5},{5,4},{6,7},{7,6},{8,9},{9,8},{10,11... | collective-permute-start | bytes 786440 | tf_op jit(solution)/shard_map/ppermute | solution.py:230
  5.8 9.8 %copy-start.6 = (bf16[2,12,60,60]{3,0,2,1:T(2,128)(2,1)S(1)}, bf16[2,12,60,60]{3,0,2,1:T(2,128)(2,1)}, u32[]{:S(2)}) copy-start(bf16[2,12,60,60]{3,0,2,1:T(2,128)(2,1)} %param.16) | copy-start | bytes 518404
  7.1 17.9 %copy-start.3 = (f32[12,60]{1,0:T(8,128)S(1)}, f32[12,60]{1,0:T(8,128)}, u32[]{:S(2)}) copy-start(f32[12,60]{1,0:T(8,128)} %weights_ref.1) | copy-start | bytes 8644
  9.6 10.2 %collective-permute-start.5 = (bf16[64,1024]{1,0:T(8,128)(2,1)S(1)}, bf16[64,1024]{1,0:T(8,128)(2,1)S(1)}, u32[]{:S(2)}, u32[]{:S(2)}) collective-permute-start(bf16[64,1024]{1,0:T(8,128)(2,1)S(1)} %add_convert_fusion.1.refs_0_), channel_id=1, source_target_pairs={{0,4},{4,0},{8,12},{12,8},{1,5},{5,1},{9,13},{13,9},{2,6},{6,2},{1... | collective-permute-start | bytes 393224 | tf_op jit(solution)/shard_map/ppermute | solution.py:278
  11.8 8.0 %collective-permute-start.3 = (bf16[64,1024]{1,0:T(8,128)(2,1)S(1)}, bf16[64,1024]{1,0:T(8,128)(2,1)S(1)}, u32[]{:S(2)}, u32[]{:S(2)}) collective-permute-start(bf16[64,1024]{1,0:T(8,128)(2,1)S(1)} %add_convert_fusion.1.refs_0_), channel_id=1, source_target_pairs={{0,8},{4,12},{8,0},{12,4},{1,9},{5,13},{9,1},{13,5},{2,10},{6,14},... | collective-permute-start | bytes 393224 | tf_op jit(solution)/shard_map/ppermute | solution.py:278
  14.4 7.4 %collective-permute-start.6 = (bf16[64,1024]{1,0:T(8,128)(2,1)S(1)}, bf16[64,1024]{1,0:T(8,128)(2,1)S(1)}, u32[]{:S(2)}, u32[]{:S(2)}) collective-permute-start(bf16[64,1024]{1,0:T(8,128)(2,1)S(1)} %add_convert_fusion.refs_1_), channel_id=1, source_target_pairs={{0,4},{4,0},{8,12},{12,8},{1,5},{5,1},{9,13},{13,9},{2,6},{6,2},{1... | collective-permute-start | bytes 393224 | tf_op jit(solution)/shard_map/ppermute | solution.py:278
  14.9 9.7 %collective-permute-start.4 = (bf16[64,1024]{1,0:T(8,128)(2,1)S(1)}, bf16[64,1024]{1,0:T(8,128)(2,1)S(1)}, u32[]{:S(2)}, u32[]{:S(2)}) collective-permute-start(bf16[64,1024]{1,0:T(8,128)(2,1)S(1)} %add_convert_fusion.refs_1_), channel_id=1, source_target_pairs={{0,8},{4,12},{8,0},{12,4},{1,9},{5,13},{9,1},{13,5},{2,10},{6,14},... | collective-permute-start | bytes 393224 | tf_op jit(solution)/shard_map/ppermute | solution.py:278
  15.7 10.9 %collective-permute-start.10 = (bf16[64,1024]{1,0:T(8,128)(2,1)S(1)}, bf16[64,1024]{1,0:T(8,128)(2,1)S(1)}, u32[]{:S(2)}, u32[]{:S(2)}) collective-permute-start(bf16[64,1024]{1,0:T(8,128)(2,1)S(1)} %add_convert_fusion.1.refs_0_), channel_id=1, source_target_pairs={{0,1},{1,0},{2,3},{3,2},{4,5},{5,4},{6,7},{7,6},{8,9},{9,8},{10,11... | collective-permute-start | bytes 393224 | tf_op jit(solution)/shard_map/ppermute | solution.py:281
  19.8 7.0 %collective-permute-start.9 = (bf16[64,1024]{1,0:T(8,128)(2,1)S(1)}, bf16[64,1024]{1,0:T(8,128)(2,1)S(1)}, u32[]{:S(2)}, u32[]{:S(2)}) collective-permute-start(bf16[64,1024]{1,0:T(8,128)(2,1)S(1)} %add_convert_fusion.refs_1_), channel_id=1, source_target_pairs={{0,1},{1,0},{2,3},{3,2},{4,5},{5,4},{6,7},{7,6},{8,9},{9,8},{10,11... | collective-permute-start | bytes 393224 | tf_op jit(solution)/shard_map/ppermute | solution.py:281
  19.8 7.5 %collective-permute-start.14 = (bf16[64,1024]{1,0:T(8,128)(2,1)S(1)}, bf16[64,1024]{1,0:T(8,128)(2,1)S(1)}, u32[]{:S(2)}, u32[]{:S(2)}) collective-permute-start(bf16[64,1024]{1,0:T(8,128)(2,1)S(1)} %collective-permute-done.5.refs_4_), channel_id=1, source_target_pairs={{0,1},{1,0},{2,3},{3,2},{4,5},{5,4},{6,7},{7,6},{8,9},{9,8},{10,11... | collective-permute-start | bytes 393224 | tf_op jit(solution)/shard_map/ppermute | solution.py:281
  21.9 5.7 %collective-permute-start.7 = (bf16[64,1024]{1,0:T(8,128)(2,1)S(1)}, bf16[64,1024]{1,0:T(8,128)(2,1)S(1)}, u32[]{:S(2)}, u32[]{:S(2)}) collective-permute-start(bf16[64,1024]{1,0:T(8,128)(2,1)S(1)} %collective-permute-done.3.refs_2_), channel_id=1, source_target_pairs={{0,4},{4,0},{8,12},{12,8},{1,5},{5,1},{9,13},{13,9},{2,6},{6,2},{1... | collective-permute-start | bytes 393224 | tf_op jit(solution)/shard_map/ppermute | solution.py:278
  24.7 5.0 %collective-permute-start.8 = (bf16[64,1024]{1,0:T(8,128)(2,1)S(1)}, bf16[64,1024]{1,0:T(8,128)(2,1)S(1)}, u32[]{:S(2)}, u32[]{:S(2)}) collective-permute-start(bf16[64,1024]{1,0:T(8,128)(2,1)S(1)} %collective-permute-done.4.refs_3_), channel_id=1, source_target_pairs={{0,4},{4,0},{8,12},{12,8},{1,5},{5,1},{9,13},{13,9},{2,6},{6,2},{1... | collective-permute-start | bytes 393224 | tf_op jit(solution)/shard_map/ppermute | solution.py:278
  26.7 5.6 %collective-permute-start.12 = (bf16[64,1024]{1,0:T(8,128)(2,1)S(1)}, bf16[64,1024]{1,0:T(8,128)(2,1)S(1)}, u32[]{:S(2)}, u32[]{:S(2)}) collective-permute-start(bf16[64,1024]{1,0:T(8,128)(2,1)S(1)} %collective-permute-done.3.refs_2_), channel_id=1, source_target_pairs={{0,1},{1,0},{2,3},{3,2},{4,5},{5,4},{6,7},{7,6},{8,9},{9,8},{10,11... | collective-permute-start | bytes 393224 | tf_op jit(solution)/shard_map/ppermute | solution.py:281
  26.8 5.5 %collective-permute-start.13 = (bf16[64,1024]{1,0:T(8,128)(2,1)S(1)}, bf16[64,1024]{1,0:T(8,128)(2,1)S(1)}, u32[]{:S(2)}, u32[]{:S(2)}) collective-permute-start(bf16[64,1024]{1,0:T(8,128)(2,1)S(1)} %collective-permute-done.6.refs_5_), channel_id=1, source_target_pairs={{0,1},{1,0},{2,3},{3,2},{4,5},{5,4},{6,7},{7,6},{8,9},{9,8},{10,11... | collective-permute-start | bytes 393224 | tf_op jit(solution)/shard_map/ppermute | solution.py:281
  27.3 5.0 %collective-permute-start.11 = (bf16[64,1024]{1,0:T(8,128)(2,1)S(1)}, bf16[64,1024]{1,0:T(8,128)(2,1)S(1)}, u32[]{:S(2)}, u32[]{:S(2)}) collective-permute-start(bf16[64,1024]{1,0:T(8,128)(2,1)S(1)} %collective-permute-done.4.refs_3_), channel_id=1, source_target_pairs={{0,1},{1,0},{2,3},{3,2},{4,5},{5,4},{6,7},{7,6},{8,9},{9,8},{10,11... | collective-permute-start | bytes 393224 | tf_op jit(solution)/shard_map/ppermute | solution.py:281
  27.5 5.8 %collective-permute-start.16 = (bf16[64,1024]{1,0:T(8,128)(2,1)S(1)}, bf16[64,1024]{1,0:T(8,128)(2,1)S(1)}, u32[]{:S(2)}, u32[]{:S(2)}) collective-permute-start(bf16[64,1024]{1,0:T(8,128)(2,1)S(1)} %collective-permute-done.7.y0_ref), channel_id=1, source_target_pairs={{0,1},{1,0},{2,3},{3,2},{4,5},{5,4},{6,7},{7,6},{8,9},{9,8},{10,11... | collective-permute-start | bytes 393224 | tf_op jit(solution)/shard_map/ppermute | solution.py:281
  29.6 3.7 %collective-permute-start.15 = (bf16[64,1024]{1,0:T(8,128)(2,1)S(1)}, bf16[64,1024]{1,0:T(8,128)(2,1)S(1)}, u32[]{:S(2)}, u32[]{:S(2)}) collective-permute-start(bf16[64,1024]{1,0:T(8,128)(2,1)S(1)} %collective-permute-done.8.y1_ref), channel_id=1, source_target_pairs={{0,1},{1,0},{2,3},{3,2},{4,5},{5,4},{6,7},{7,6},{8,9},{9,8},{10,11... | collective-permute-start | bytes 393224 | tf_op jit(solution)/shard_map/ppermute | solution.py:281
  36.0 1.4 %collective-permute-start.17 = (f32[2,1024]{1,0:T(2,128)S(1)}, f32[2,1024]{1,0:T(2,128)S(1)}, u32[]{:S(2)}, u32[]{:S(2)}) collective-permute-start(f32[2,1024]{1,0:T(2,128)S(1)} %maximum_select_fusion), channel_id=1, source_target_pairs={{0,1},{1,0},{2,3},{3,2},{4,5},{5,4},{6,7},{7,6},{8,9},{9,8},{10,11... | collective-permute-start | bytes 24584 | tf_op jit(solution)/shard_map/ppermute | solution.py:340
  37.4 3.7 %collective-permute-start.18 = (f32[2,1024]{1,0:T(2,128)S(1)}, f32[2,1024]{1,0:T(2,128)S(1)}, u32[]{:S(2)}, u32[]{:S(2)}) collective-permute-start(f32[2,1024]{1,0:T(2,128)S(1)} %fusion), channel_id=1, source_target_pairs={{0,4},{4,0},{8,12},{12,8},{1,5},{5,1},{9,13},{13,9},{2,6},{6,2},{1... | collective-permute-start | bytes 24584 | tf_op jit(solution)/shard_map/ppermute | solution.py:343
  41.1 4.6 %collective-permute-start.19 = (f32[2,1024]{1,0:T(2,128)S(1)}, f32[2,1024]{1,0:T(2,128)S(1)}, u32[]{:S(2)}, u32[]{:S(2)}) collective-permute-start(f32[2,1024]{1,0:T(2,128)S(1)} %fusion.1), channel_id=1, source_target_pairs={{0,8},{4,12},{8,0},{12,4},{1,9},{5,13},{9,1},{13,5},{2,10},{6,14},... | collective-permute-start | bytes 24584 | tf_op jit(solution)/shard_map/ppermute | solution.py:343

commit v3 on v2

--- a/solution.py
+++ b/solution.py
@@ -117,7 +117,8 @@
             r, i = (jnp.where(first ^ (h == 1), d[:half], d[half:]) for d in (dr, di))
             parts += [jnp.concatenate([r, gap, i, gap], 1), rows]
             parts += [jnp.concatenate([-i, gap, r, gap], 1), rows]
-        mix_ref[q] = jnp.concatenate(parts, 0).T.astype(BF16)
+        mix_ref[0, q] = jnp.concatenate(parts, 0).T.astype(BF16)
+        mix_ref[1, q] = jnp.concatenate(parts[4:] + parts[:4], 0).T.astype(BF16)
     w = weights_ref[...]
     w = jnp.concatenate([w, jnp.zeros((q_rows, 128 - modes), F32)], 1)
     w = jnp.concatenate([w, jnp.zeros((128 - q_rows, 128), F32)], 0).T
@@ -145,9 +146,9 @@
                 x_ref[row : row + 16, n * 128 : (n + 1) * 128] = both[:, c * 128 : (c + 1) * 128]
 
 
-def lift_kernel(k, width, a_ref, *refs):
+def lift_kernel(width, a_ref, *refs):
     for i in range(0, len(refs) - 1, 2):
-        lift(a_ref[k], refs[i : i + 2], refs[-1], i * width, width)
+        lift(a_ref[0], refs[i : i + 2], refs[-1], i * width, width)
 
 
 def coupling_kernel(
@@ -178,7 +179,7 @@
     for q in range(q_rows):
         z = zs[q * rows : (q + 1) * rows, :].reshape(width, pitch, 128)[:, :width]
         z = z.reshape(width * width, 128).astype(BF16)
-        res = lax.dot_general(d_ref[q], z, NT, preferred_element_type=F32)
+        res = lax.dot_general(d_ref[k, q], z, NT, preferred_element_type=F32)
         sq = res[:BRANCH_PAD] * res[:BRANCH_PAD] + res[BRANCH_PAD:] * res[BRANCH_PAD:]
         out_ref[q] = sq[:modes].astype(BF16)
         weighted = sq * w_ref[q]
@@ -227,14 +228,6 @@
         compiler_params=pltpu.CompilerParams(vmem_limit_bytes=16 * MIB),
         name="electron_sum",
     )(factor, table)
-    mine, other = [parts[0]], [lax.ppermute(parts[1], "ma", flip(n_ma, 1))]
-    for s in range(1, n_ea):
-        cross = [
-            (e * n_ma + c, (e + s) % n_ea * n_ma + (c ^ 1)) for e in range(n_ea) for c in range(n_ma)
-        ]
-        mine.append(lax.ppermute(parts[s * k_rows], "ea", shift(n_ea, s)))
-        other.append(lax.ppermute(parts[s * k_rows + 1], ("ea", "ma"), cross))
-
     masks = [0]
     distance = n_pb // 2
     while distance:
@@ -257,7 +250,7 @@
     mix, weights = pl.pallas_call(
         functools.partial(mode_kernel, half),
         out_shape=[
-            jax.ShapeDtypeStruct((q_rows, 2 * BRANCH_PAD, n_ma * 2 * MODE_PAD), BF16),
+            jax.ShapeDtypeStruct((2, q_rows, 2 * BRANCH_PAD, n_ma * 2 * MODE_PAD), BF16),
             jax.ShapeDtypeStruct((q_rows, BRANCH_PAD, 1), F32),
         ],
         in_specs=[VMEM, VMEM],
@@ -267,6 +260,14 @@
         name="mode_rotation",
     )(modes_q, weights_q)
 
+    mine, other = [parts[0]], [lax.ppermute(parts[1], "ma", flip(n_ma, 1))]
+    for s in range(1, n_ea):
+        cross = [
+            (e * n_ma + c, (e + s) % n_ea * n_ma + (c ^ 1)) for e in range(n_ea) for c in range(n_ma)
+        ]
+        mine.append(lax.ppermute(parts[s * k_rows], "ea", shift(n_ea, s)))
+        other.append(lax.ppermute(parts[s * k_rows + 1], ("ea", "ma"), cross))
+
     mine[0], left, kron = lax.optimization_barrier((mine[0], left, kron))
     by_k = [sum(y.astype(F32) for y in part).astype(BF16) for part in (mine, other)]
 
@@ -274,24 +275,28 @@
     halves = [[y] for y in by_k]
     distance = n_pb // 2
     while distance:
-        for half_blocks in halves:
-            half_blocks += [lax.ppermute(y, "pb", flip(n_pb, distance)) for y in half_blocks]
+        for h, blocks in enumerate(halves):
+            came = [lax.ppermute(blocks[0], "pb", flip(n_pb, distance))]
+            for y in blocks[1:]:
+                if h == 0:
+                    y, _ = lax.optimization_barrier((y, came[0]))
+                came.append(lax.ppermute(y, "pb", flip(n_pb, distance)))
+            blocks += came
         distance //= 2
     held = [y for pair in zip(*halves) for y in pair]
-    swapped = [lax.ppermute(y, "ma", swap) for y in held]
-    swapped = [swapped[i ^ 1] for i in range(len(swapped))]
-
+    early = pl.pallas_call(
+        functools.partial(lift_kernel, width),
+        out_shape=jax.ShapeDtypeStruct(((n_pb - 1) * 2 * width, width * 128), BF16),
+        in_specs=[VMEM] * (2 * n_pb - 1),
+        out_specs=VMEM,
+        cost_estimate=cost(1),
+        compiler_params=pltpu.CompilerParams(vmem_limit_bytes=(4 + n_pb) * MIB),
+        name="lift",
+    )(kron, *held[:-2])
+    early = (early, lax.ppermute(early, "ma", swap))
+    last = (held[-2:], [lax.ppermute(y, "ma", swap) for y in held[-2:]])
     results = []
-    for k, blocks in enumerate((held, swapped)):
-        early = pl.pallas_call(
-            functools.partial(lift_kernel, k, width),
-            out_shape=jax.ShapeDtypeStruct(((n_pb - 1) * 2 * width, width * 128), BF16),
-            in_specs=[VMEM] * (2 * n_pb - 1),
-            out_specs=VMEM,
-            cost_estimate=cost(1),
-            compiler_params=pltpu.CompilerParams(vmem_limit_bytes=(4 + n_pb) * MIB),
-            name="lift",
-        )(kron, *blocks[:-2])
+    for k in range(k_rows):
         results.append(
             pl.pallas_call(
                 functools.partial(
@@ -307,10 +312,10 @@
                     pltpu.VMEM((2 * width, width * 128), BF16),
                     pltpu.VMEM((q_rows * width * (width + 8), 128), F32),
                 ],
-                cost_estimate=cost(4),
+                cost_estimate=cost(40),
                 compiler_params=pltpu.CompilerParams(vmem_limit_bytes=(14 + n_pb) * MIB),
                 name="coupling",
-            )(early, *blocks[-2:], kron, left, mix, weights)
+            )(early[k], *last[k], kron, left, mix, weights)
         )
     (first, mean), (second, rest) = results
     core = lax.axis_index("ma")
@@ -337,8 +342,12 @@
             name="order",
         )(*operands)
     out = jnp.transpose(out, (0, 2, 1, 3))
-    mean = mean + lax.ppermute(mean, "ma", swap)
-    distance = 1
+    cross = [(z * n_ma + c, (z ^ 1) * n_ma + (c ^ 1)) for z in range(n_pb) for c in range(n_ma)]
+    z_mean = lax.ppermute(mean, "pb", flip(n_pb, 1))
+    c_mean = lax.ppermute(mean, ("pb", "ma"), cross)
+    m_mean = lax.ppermute(mean, "ma", swap)
+    mean = (mean + m_mean) + (z_mean + c_mean)
+    distance = 2
     while distance < n_pb:
         mean = mean + lax.ppermute(mean, "pb", flip(n_pb, distance))
         distance *= 2

time: 46.5 us -> 44.6 us (0.959)
  Pallas kernels: 13.1 us -> 12.2 us
  starting transfers between devices: 15.8 us -> 15.3 us
    ppermute x2 -> x1, waiting for transfers between devices: 2.66 us -> 0.14 us  [body(): mean = mean + lax.ppermute(mean, 'pb', flip(n_pb, distance))]
    ppermute x15 -> x12, waiting for transfers between devices: 9.79 us -> 11.9 us  [the longest x4 8.49 us: body(): came = [lax.ppermute(blocks[0], 'pb', flip(n_pb, distance))]]
    ppermute x15 -> x12, starting transfers between devices: 9.88 us -> 8.67 us  [the longest x4 6.1 us: body(): came = [lax.ppermute(blocks[0], 'pb', flip(n_pb, distance))]]
    pallas_call x2 -> x1, Pallas kernels: 2.03 us -> 1.02 us  [body(): pl.pallas_call(functools.partial(lift_kernel, width), out_shape=jax.Shape...]
    ppermute x2 -> x1, starting transfers between devices: 2.69 us -> 3.38 us  [body(): mean = mean + lax.ppermute(mean, 'pb', flip(n_pb, distance))]
  transfers between devices with their start and end apart: 20 -> 16, of which waited for: 9 -> 8; matrix products, arithmetic and copies ran while one was open for 0% -> 0% of each run, Pallas kernels for 20% -> 19%
where the time goes in v3:
time: 44.6 us; the launch traced here: 44.4 us
  starting transfers between devices  15.3 us (34%)
  waiting for transfers between devices  14.5 us (33%)
  Pallas kernels  12.2 us (27%)
  other arithmetic  1.41 us (3%)
  between operations  0.8 us (2%)
    ppermute x4, waiting for transfers between devices, body(): came = [lax.ppermute(blocks[0], 'pb', flip(n_pb, distance))]  8.49 us
    ppermute x4, starting transfers between devices, body(): came = [lax.ppermute(blocks[0], 'pb', flip(n_pb, distance))]  6.1 us
    pallas_call x2, Pallas kernels, body(): pl.pallas_call(functools.partial(coupling_kernel, k, width, modes, q_rows...  5.25 us
    ppermute x1, starting transfers between devices, body(): mean = mean + lax.ppermute(mean, 'pb', flip(n_pb, distance))  3.38 us
    ppermute x2, waiting for transfers between devices, body(): came.append(lax.ppermute(y, 'pb', flip(n_pb, distance)))  3.13 us
    ppermute x1, starting transfers between devices, body(): mine.append(lax.ppermute(parts[s * k_rows], 'ea', shift(n_ea, s)))  3 us
    pallas_call x2, Pallas kernels, body(): pl.pallas_call(order_kernel, grid=(1,), out_shape=jax.ShapeDtypeStruct((q...  2.97 us
    ppermute x1, waiting for transfers between devices, body(): mine.append(lax.ppermute(parts[s * k_rows], 'ea', shift(n_ea, s)))  2.42 us
  transfers between devices with their start and end apart: 16, of which 8 were waited for; matrix products, arithmetic and copies ran while one was open for 0% of the time, Pallas kernels for 19%

profile of v3, /device:TPU:0, one launch (start us, length us, event | category | flops | bytes accessed | tf_op | source)
XLA Modules:
  0.0 44.4 jit_solution(9031911029596742382)
XLA Ops:
  0.6 0.7 %pad_add_fusion.coords_ref = s32[6,3]{1,0:T(8,128)S(1)} fusion(s32[2,3]{1,0:T(2,128)} %param.10, s32[4,3]{1,0:T(4,128)} %param.12), kind=kLoop, calls=%fused_computation.4 | loop fusion | flops 18 | bytes 144 | tf_op jit(solution)/shard_map/concatenate | solution.py:218
  1.3 0.0 copy-start.1
  1.3 0.7 %electron_phases.1.factor_ref = bf16[256,120]{1,0:T(8,128)(2,1)S(1)} custom-call(s32[6,3]{1,0:T(8,128)S(1)} %pad_add_fusion.coords_ref), custom_call_target="tpu_custom_call" | custom-call | flops 2000000000 | bytes 6000000 | tf_op jit(solution)/shard_map/electron_phases/pallas_call | solution.py:210
  2.1 0.2 copy-done.1
  2.3 0.0 copy-start
  2.3 0.0 copy-start.2
  2.3 0.0 copy-start.4
  2.3 0.0 copy-start.5
  2.3 0.3 electron_sum.1
  2.6 3.0 %collective-permute-start = (bf16[64,1024]{1,0:T(8,128)(2,1)S(1)}, bf16[64,1024]{1,0:T(8,128)(2,1)S(1)}, u32[]{:S(2)}, u32[]{:S(2)}) collective-permute-start(bf16[64,1024]{1,0:T(8,128)(2,1)S(1)} %get-tuple-element.23), channel_id=1, source_target_pairs={{0,2},{2,0},{1,3},{3,1},{4,6},{6,4},{5,7},{7,5},{8,10},{10,8},{9,1... | collective-permute-start | bytes 393224 | tf_op jit(solution)/shard_map/ppermute | solution.py:268
  5.6 0.0 collective-permute-start.2
  5.6 0.2 collective-permute-start.1
  5.8 0.0 copy-done
  5.8 0.0 copy-done.2
  5.8 0.0 copy-done.4
  5.8 0.0 copy-done.5
  5.8 0.0 copy-start.6
  5.8 1.3 %rotations.1 = (bf16[2,384,256]{2,1,0:T(8,128)(2,1)S(1)}, bf16[2,256,512]{2,1,0:T(8,128)(2,1)S(1)}) custom-call(s32[4,3]{1,0:T(4,128)S(1)} %copy-done.4, s32[3,24]{1,0:T(4,128)S(1)} %bitcast.4, bf16[2,2,32,32]{3,2,1,0:T(8,128)(2,1)S(1)} %copy-done.2, bf16[2,12,2,32,32]{4,3,2,1,0:T(8,128)(2,1)S(1)} %copy-done), custom_call_target="tpu_custom_call" | custom-call | flops 2000000000 | bytes 6000000 | tf_op jit(solution)/shard_map/rotations/pallas_call | solution.py:237
  7.1 0.0 copy-start.3
  7.1 2.4 %collective-permute-done = bf16[64,1024]{1,0:T(8,128)(2,1)S(1)} collective-permute-done((bf16[64,1024]{1,0:T(8,128)(2,1)S(1)}, bf16[64,1024]{1,0:T(8,128)(2,1)S(1)}, u32[]{:S(2)}, u32[]{:S(2)}) %collective-permute-start) | collective-permute-done | bytes 131104 | tf_op jit(solution)/shard_map/ppermute | solution.py:268
  9.6 2.2 %collective-permute-start.5 = (bf16[64,1024]{1,0:T(8,128)(2,1)S(1)}, bf16[64,1024]{1,0:T(8,128)(2,1)S(1)}, u32[]{:S(2)}, u32[]{:S(2)}) collective-permute-start(bf16[64,1024]{1,0:T(8,128)(2,1)S(1)} %add_convert_fusion.1.refs_0_), channel_id=1, source_target_pairs={{0,4},{4,0},{8,12},{12,8},{1,5},{5,1},{9,13},{13,9},{2,6},{6,2},{1... | collective-permute-start | bytes 393224 | tf_op jit(solution)/shard_map/ppermute | solution.py:279
  11.8 2.6 %collective-permute-start.3 = (bf16[64,1024]{1,0:T(8,128)(2,1)S(1)}, bf16[64,1024]{1,0:T(8,128)(2,1)S(1)}, u32[]{:S(2)}, u32[]{:S(2)}) collective-permute-start(bf16[64,1024]{1,0:T(8,128)(2,1)S(1)} %add_convert_fusion.1.refs_0_), channel_id=1, source_target_pairs={{0,8},{4,12},{8,0},{12,4},{1,9},{5,13},{9,1},{13,5},{2,10},{6,14},... | collective-permute-start | bytes 393224 | tf_op jit(solution)/shard_map/ppermute | solution.py:279
  14.4 0.0 collective-permute-done.2
  14.4 0.0 collective-permute-done.1
  14.4 0.4 collective-permute-start.4
  14.8 0.0 copy-done.6
  14.8 0.1 copy.12.modes_ref
  14.9 0.9 %collective-permute-start.6 = (bf16[64,1024]{1,0:T(8,128)(2,1)S(1)}, bf16[64,1024]{1,0:T(8,128)(2,1)S(1)}, u32[]{:S(2)}, u32[]{:S(2)}) collective-permute-start(bf16[64,1024]{1,0:T(8,128)(2,1)S(1)} %add_convert_fusion.refs_1_), channel_id=1, source_target_pairs={{0,4},{4,0},{8,12},{12,8},{1,5},{5,1},{9,13},{13,9},{2,6},{6,2},{1... | collective-permute-start | bytes 393224 | tf_op jit(solution)/shard_map/ppermute | solution.py:279
  15.8 0.1 collective-permute-done.5.refs_4_
  15.9 6.5 %collective-permute-done.3.refs_2_ = bf16[64,1024]{1,0:T(8,128)(2,1)S(1)} collective-permute-done((bf16[64,1024]{1,0:T(8,128)(2,1)S(1)}, bf16[64,1024]{1,0:T(8,128)(2,1)S(1)}, u32[]{:S(2)}, u32[]{:S(2)}) %collective-permute-start.3) | collective-permute-done | bytes 131104 | tf_op jit(solution)/shard_map/ppermute | solution.py:279
  22.4 0.3 collective-permute-start.7
  22.6 1.9 %collective-permute-done.4.refs_3_ = bf16[64,1024]{1,0:T(8,128)(2,1)S(1)} collective-permute-done((bf16[64,1024]{1,0:T(8,128)(2,1)S(1)}, bf16[64,1024]{1,0:T(8,128)(2,1)S(1)}, u32[]{:S(2)}, u32[]{:S(2)}) %collective-permute-start.4) | collective-permute-done | bytes 131104 | tf_op jit(solution)/shard_map/ppermute | solution.py:279
  24.5 0.0 collective-permute-start.8
  24.6 0.0 copy-done.3
  24.6 0.7 %mode_rotation.1 = (bf16[2,12,128,128]{3,2,1,0:T(8,128)(2,1)S(1)}, f32[12,64,1]{2,1,0:T(8,128)S(1)}) custom-call(bf16[2,12,60,60]{3,2,1,0:T(8,128)(2,1)S(1)} %copy.12.modes_ref, f32[12,60]{1,0:T(8,128)S(1)} %copy-done.3), custom_call_target="tpu_custom_call" | custom-call | flops 2000000000 | bytes 6000000 | tf_op jit(solution)/shard_map/mode_rotation/pallas_call | solution.py:250
  25.3 0.0 collective-permute-done.6.refs_5_
  25.3 1.0 %lift.1.early_ref = bf16[192,4096]{1,0:T(8,128)(2,1)S(1)} custom-call(bf16[2,256,512]{2,1,0:T(8,128)(2,1)S(1)} %get-tuple-element.21.a_ref, bf16[64,1024]{1,0:T(8,128)(2,1)S(1)} %add_convert_fusion.1.refs_0_, bf16[64,1024]{1,0:T(8,128)(2,1)S(1)} %add_convert_fusion.refs_1_, bf16[64,1024]{1,0:T(8,128)(2,1)S(1)} %collective-permute-done.3.refs_2_, ...), custom_call_target="tpu_custom_call" | custom-call | flops 1000000000 | bytes 3000000 | tf_op jit(solution)/shard_map/lift/pallas_call | solution.py:287
  26.3 0.1 collective-permute-start.9
  26.4 1.2 %collective-permute-done.7.y0_ref = bf16[64,1024]{1,0:T(8,128)(2,1)S(1)} collective-permute-done((bf16[64,1024]{1,0:T(8,128)(2,1)S(1)}, bf16[64,1024]{1,0:T(8,128)(2,1)S(1)}, u32[]{:S(2)}, u32[]{:S(2)}) %collective-permute-start.7) | collective-permute-done | bytes 131104 | tf_op jit(solution)/shard_map/ppermute | solution.py:283
  27.5 0.0 collective-permute-start.10
  27.5 2.0 %collective-permute-done.8.y1_ref = bf16[64,1024]{1,0:T(8,128)(2,1)S(1)} collective-permute-done((bf16[64,1024]{1,0:T(8,128)(2,1)S(1)}, bf16[64,1024]{1,0:T(8,128)(2,1)S(1)}, u32[]{:S(2)}, u32[]{:S(2)}) %collective-permute-start.8) | collective-permute-done | bytes 131104 | tf_op jit(solution)/shard_map/ppermute | solution.py:283
  29.5 0.0 collective-permute-start.11
  29.5 2.6 %coupling.2 = (bf16[12,60,1024]{2,1,0:T(8,128)(2,1)S(1)}, f32[1,1024]{1,0:T(1,128)S(1)}) custom-call(bf16[192,4096]{1,0:T(8,128)(2,1)S(1)} %lift.1.early_ref, bf16[64,1024]{1,0:T(8,128)(2,1)S(1)} %collective-permute-done.7.y0_ref, bf16[64,1024]{1,0:T(8,128)(2,1)S(1)} %collective-permute-done.8.y1_ref, bf16[2,256,512]{2,1,0:T(8,128)(2,1)S(1)} %get-tuple-element.21.a_ref, ...), custom_call_target="tpu_custom_call" | custom-call | flops 40000000000 | bytes 120000000 | tf_op jit(solution)/shard_map/coupling/pallas_call | solution.py:301
  32.1 0.0 collective-permute-done.10.y0_ref
  32.1 0.0 collective-permute-done.11.y1_ref
  32.1 0.0 collective-permute-done.9.early_ref
  32.1 2.6 %coupling.3 = (bf16[12,60,1024]{2,1,0:T(8,128)(2,1)S(1)}, f32[1,1024]{1,0:T(1,128)S(1)}) custom-call(bf16[192,4096]{1,0:T(8,128)(2,1)S(1)} %collective-permute-done.9.early_ref, bf16[64,1024]{1,0:T(8,128)(2,1)S(1)} %collective-permute-done.10.y0_ref, bf16[64,1024]{1,0:T(8,128)(2,1)S(1)} %collective-permute-done.11.y1_ref, ...), custom_call_target="tpu_custom_call" | custom-call | flops 40000000000 | bytes 120000000 | tf_op jit(solution)/shard_map/coupling/pallas_call | solution.py:301
  34.8 0.9 %collective-permute-start.13 = (f32[2,1024]{1,0:T(2,128)S(1)}, f32[2,1024]{1,0:T(2,128)S(1)}, u32[]{:S(2)}, u32[]{:S(2)}) collective-permute-start(f32[2,1024]{1,0:T(2,128)S(1)} %maximum_select_fusion), channel_id=1, source_target_pairs={{0,4},{4,0},{8,12},{12,8},{1,5},{5,1},{9,13},{13,9},{2,6},{6,2},{1... | collective-permute-start | bytes 24584 | tf_op jit(solution)/shard_map/ppermute | solution.py:346
  35.7 1.0 %collective-permute-start.14 = (f32[2,1024]{1,0:T(2,128)S(1)}, f32[2,1024]{1,0:T(2,128)S(1)}, u32[]{:S(2)}, u32[]{:S(2)}) collective-permute-start(f32[2,1024]{1,0:T(2,128)S(1)} %maximum_select_fusion), channel_id=1, source_target_pairs={{0,5},{1,4},{4,1},{5,0},{8,13},{9,12},{12,9},{13,8},{2,7},{3,6},{6... | collective-permute-start | bytes 24584 | tf_op jit(solution)/shard_map/ppermute | solution.py:347
  36.7 0.3 collective-permute-start.12
  37.0 1.5 %order.2.refs_0_ = bf16[12,60,2,1024]{3,2,1,0:T(2,128)(2,1)} custom-call(bf16[12,60,1024]{2,1,0:T(8,128)(2,1)S(1)} %get-tuple-element.30.first_ref, bf16[12,60,1024]{2,1,0:T(8,128)(2,1)S(1)} %get-tuple-element.31.second_ref), custom_call_target="tpu_custom_call" | custom-call | flops 2000000000 | bytes 6000000 | tf_op jit(solution)/shard_map/order/pallas_call | solution.py:330
  38.5 0.0 collective-permute-done.13
  38.5 0.3 collective-permute-done.14
  38.8 0.0 collective-permute-done.12
  38.8 3.4 %collective-permute-start.15 = (f32[2,1024]{1,0:T(2,128)S(1)}, f32[2,1024]{1,0:T(2,128)S(1)}, u32[]{:S(2)}, u32[]{:S(2)}) collective-permute-start(f32[2,1024]{1,0:T(2,128)S(1)} %add_add_fusion), channel_id=1, source_target_pairs={{0,8},{4,12},{8,0},{12,4},{1,9},{5,13},{9,1},{13,5},{2,10},{6,14},... | collective-permute-start | bytes 24584 | tf_op jit(solution)/shard_map/ppermute | solution.py:352
  42.2 1.5 %order.3 = bf16[12,60,2,1024]{3,2,1,0:T(2,128)(2,1)} custom-call(bf16[12,60,1024]{2,1,0:T(8,128)(2,1)S(1)} %get-tuple-element.30.first_ref, bf16[12,60,1024]{2,1,0:T(8,128)(2,1)S(1)} %get-tuple-element.31.second_ref, bf16[12,60,2,1024]{3,2,1,0:T(2,128)(2,1)} %order.2.refs_0_), custom_call_target="tpu_custom_call", output_to_operand_aliasing={{}: (2, {})} | custom-call | flops 2000000000 | bytes 6000000 | tf_op jit(solution)/shard_map/order/pallas_call | solution.py:330
  43.7 0.1 collective-permute-done.15
  43.8 0.6 %add.23 = f32[2,1024]{1,0:T(2,128)} add(f32[2,1024]{1,0:T(2,128)S(1)} %add_add_fusion, f32[2,1024]{1,0:T(2,128)S(1)} %collective-permute-done.15) | non-fusion elementwise | flops 2048 | bytes 24576 | tf_op jit(solution)/shard_map/add | solution.py:352
  (4 shorter events, 0.1 us)
Async XLA Ops:
  1.3 0.9 %copy-start.1 = (bf16[2,1,2,30,1024]{4,2,3,1,0:T(2,128)(2,1)S(1)}, bf16[2,1,2,30,1024]{4,2,3,1,0:T(2,128)(2,1)}, u32[]{:S(2)}) copy-start(bf16[2,1,2,30,1024]{4,2,3,1,0:T(2,128)(2,1)} %param.9) | copy-start | bytes 737284
  2.3 3.5 %copy-start = (bf16[2,12,2,32,32]{4,3,2,1,0:T(8,128)(2,1)S(1)}, bf16[2,12,2,32,32]{4,3,2,1,0:T(8,128)(2,1)}, u32[]{:S(2)}) copy-start(bf16[2,12,2,32,32]{4,3,2,1,0:T(8,128)(2,1)} %u_kq_ref.1) | copy-start | bytes 294916
  2.3 3.5 %copy-start.2 = (bf16[2,2,32,32]{3,2,1,0:T(8,128)(2,1)S(1)}, bf16[2,2,32,32]{3,2,1,0:T(8,128)(2,1)}, u32[]{:S(2)}) copy-start(bf16[2,2,32,32]{3,2,1,0:T(8,128)(2,1)} %u_k_ref.1) | copy-start | bytes 24580
  2.3 3.5 %copy-start.4 = (s32[4,3]{1,0:T(4,128)S(1)}, s32[4,3]{1,0:T(4,128)}, u32[]{:S(2)}) copy-start(s32[4,3]{1,0:T(4,128)} %r_ref.1) | copy-start | bytes 148
  2.3 3.5 %copy-start.5 = (s32[24,3]{0,1:T(4,128)S(1)}, s32[24,3]{0,1:T(4,128)}, u32[]{:S(2)}) copy-start(s32[24,3]{0,1:T(4,128)} %param.13) | copy-start | bytes 868
  2.6 6.9 %collective-permute-start = (bf16[64,1024]{1,0:T(8,128)(2,1)S(1)}, bf16[64,1024]{1,0:T(8,128)(2,1)S(1)}, u32[]{:S(2)}, u32[]{:S(2)}) collective-permute-start(bf16[64,1024]{1,0:T(8,128)(2,1)S(1)} %get-tuple-element.23), channel_id=1, source_target_pairs={{0,2},{2,0},{1,3},{3,1},{4,6},{6,4},{5,7},{7,5},{8,10},{10,8},{9,1... | collective-permute-start | bytes 393224 | tf_op jit(solution)/shard_map/ppermute | solution.py:268
  5.6 8.8 %collective-permute-start.2 = (bf16[64,1024]{1,0:T(8,128)(2,1)S(1)}, bf16[64,1024]{1,0:T(8,128)(2,1)S(1)}, u32[]{:S(2)}, u32[]{:S(2)}) collective-permute-start(bf16[64,1024]{1,0:T(8,128)(2,1)S(1)} %get-tuple-element.25), channel_id=1, source_target_pairs={{0,3},{1,2},{2,1},{3,0},{4,7},{5,6},{6,5},{7,4},{8,11},{9,10},{10,... | collective-permute-start | bytes 393224 | tf_op jit(solution)/shard_map/ppermute | solution.py:269
  5.6 8.8 %collective-permute-start.1 = (f32[64,1024]{1,0:T(8,128)S(1)}, f32[64,1024]{1,0:T(8,128)S(1)}, u32[]{:S(2)}, u32[]{:S(2)}) collective-permute-start(f32[64,1024]{1,0:T(8,128)S(1)} %get-tuple-element.24), channel_id=1, source_target_pairs={{0,1},{1,0},{2,3},{3,2},{4,5},{5,4},{6,7},{7,6},{8,9},{9,8},{10,11... | collective-permute-start | bytes 786440 | tf_op jit(solution)/shard_map/ppermute | solution.py:263
  5.8 9.0 %copy-start.6 = (bf16[2,12,60,60]{3,0,2,1:T(2,128)(2,1)S(1)}, bf16[2,12,60,60]{3,0,2,1:T(2,128)(2,1)}, u32[]{:S(2)}) copy-start(bf16[2,12,60,60]{3,0,2,1:T(2,128)(2,1)} %param.16) | copy-start | bytes 518404
  7.1 17.5 %copy-start.3 = (f32[12,60]{1,0:T(8,128)S(1)}, f32[12,60]{1,0:T(8,128)}, u32[]{:S(2)}) copy-start(f32[12,60]{1,0:T(8,128)} %weights_ref.1) | copy-start | bytes 8644
  9.6 6.4 %collective-permute-start.5 = (bf16[64,1024]{1,0:T(8,128)(2,1)S(1)}, bf16[64,1024]{1,0:T(8,128)(2,1)S(1)}, u32[]{:S(2)}, u32[]{:S(2)}) collective-permute-start(bf16[64,1024]{1,0:T(8,128)(2,1)S(1)} %add_convert_fusion.1.refs_0_), channel_id=1, source_target_pairs={{0,4},{4,0},{8,12},{12,8},{1,5},{5,1},{9,13},{13,9},{2,6},{6,2},{1... | collective-permute-start | bytes 393224 | tf_op jit(solution)/shard_map/ppermute | solution.py:279
  11.8 10.6 %collective-permute-start.3 = (bf16[64,1024]{1,0:T(8,128)(2,1)S(1)}, bf16[64,1024]{1,0:T(8,128)(2,1)S(1)}, u32[]{:S(2)}, u32[]{:S(2)}) collective-permute-start(bf16[64,1024]{1,0:T(8,128)(2,1)S(1)} %add_convert_fusion.1.refs_0_), channel_id=1, source_target_pairs={{0,8},{4,12},{8,0},{12,4},{1,9},{5,13},{9,1},{13,5},{2,10},{6,14},... | collective-permute-start | bytes 393224 | tf_op jit(solution)/shard_map/ppermute | solution.py:279
  14.4 10.1 %collective-permute-start.4 = (bf16[64,1024]{1,0:T(8,128)(2,1)S(1)}, bf16[64,1024]{1,0:T(8,128)(2,1)S(1)}, u32[]{:S(2)}, u32[]{:S(2)}) collective-permute-start(bf16[64,1024]{1,0:T(8,128)(2,1)S(1)} %add_convert_fusion.refs_1_), channel_id=1, source_target_pairs={{0,8},{4,12},{8,0},{12,4},{1,9},{5,13},{9,1},{13,5},{2,10},{6,14},... | collective-permute-start | bytes 393224 | tf_op jit(solution)/shard_map/ppermute | solution.py:279
  14.9 10.4 %collective-permute-start.6 = (bf16[64,1024]{1,0:T(8,128)(2,1)S(1)}, bf16[64,1024]{1,0:T(8,128)(2,1)S(1)}, u32[]{:S(2)}, u32[]{:S(2)}) collective-permute-start(bf16[64,1024]{1,0:T(8,128)(2,1)S(1)} %add_convert_fusion.refs_1_), channel_id=1, source_target_pairs={{0,4},{4,0},{8,12},{12,8},{1,5},{5,1},{9,13},{13,9},{2,6},{6,2},{1... | collective-permute-start | bytes 393224 | tf_op jit(solution)/shard_map/ppermute | solution.py:279
  22.4 5.1 %collective-permute-start.7 = (bf16[64,1024]{1,0:T(8,128)(2,1)S(1)}, bf16[64,1024]{1,0:T(8,128)(2,1)S(1)}, u32[]{:S(2)}, u32[]{:S(2)}) collective-permute-start(bf16[64,1024]{1,0:T(8,128)(2,1)S(1)} %collective-permute-done.3.refs_2_), channel_id=1, source_target_pairs={{0,4},{4,0},{8,12},{12,8},{1,5},{5,1},{9,13},{13,9},{2,6},{6,2},{1... | collective-permute-start | bytes 393224 | tf_op jit(solution)/shard_map/ppermute | solution.py:283
  24.5 5.0 %collective-permute-start.8 = (bf16[64,1024]{1,0:T(8,128)(2,1)S(1)}, bf16[64,1024]{1,0:T(8,128)(2,1)S(1)}, u32[]{:S(2)}, u32[]{:S(2)}) collective-permute-start(bf16[64,1024]{1,0:T(8,128)(2,1)S(1)} %collective-permute-done.4.refs_3_), channel_id=1, source_target_pairs={{0,4},{4,0},{8,12},{12,8},{1,5},{5,1},{9,13},{13,9},{2,6},{6,2},{1... | collective-permute-start | bytes 393224 | tf_op jit(solution)/shard_map/ppermute | solution.py:283
  26.3 5.9 %collective-permute-start.9 = (bf16[192,4096]{1,0:T(8,128)(2,1)S(1)}, bf16[192,4096]{1,0:T(8,128)(2,1)S(1)}, u32[]{:S(2)}, u32[]{:S(2)}) collective-permute-start(bf16[192,4096]{1,0:T(8,128)(2,1)S(1)} %lift.1.early_ref), channel_id=1, source_target_pairs={{0,1},{1,0},{2,3},{3,2},{4,5},{5,4},{6,7},{7,6},{8,9},{9,8},{10,11... | collective-permute-start | bytes 4718600 | tf_op jit(solution)/shard_map/ppermute | solution.py:296
  27.5 4.6 %collective-permute-start.10 = (bf16[64,1024]{1,0:T(8,128)(2,1)S(1)}, bf16[64,1024]{1,0:T(8,128)(2,1)S(1)}, u32[]{:S(2)}, u32[]{:S(2)}) collective-permute-start(bf16[64,1024]{1,0:T(8,128)(2,1)S(1)} %collective-permute-done.7.y0_ref), channel_id=1, source_target_pairs={{0,1},{1,0},{2,3},{3,2},{4,5},{5,4},{6,7},{7,6},{8,9},{9,8},{10,11... | collective-permute-start | bytes 393224 | tf_op jit(solution)/shard_map/ppermute | solution.py:297
  29.5 2.6 %collective-permute-start.11 = (bf16[64,1024]{1,0:T(8,128)(2,1)S(1)}, bf16[64,1024]{1,0:T(8,128)(2,1)S(1)}, u32[]{:S(2)}, u32[]{:S(2)}) collective-permute-start(bf16[64,1024]{1,0:T(8,128)(2,1)S(1)} %collective-permute-done.8.y1_ref), channel_id=1, source_target_pairs={{0,1},{1,0},{2,3},{3,2},{4,5},{5,4},{6,7},{7,6},{8,9},{9,8},{10,11... | collective-permute-start | bytes 393224 | tf_op jit(solution)/shard_map/ppermute | solution.py:297
  34.8 3.7 %collective-permute-start.13 = (f32[2,1024]{1,0:T(2,128)S(1)}, f32[2,1024]{1,0:T(2,128)S(1)}, u32[]{:S(2)}, u32[]{:S(2)}) collective-permute-start(f32[2,1024]{1,0:T(2,128)S(1)} %maximum_select_fusion), channel_id=1, source_target_pairs={{0,4},{4,0},{8,12},{12,8},{1,5},{5,1},{9,13},{13,9},{2,6},{6,2},{1... | collective-permute-start | bytes 24584 | tf_op jit(solution)/shard_map/ppermute | solution.py:346
  35.7 3.1 %collective-permute-start.14 = (f32[2,1024]{1,0:T(2,128)S(1)}, f32[2,1024]{1,0:T(2,128)S(1)}, u32[]{:S(2)}, u32[]{:S(2)}) collective-permute-start(f32[2,1024]{1,0:T(2,128)S(1)} %maximum_select_fusion), channel_id=1, source_target_pairs={{0,5},{1,4},{4,1},{5,0},{8,13},{9,12},{12,9},{13,8},{2,7},{3,6},{6... | collective-permute-start | bytes 24584 | tf_op jit(solution)/shard_map/ppermute | solution.py:347
  36.7 2.1 %collective-permute-start.12 = (f32[2,1024]{1,0:T(2,128)S(1)}, f32[2,1024]{1,0:T(2,128)S(1)}, u32[]{:S(2)}, u32[]{:S(2)}) collective-permute-start(f32[2,1024]{1,0:T(2,128)S(1)} %maximum_select_fusion), channel_id=1, source_target_pairs={{0,1},{1,0},{2,3},{3,2},{4,5},{5,4},{6,7},{7,6},{8,9},{9,8},{10,11... | collective-permute-start | bytes 24584 | tf_op jit(solution)/shard_map/ppermute | solution.py:348
  38.8 5.0 %collective-permute-start.15 = (f32[2,1024]{1,0:T(2,128)S(1)}, f32[2,1024]{1,0:T(2,128)S(1)}, u32[]{:S(2)}, u32[]{:S(2)}) collective-permute-start(f32[2,1024]{1,0:T(2,128)S(1)} %add_add_fusion), channel_id=1, source_target_pairs={{0,8},{4,12},{8,0},{12,4},{1,9},{5,13},{9,1},{13,5},{2,10},{6,14},... | collective-permute-start | bytes 24584 | tf_op jit(solution)/shard_map/ppermute | solution.py:352

commit v4 on v3

--- a/solution.py
+++ b/solution.py
@@ -45,20 +45,19 @@
                 turns.append(jnp.full((1, 128), wrap(t), jnp.int32))
     cos, sin = phases(jnp.concatenate(turns, 0))
     wide = half * rows_e
-    at = lax.broadcasted_iota(jnp.int32, (MODE_PAD, 2 * wide), 0)
-    lane = lax.broadcasted_iota(jnp.int32, (MODE_PAD, 2 * wide), 1)
-    imag = lane >= wide
-    own = jnp.where(imag, lane - wide, lane) - at * rows_e
-    rows = []
+    at = lax.broadcasted_iota(jnp.int32, (2 * MODE_PAD, 2 * wide), 0)
+    lane = lax.broadcasted_iota(jnp.int32, (2 * MODE_PAD, 2 * wide), 1)
+    imag, to_imag = lane >= wide, at >= half
+    own = jnp.where(imag, lane - wide, lane) - jnp.where(to_imag, at - half, at) * rows_e
+    same = imag == to_imag
+    sign = jnp.where(to_imag, 1.0, -1.0)
     for i in range(n_ea * n_k):
-        for out in range(2):
-            value = jnp.zeros((MODE_PAD, 2 * wide), F32)
-            for e in range(rows_e):
-                j = i * rows_e + e
-                c, d = cos[j : j + 1, : 2 * wide], sin[j : j + 1, : 2 * wide]
-                value = jnp.where(own == e, jnp.where(imag, c, d) if out else jnp.where(imag, -d, c), value)
-            rows.append(value)
-    factor_ref[...] = jnp.concatenate(rows, 0).astype(BF16)
+        value = jnp.zeros((2 * MODE_PAD, 2 * wide), F32)
+        for e in range(rows_e):
+            j = i * rows_e + e
+            c, d = cos[j : j + 1, : 2 * wide], sin[j : j + 1, : 2 * wide]
+            value = jnp.where(own == e, jnp.where(same, c, sign * d), value)
+        factor_ref[i * 2 * MODE_PAD : (i + 1) * 2 * MODE_PAD] = value.astype(BF16)
 
 
 def electron_kernel(factor_ref, table_ref, *outs):
@@ -66,7 +65,9 @@
     data = jnp.concatenate([table_ref[c, 0].reshape(half * rows_e, pairs) for c in range(2)], 0)
     total = jnp.dot(factor_ref[...], data, preferred_element_type=F32)
     for i, out in enumerate(outs):
-        out[...] = total[i * 2 * MODE_PAD : (i + 1) * 2 * MODE_PAD].astype(out.dtype)
+        part = total[i * 2 * MODE_PAD : i * 2 * MODE_PAD + 2 * half]
+        part = jnp.concatenate([part[:, : pairs // 2], part[:, pairs // 2 :]], 0)
+        out[...] = part.astype(out.dtype)
 
 
 def rotation_kernel(masks, r_ref, q_ref, u_k_ref, u_kq_ref, left_ref, kron_ref):
@@ -127,14 +128,21 @@
 
 
 def lift(a_mat, y_refs, x_ref, first_row, width):
-    quarter = MODE_PAD
+    half = y_refs[0].shape[0] // 4
+    gap = jnp.zeros((MODE_PAD - half, 8 * width), F32)
     for t in range(width // 16):
         parts = []
         for u in range(2):
-            lanes = slice((2 * t + u) * 8 * width, (2 * t + u + 1) * 8 * width)
-            p = [ref[i * quarter : (i + 1) * quarter, lanes] for ref in y_refs for i in range(2)]
-            y = jnp.concatenate(p, 0)
-            turned = jnp.concatenate([-p[1], p[0], -p[3], p[2]], 0)
+            chunk = 2 * t + u
+            lanes = chunk % (width // 16) * 8 * width
+            first = chunk // (width // 16) * 2 * half
+            y, turned = [], []
+            for ref in y_refs:
+                rows = ref[:, lanes : lanes + 8 * width].astype(F32)
+                r, i = rows[first : first + half], rows[first + half : first + 2 * half]
+                y += [r, gap, i, gap]
+                turned += [-i, gap, r, gap]
+            y, turned = (jnp.concatenate(z, 0).astype(BF16) for z in (y, turned))
             rhs = jnp.concatenate(
                 [jnp.concatenate([y, turned], 1), jnp.concatenate([turned, -y], 1)], 0
             )
@@ -219,7 +227,7 @@
     parts = pl.pallas_call(
         electron_kernel,
         out_shape=[
-            jax.ShapeDtypeStruct((2 * MODE_PAD, pairs), F32 if i < k_rows else BF16)
+            jax.ShapeDtypeStruct((4 * half, pairs // 2), F32 if i < k_rows else BF16)
             for i in range(n_parts)
         ],
         in_specs=[VMEM, VMEM],

time: 44.6 us -> 43.6 us (0.978)
  waiting for transfers between devices: 14.5 us -> 13.4 us
    ppermute x4, waiting for transfers between devices: 8.49 us -> 7.92 us  [body(): came = [lax.ppermute(blocks[0], 'pb', flip(n_pb, distance))]]
  transfers between devices with their start and end apart: 16 -> 16, of which waited for: 8 -> 7; matrix products, arithmetic and copies ran while one was open for 0% -> 0% of each run, Pallas kernels for 19% -> 20%
where the time goes in v4:
time: 43.6 us; the launch traced here: 43.5 us
  starting transfers between devices  15.4 us (35%)
  waiting for transfers between devices  13.4 us (31%)
  Pallas kernels  12.2 us (28%)
  other arithmetic  1.4 us (3%)
  between operations  0.8 us (2%)
    ppermute x4, waiting for transfers between devices, body(): came = [lax.ppermute(blocks[0], 'pb', flip(n_pb, distance))]  7.92 us
    ppermute x4, starting transfers between devices, body(): came = [lax.ppermute(blocks[0], 'pb', flip(n_pb, distance))]  6.13 us
    pallas_call x2, Pallas kernels, body(): pl.pallas_call(functools.partial(coupling_kernel, k, width, modes, q_rows...  5.28 us
    ppermute x1, starting transfers between devices, body(): mean = mean + lax.ppermute(mean, 'pb', flip(n_pb, distance))  3.47 us
    ppermute x1, starting transfers between devices, body(): mine.append(lax.ppermute(parts[s * k_rows], 'ea', shift(n_ea, s)))  3 us
    pallas_call x2, Pallas kernels, body(): pl.pallas_call(order_kernel, grid=(1,), out_shape=jax.ShapeDtypeStruct((q...  2.97 us
    ppermute x2, waiting for transfers between devices, body(): came.append(lax.ppermute(y, 'pb', flip(n_pb, distance)))  2.97 us
    ppermute x1, waiting for transfers between devices, body(): mine.append(lax.ppermute(parts[s * k_rows], 'ea', shift(n_ea, s)))  2.22 us
  transfers between devices with their start and end apart: 16, of which 7 were waited for; matrix products, arithmetic and copies ran while one was open for 0% of the time, Pallas kernels for 20%

profile of v4, /device:TPU:0, one launch (start us, length us, event | category | flops | bytes accessed | tf_op | source)
XLA Modules:
  0.0 43.5 jit_solution(1956756075814790153)
XLA Ops:
  0.6 0.7 %pad_add_fusion.coords_ref = s32[6,3]{1,0:T(8,128)S(1)} fusion(s32[2,3]{1,0:T(2,128)} %param.10, s32[4,3]{1,0:T(4,128)} %param.12), kind=kLoop, calls=%fused_computation.4 | loop fusion | flops 18 | bytes 144 | tf_op jit(solution)/shard_map/concatenate | solution.py:226
  1.3 0.0 copy-start.1
  1.3 0.7 %electron_phases.1.factor_ref = bf16[256,120]{1,0:T(8,128)(2,1)S(1)} custom-call(s32[6,3]{1,0:T(8,128)S(1)} %pad_add_fusion.coords_ref), custom_call_target="tpu_custom_call" | custom-call | flops 2000000000 | bytes 6000000 | tf_op jit(solution)/shard_map/electron_phases/pallas_call | solution.py:218
  2.1 0.2 copy-done.1
  2.3 0.0 copy-start
  2.3 0.0 copy-start.2
  2.3 0.0 copy-start.4
  2.3 0.0 copy-start.5
  2.3 0.3 electron_sum.1
  2.6 3.0 %collective-permute-start = (bf16[120,512]{1,0:T(8,128)(2,1)S(1)}, bf16[120,512]{1,0:T(8,128)(2,1)S(1)}, u32[]{:S(2)}, u32[]{:S(2)}) collective-permute-start(bf16[120,512]{1,0:T(8,128)(2,1)S(1)} %get-tuple-element.23), channel_id=1, source_target_pairs={{0,2},{2,0},{1,3},{3,1},{4,6},{6,4},{5,7},{7,5},{8,10},{10,8},{9,1... | collective-permute-start | bytes 368648 | tf_op jit(solution)/shard_map/ppermute | solution.py:276
  5.6 0.0 collective-permute-start.2
  5.6 0.2 collective-permute-start.1
  5.8 0.0 copy-done
  5.8 0.0 copy-done.2
  5.8 0.0 copy-done.4
  5.8 0.0 copy-done.5
  5.8 0.0 copy-start.6
  5.8 1.3 %rotations.1 = (bf16[2,384,256]{2,1,0:T(8,128)(2,1)S(1)}, bf16[2,256,512]{2,1,0:T(8,128)(2,1)S(1)}) custom-call(s32[4,3]{1,0:T(4,128)S(1)} %copy-done.4, s32[3,24]{1,0:T(4,128)S(1)} %bitcast.4, bf16[2,2,32,32]{3,2,1,0:T(8,128)(2,1)S(1)} %copy-done.2, bf16[2,12,2,32,32]{4,3,2,1,0:T(8,128)(2,1)S(1)} %copy-done), custom_call_target="tpu_custom_call" | custom-call | flops 2000000000 | bytes 6000000 | tf_op jit(solution)/shard_map/rotations/pallas_call | solution.py:245
  7.1 0.0 copy-start.3
  7.1 2.2 %collective-permute-done = bf16[120,512]{1,0:T(8,128)(2,1)S(1)} collective-permute-done((bf16[120,512]{1,0:T(8,128)(2,1)S(1)}, bf16[120,512]{1,0:T(8,128)(2,1)S(1)}, u32[]{:S(2)}, u32[]{:S(2)}) %collective-permute-start) | collective-permute-done | bytes 122912 | tf_op jit(solution)/shard_map/ppermute | solution.py:276
  9.4 2.1 %collective-permute-start.5 = (bf16[120,512]{1,0:T(8,128)(2,1)S(1)}, bf16[120,512]{1,0:T(8,128)(2,1)S(1)}, u32[]{:S(2)}, u32[]{:S(2)}) collective-permute-start(bf16[120,512]{1,0:T(8,128)(2,1)S(1)} %add_convert_fusion.1.refs_0_), channel_id=1, source_target_pairs={{0,4},{4,0},{8,12},{12,8},{1,5},{5,1},{9,13},{13,9},{2,6},{6,2},{1... | collective-permute-start | bytes 368648 | tf_op jit(solution)/shard_map/ppermute | solution.py:287
  11.4 2.6 %collective-permute-start.3 = (bf16[120,512]{1,0:T(8,128)(2,1)S(1)}, bf16[120,512]{1,0:T(8,128)(2,1)S(1)}, u32[]{:S(2)}, u32[]{:S(2)}) collective-permute-start(bf16[120,512]{1,0:T(8,128)(2,1)S(1)} %add_convert_fusion.1.refs_0_), channel_id=1, source_target_pairs={{0,8},{4,12},{8,0},{12,4},{1,9},{5,13},{9,1},{13,5},{2,10},{6,14},... | collective-permute-start | bytes 368648 | tf_op jit(solution)/shard_map/ppermute | solution.py:287
  14.0 0.0 collective-permute-done.2
  14.0 0.0 collective-permute-done.1
  14.1 0.4 collective-permute-start.4
  14.4 0.0 copy-done.6
  14.4 0.1 copy.12.modes_ref
  14.5 1.1 %collective-permute-start.6 = (bf16[120,512]{1,0:T(8,128)(2,1)S(1)}, bf16[120,512]{1,0:T(8,128)(2,1)S(1)}, u32[]{:S(2)}, u32[]{:S(2)}) collective-permute-start(bf16[120,512]{1,0:T(8,128)(2,1)S(1)} %add_convert_fusion.refs_1_), channel_id=1, source_target_pairs={{0,4},{4,0},{8,12},{12,8},{1,5},{5,1},{9,13},{13,9},{2,6},{6,2},{1... | collective-permute-start | bytes 368648 | tf_op jit(solution)/shard_map/ppermute | solution.py:287
  15.6 0.0 collective-permute-done.5.refs_4_
  15.6 6.2 %collective-permute-done.3.refs_2_ = bf16[120,512]{1,0:T(8,128)(2,1)S(1)} collective-permute-done((bf16[120,512]{1,0:T(8,128)(2,1)S(1)}, bf16[120,512]{1,0:T(8,128)(2,1)S(1)}, u32[]{:S(2)}, u32[]{:S(2)}) %collective-permute-start.3) | collective-permute-done | bytes 122912 | tf_op jit(solution)/shard_map/ppermute | solution.py:287
  21.8 0.2 collective-permute-start.7
  21.9 1.8 %collective-permute-done.4.refs_3_ = bf16[120,512]{1,0:T(8,128)(2,1)S(1)} collective-permute-done((bf16[120,512]{1,0:T(8,128)(2,1)S(1)}, bf16[120,512]{1,0:T(8,128)(2,1)S(1)}, u32[]{:S(2)}, u32[]{:S(2)}) %collective-permute-start.4) | collective-permute-done | bytes 122912 | tf_op jit(solution)/shard_map/ppermute | solution.py:287
  23.7 0.1 collective-permute-start.8
  23.8 0.0 copy-done.3
  23.8 0.7 %mode_rotation.1 = (bf16[2,12,128,128]{3,2,1,0:T(8,128)(2,1)S(1)}, f32[12,64,1]{2,1,0:T(8,128)S(1)}) custom-call(bf16[2,12,60,60]{3,2,1,0:T(8,128)(2,1)S(1)} %copy.12.modes_ref, f32[12,60]{1,0:T(8,128)S(1)} %copy-done.3), custom_call_target="tpu_custom_call" | custom-call | flops 2000000000 | bytes 6000000 | tf_op jit(solution)/shard_map/mode_rotation/pallas_call | solution.py:258
  24.5 0.0 collective-permute-done.6.refs_5_
  24.5 1.0 %lift.1.early_ref = bf16[192,4096]{1,0:T(8,128)(2,1)S(1)} custom-call(bf16[2,256,512]{2,1,0:T(8,128)(2,1)S(1)} %get-tuple-element.21.a_ref, bf16[120,512]{1,0:T(8,128)(2,1)S(1)} %add_convert_fusion.1.refs_0_, bf16[120,512]{1,0:T(8,128)(2,1)S(1)} %add_convert_fusion.refs_1_, bf16[120,512]{1,0:T(8,128)(2,1)S(1)} %collective-permute-done.3.refs_2_, ...), custom_call_target="tpu_custom_call" | custom-call | flops 1000000000 | bytes 3000000 | tf_op jit(solution)/shard_map/lift/pallas_call | solution.py:295
  25.5 0.1 collective-permute-start.9
  25.6 1.1 %collective-permute-done.7.y0_ref = bf16[120,512]{1,0:T(8,128)(2,1)S(1)} collective-permute-done((bf16[120,512]{1,0:T(8,128)(2,1)S(1)}, bf16[120,512]{1,0:T(8,128)(2,1)S(1)}, u32[]{:S(2)}, u32[]{:S(2)}) %collective-permute-start.7) | collective-permute-done | bytes 122912 | tf_op jit(solution)/shard_map/ppermute | solution.py:291
  26.7 0.0 collective-permute-start.10
  26.7 1.9 %collective-permute-done.8.y1_ref = bf16[120,512]{1,0:T(8,128)(2,1)S(1)} collective-permute-done((bf16[120,512]{1,0:T(8,128)(2,1)S(1)}, bf16[120,512]{1,0:T(8,128)(2,1)S(1)}, u32[]{:S(2)}, u32[]{:S(2)}) %collective-permute-start.8) | collective-permute-done | bytes 122912 | tf_op jit(solution)/shard_map/ppermute | solution.py:291
  28.6 0.0 collective-permute-start.11
  28.6 2.6 %coupling.2 = (bf16[12,60,1024]{2,1,0:T(8,128)(2,1)S(1)}, f32[1,1024]{1,0:T(1,128)S(1)}) custom-call(bf16[192,4096]{1,0:T(8,128)(2,1)S(1)} %lift.1.early_ref, bf16[120,512]{1,0:T(8,128)(2,1)S(1)} %collective-permute-done.7.y0_ref, bf16[120,512]{1,0:T(8,128)(2,1)S(1)} %collective-permute-done.8.y1_ref, bf16[2,256,512]{2,1,0:T(8,128)(2,1)S(1)} %get-tuple-element.21.a_ref, ...), custom_call_target="tpu_custom_call" | custom-call | flops 40000000000 | bytes 120000000 | tf_op jit(solution)/shard_map/coupling/pallas_call | solution.py:309
  31.2 0.0 collective-permute-done.10.y0_ref
  31.2 0.0 collective-permute-done.11.y1_ref
  31.2 0.0 collective-permute-done.9.early_ref
  31.2 2.7 %coupling.3 = (bf16[12,60,1024]{2,1,0:T(8,128)(2,1)S(1)}, f32[1,1024]{1,0:T(1,128)S(1)}) custom-call(bf16[192,4096]{1,0:T(8,128)(2,1)S(1)} %collective-permute-done.9.early_ref, bf16[120,512]{1,0:T(8,128)(2,1)S(1)} %collective-permute-done.10.y0_ref, bf16[120,512]{1,0:T(8,128)(2,1)S(1)} %collective-permute-done.11.y1_ref, ...), custom_call_target="tpu_custom_call" | custom-call | flops 40000000000 | bytes 120000000 | tf_op jit(solution)/shard_map/coupling/pallas_call | solution.py:309
  33.9 0.7 %collective-permute-start.13 = (f32[2,1024]{1,0:T(2,128)S(1)}, f32[2,1024]{1,0:T(2,128)S(1)}, u32[]{:S(2)}, u32[]{:S(2)}) collective-permute-start(f32[2,1024]{1,0:T(2,128)S(1)} %maximum_select_fusion), channel_id=1, source_target_pairs={{0,4},{4,0},{8,12},{12,8},{1,5},{5,1},{9,13},{13,9},{2,6},{6,2},{1... | collective-permute-start | bytes 24584 | tf_op jit(solution)/shard_map/ppermute | solution.py:354
  34.6 1.2 %collective-permute-start.14 = (f32[2,1024]{1,0:T(2,128)S(1)}, f32[2,1024]{1,0:T(2,128)S(1)}, u32[]{:S(2)}, u32[]{:S(2)}) collective-permute-start(f32[2,1024]{1,0:T(2,128)S(1)} %maximum_select_fusion), channel_id=1, source_target_pairs={{0,5},{1,4},{4,1},{5,0},{8,13},{9,12},{12,9},{13,8},{2,7},{3,6},{6... | collective-permute-start | bytes 24584 | tf_op jit(solution)/shard_map/ppermute | solution.py:355
  35.9 0.3 collective-permute-start.12
  36.1 1.5 %order.2.refs_0_ = bf16[12,60,2,1024]{3,2,1,0:T(2,128)(2,1)} custom-call(bf16[12,60,1024]{2,1,0:T(8,128)(2,1)S(1)} %get-tuple-element.30.first_ref, bf16[12,60,1024]{2,1,0:T(8,128)(2,1)S(1)} %get-tuple-element.31.second_ref), custom_call_target="tpu_custom_call" | custom-call | flops 2000000000 | bytes 6000000 | tf_op jit(solution)/shard_map/order/pallas_call | solution.py:338
  37.6 0.1 collective-permute-done.13
  37.7 0.0 collective-permute-done.14
  37.7 0.0 collective-permute-done.12
  37.8 3.5 %collective-permute-start.15 = (f32[2,1024]{1,0:T(2,128)S(1)}, f32[2,1024]{1,0:T(2,128)S(1)}, u32[]{:S(2)}, u32[]{:S(2)}) collective-permute-start(f32[2,1024]{1,0:T(2,128)S(1)} %add_add_fusion), channel_id=1, source_target_pairs={{0,8},{4,12},{8,0},{12,4},{1,9},{5,13},{9,1},{13,5},{2,10},{6,14},... | collective-permute-start | bytes 24584 | tf_op jit(solution)/shard_map/ppermute | solution.py:360
  41.2 1.5 %order.3 = bf16[12,60,2,1024]{3,2,1,0:T(2,128)(2,1)} custom-call(bf16[12,60,1024]{2,1,0:T(8,128)(2,1)S(1)} %get-tuple-element.30.first_ref, bf16[12,60,1024]{2,1,0:T(8,128)(2,1)S(1)} %get-tuple-element.31.second_ref, bf16[12,60,2,1024]{3,2,1,0:T(2,128)(2,1)} %order.2.refs_0_), custom_call_target="tpu_custom_call", output_to_operand_aliasing={{}: (2, {})} | custom-call | flops 2000000000 | bytes 6000000 | tf_op jit(solution)/shard_map/order/pallas_call | solution.py:338
  42.7 0.1 collective-permute-done.15
  42.9 0.6 %add.23 = f32[2,1024]{1,0:T(2,128)} add(f32[2,1024]{1,0:T(2,128)S(1)} %add_add_fusion, f32[2,1024]{1,0:T(2,128)S(1)} %collective-permute-done.15) | non-fusion elementwise | flops 2048 | bytes 24576 | tf_op jit(solution)/shard_map/add | solution.py:360
  (4 shorter events, 0.1 us)
Async XLA Ops:
  1.3 0.9 %copy-start.1 = (bf16[2,1,2,30,1024]{4,2,3,1,0:T(2,128)(2,1)S(1)}, bf16[2,1,2,30,1024]{4,2,3,1,0:T(2,128)(2,1)}, u32[]{:S(2)}) copy-start(bf16[2,1,2,30,1024]{4,2,3,1,0:T(2,128)(2,1)} %param.9) | copy-start | bytes 737284
  2.3 3.5 %copy-start = (bf16[2,12,2,32,32]{4,3,2,1,0:T(8,128)(2,1)S(1)}, bf16[2,12,2,32,32]{4,3,2,1,0:T(8,128)(2,1)}, u32[]{:S(2)}) copy-start(bf16[2,12,2,32,32]{4,3,2,1,0:T(8,128)(2,1)} %u_kq_ref.1) | copy-start | bytes 294916
  2.3 3.5 %copy-start.2 = (bf16[2,2,32,32]{3,2,1,0:T(8,128)(2,1)S(1)}, bf16[2,2,32,32]{3,2,1,0:T(8,128)(2,1)}, u32[]{:S(2)}) copy-start(bf16[2,2,32,32]{3,2,1,0:T(8,128)(2,1)} %u_k_ref.1) | copy-start | bytes 24580
  2.3 3.5 %copy-start.4 = (s32[4,3]{1,0:T(4,128)S(1)}, s32[4,3]{1,0:T(4,128)}, u32[]{:S(2)}) copy-start(s32[4,3]{1,0:T(4,128)} %r_ref.1) | copy-start | bytes 148
  2.3 3.5 %copy-start.5 = (s32[24,3]{0,1:T(4,128)S(1)}, s32[24,3]{0,1:T(4,128)}, u32[]{:S(2)}) copy-start(s32[24,3]{0,1:T(4,128)} %param.13) | copy-start | bytes 868
  2.6 6.7 %collective-permute-start = (bf16[120,512]{1,0:T(8,128)(2,1)S(1)}, bf16[120,512]{1,0:T(8,128)(2,1)S(1)}, u32[]{:S(2)}, u32[]{:S(2)}) collective-permute-start(bf16[120,512]{1,0:T(8,128)(2,1)S(1)} %get-tuple-element.23), channel_id=1, source_target_pairs={{0,2},{2,0},{1,3},{3,1},{4,6},{6,4},{5,7},{7,5},{8,10},{10,8},{9,1... | collective-permute-start | bytes 368648 | tf_op jit(solution)/shard_map/ppermute | solution.py:276
  5.6 8.4 %collective-permute-start.2 = (bf16[120,512]{1,0:T(8,128)(2,1)S(1)}, bf16[120,512]{1,0:T(8,128)(2,1)S(1)}, u32[]{:S(2)}, u32[]{:S(2)}) collective-permute-start(bf16[120,512]{1,0:T(8,128)(2,1)S(1)} %get-tuple-element.25), channel_id=1, source_target_pairs={{0,3},{1,2},{2,1},{3,0},{4,7},{5,6},{6,5},{7,4},{8,11},{9,10},{10,... | collective-permute-start | bytes 368648 | tf_op jit(solution)/shard_map/ppermute | solution.py:277
  5.6 8.4 %collective-permute-start.1 = (f32[120,512]{1,0:T(8,128)S(1)}, f32[120,512]{1,0:T(8,128)S(1)}, u32[]{:S(2)}, u32[]{:S(2)}) collective-permute-start(f32[120,512]{1,0:T(8,128)S(1)} %get-tuple-element.24), channel_id=1, source_target_pairs={{0,1},{1,0},{2,3},{3,2},{4,5},{5,4},{6,7},{7,6},{8,9},{9,8},{10,11... | collective-permute-start | bytes 737288 | tf_op jit(solution)/shard_map/ppermute | solution.py:271
  5.8 8.6 %copy-start.6 = (bf16[2,12,60,60]{3,0,2,1:T(2,128)(2,1)S(1)}, bf16[2,12,60,60]{3,0,2,1:T(2,128)(2,1)}, u32[]{:S(2)}) copy-start(bf16[2,12,60,60]{3,0,2,1:T(2,128)(2,1)} %param.16) | copy-start | bytes 518404
  7.1 16.7 %copy-start.3 = (f32[12,60]{1,0:T(8,128)S(1)}, f32[12,60]{1,0:T(8,128)}, u32[]{:S(2)}) copy-start(f32[12,60]{1,0:T(8,128)} %weights_ref.1) | copy-start | bytes 8644
  9.4 6.3 %collective-permute-start.5 = (bf16[120,512]{1,0:T(8,128)(2,1)S(1)}, bf16[120,512]{1,0:T(8,128)(2,1)S(1)}, u32[]{:S(2)}, u32[]{:S(2)}) collective-permute-start(bf16[120,512]{1,0:T(8,128)(2,1)S(1)} %add_convert_fusion.1.refs_0_), channel_id=1, source_target_pairs={{0,4},{4,0},{8,12},{12,8},{1,5},{5,1},{9,13},{13,9},{2,6},{6,2},{1... | collective-permute-start | bytes 368648 | tf_op jit(solution)/shard_map/ppermute | solution.py:287
  11.4 10.4 %collective-permute-start.3 = (bf16[120,512]{1,0:T(8,128)(2,1)S(1)}, bf16[120,512]{1,0:T(8,128)(2,1)S(1)}, u32[]{:S(2)}, u32[]{:S(2)}) collective-permute-start(bf16[120,512]{1,0:T(8,128)(2,1)S(1)} %add_convert_fusion.1.refs_0_), channel_id=1, source_target_pairs={{0,8},{4,12},{8,0},{12,4},{1,9},{5,13},{9,1},{13,5},{2,10},{6,14},... | collective-permute-start | bytes 368648 | tf_op jit(solution)/shard_map/ppermute | solution.py:287
  14.1 9.6 %collective-permute-start.4 = (bf16[120,512]{1,0:T(8,128)(2,1)S(1)}, bf16[120,512]{1,0:T(8,128)(2,1)S(1)}, u32[]{:S(2)}, u32[]{:S(2)}) collective-permute-start(bf16[120,512]{1,0:T(8,128)(2,1)S(1)} %add_convert_fusion.refs_1_), channel_id=1, source_target_pairs={{0,8},{4,12},{8,0},{12,4},{1,9},{5,13},{9,1},{13,5},{2,10},{6,14},... | collective-permute-start | bytes 368648 | tf_op jit(solution)/shard_map/ppermute | solution.py:287
  14.5 10.0 %collective-permute-start.6 = (bf16[120,512]{1,0:T(8,128)(2,1)S(1)}, bf16[120,512]{1,0:T(8,128)(2,1)S(1)}, u32[]{:S(2)}, u32[]{:S(2)}) collective-permute-start(bf16[120,512]{1,0:T(8,128)(2,1)S(1)} %add_convert_fusion.refs_1_), channel_id=1, source_target_pairs={{0,4},{4,0},{8,12},{12,8},{1,5},{5,1},{9,13},{13,9},{2,6},{6,2},{1... | collective-permute-start | bytes 368648 | tf_op jit(solution)/shard_map/ppermute | solution.py:287
  21.8 4.9 %collective-permute-start.7 = (bf16[120,512]{1,0:T(8,128)(2,1)S(1)}, bf16[120,512]{1,0:T(8,128)(2,1)S(1)}, u32[]{:S(2)}, u32[]{:S(2)}) collective-permute-start(bf16[120,512]{1,0:T(8,128)(2,1)S(1)} %collective-permute-done.3.refs_2_), channel_id=1, source_target_pairs={{0,4},{4,0},{8,12},{12,8},{1,5},{5,1},{9,13},{13,9},{2,6},{6,2},{1... | collective-permute-start | bytes 368648 | tf_op jit(solution)/shard_map/ppermute | solution.py:291
  23.7 4.9 %collective-permute-start.8 = (bf16[120,512]{1,0:T(8,128)(2,1)S(1)}, bf16[120,512]{1,0:T(8,128)(2,1)S(1)}, u32[]{:S(2)}, u32[]{:S(2)}) collective-permute-start(bf16[120,512]{1,0:T(8,128)(2,1)S(1)} %collective-permute-done.4.refs_3_), channel_id=1, source_target_pairs={{0,4},{4,0},{8,12},{12,8},{1,5},{5,1},{9,13},{13,9},{2,6},{6,2},{1... | collective-permute-start | bytes 368648 | tf_op jit(solution)/shard_map/ppermute | solution.py:291
  25.5 5.7 %collective-permute-start.9 = (bf16[192,4096]{1,0:T(8,128)(2,1)S(1)}, bf16[192,4096]{1,0:T(8,128)(2,1)S(1)}, u32[]{:S(2)}, u32[]{:S(2)}) collective-permute-start(bf16[192,4096]{1,0:T(8,128)(2,1)S(1)} %lift.1.early_ref), channel_id=1, source_target_pairs={{0,1},{1,0},{2,3},{3,2},{4,5},{5,4},{6,7},{7,6},{8,9},{9,8},{10,11... | collective-permute-start | bytes 4718600 | tf_op jit(solution)/shard_map/ppermute | solution.py:304
  26.7 4.5 %collective-permute-start.10 = (bf16[120,512]{1,0:T(8,128)(2,1)S(1)}, bf16[120,512]{1,0:T(8,128)(2,1)S(1)}, u32[]{:S(2)}, u32[]{:S(2)}) collective-permute-start(bf16[120,512]{1,0:T(8,128)(2,1)S(1)} %collective-permute-done.7.y0_ref), channel_id=1, source_target_pairs={{0,1},{1,0},{2,3},{3,2},{4,5},{5,4},{6,7},{7,6},{8,9},{9,8},{10,11... | collective-permute-start | bytes 368648 | tf_op jit(solution)/shard_map/ppermute | solution.py:305
  28.6 2.6 %collective-permute-start.11 = (bf16[120,512]{1,0:T(8,128)(2,1)S(1)}, bf16[120,512]{1,0:T(8,128)(2,1)S(1)}, u32[]{:S(2)}, u32[]{:S(2)}) collective-permute-start(bf16[120,512]{1,0:T(8,128)(2,1)S(1)} %collective-permute-done.8.y1_ref), channel_id=1, source_target_pairs={{0,1},{1,0},{2,3},{3,2},{4,5},{5,4},{6,7},{7,6},{8,9},{9,8},{10,11... | collective-permute-start | bytes 368648 | tf_op jit(solution)/shard_map/ppermute | solution.py:305
  33.9 3.8 %collective-permute-start.13 = (f32[2,1024]{1,0:T(2,128)S(1)}, f32[2,1024]{1,0:T(2,128)S(1)}, u32[]{:S(2)}, u32[]{:S(2)}) collective-permute-start(f32[2,1024]{1,0:T(2,128)S(1)} %maximum_select_fusion), channel_id=1, source_target_pairs={{0,4},{4,0},{8,12},{12,8},{1,5},{5,1},{9,13},{13,9},{2,6},{6,2},{1... | collective-permute-start | bytes 24584 | tf_op jit(solution)/shard_map/ppermute | solution.py:354
  34.6 3.1 %collective-permute-start.14 = (f32[2,1024]{1,0:T(2,128)S(1)}, f32[2,1024]{1,0:T(2,128)S(1)}, u32[]{:S(2)}, u32[]{:S(2)}) collective-permute-start(f32[2,1024]{1,0:T(2,128)S(1)} %maximum_select_fusion), channel_id=1, source_target_pairs={{0,5},{1,4},{4,1},{5,0},{8,13},{9,12},{12,9},{13,8},{2,7},{3,6},{6... | collective-permute-start | bytes 24584 | tf_op jit(solution)/shard_map/ppermute | solution.py:355
  35.9 1.9 %collective-permute-start.12 = (f32[2,1024]{1,0:T(2,128)S(1)}, f32[2,1024]{1,0:T(2,128)S(1)}, u32[]{:S(2)}, u32[]{:S(2)}) collective-permute-start(f32[2,1024]{1,0:T(2,128)S(1)} %maximum_select_fusion), channel_id=1, source_target_pairs={{0,1},{1,0},{2,3},{3,2},{4,5},{5,4},{6,7},{7,6},{8,9},{9,8},{10,11... | collective-permute-start | bytes 24584 | tf_op jit(solution)/shard_map/ppermute | solution.py:356
  37.8 5.1 %collective-permute-start.15 = (f32[2,1024]{1,0:T(2,128)S(1)}, f32[2,1024]{1,0:T(2,128)S(1)}, u32[]{:S(2)}, u32[]{:S(2)}) collective-permute-start(f32[2,1024]{1,0:T(2,128)S(1)} %add_add_fusion), channel_id=1, source_target_pairs={{0,8},{4,12},{8,0},{12,4},{1,9},{5,13},{9,1},{13,5},{2,10},{6,14},... | collective-permute-start | bytes 24584 | tf_op jit(solution)/shard_map/ppermute | solution.py:360

commit v5 on v4

--- a/solution.py
+++ b/solution.py
@@ -160,19 +160,18 @@
 
 
 def coupling_kernel(
-    k, width, modes, count, early_ref, y0_ref, y1_ref, a_ref, l_ref, d_ref, w_ref, out_ref, mean_ref, late, zs
+    k, width, modes, count, early_ref, late_ref, l_ref, d_ref, w_ref, out_ref, mean_ref, zs
 ):
     q_rows = l_ref.shape[1] // width
     pitch = width + 8
     unroll = width if l_ref.shape[2] <= 512 else 4
-    lift(a_ref[k], (y0_ref, y1_ref), late, 0, width)
 
     def columns(i):
         start = i * unroll * 128
         if not isinstance(start, int):
             start = pl.multiple_of(start, unroll * 128)
         lanes = pl.ds(start, unroll * 128)
-        x = jnp.concatenate([early_ref[:, lanes], late[:, lanes]], 0)
+        x = jnp.concatenate([early_ref[:, lanes], late_ref[:, lanes]], 0)
         z = jnp.dot(l_ref[k], x, preferred_element_type=F32)
         for u in range(unroll):
             zs[pl.ds(unroll * i + u, q_rows * width, stride=pitch), :] = z[:, u * 128 : (u + 1) * 128]
@@ -274,7 +273,8 @@
             (e * n_ma + c, (e + s) % n_ea * n_ma + (c ^ 1)) for e in range(n_ea) for c in range(n_ma)
         ]
         mine.append(lax.ppermute(parts[s * k_rows], "ea", shift(n_ea, s)))
-        other.append(lax.ppermute(parts[s * k_rows + 1], ("ea", "ma"), cross))
+        late, _ = lax.optimization_barrier((parts[s * k_rows + 1], left))
+        other.append(lax.ppermute(late, ("ea", "ma"), cross))
 
     mine[0], left, kron = lax.optimization_barrier((mine[0], left, kron))
     by_k = [sum(y.astype(F32) for y in part).astype(BF16) for part in (mine, other)]
@@ -292,17 +292,20 @@
             blocks += came
         distance //= 2
     held = [y for pair in zip(*halves) for y in pair]
-    early = pl.pallas_call(
-        functools.partial(lift_kernel, width),
-        out_shape=jax.ShapeDtypeStruct(((n_pb - 1) * 2 * width, width * 128), BF16),
-        in_specs=[VMEM] * (2 * n_pb - 1),
-        out_specs=VMEM,
-        cost_estimate=cost(1),
-        compiler_params=pltpu.CompilerParams(vmem_limit_bytes=(4 + n_pb) * MIB),
-        name="lift",
-    )(kron, *held[:-2])
-    early = (early, lax.ppermute(early, "ma", swap))
-    last = (held[-2:], [lax.ppermute(y, "ma", swap) for y in held[-2:]])
+    lifted = []
+    for blocks in (held[:-2], held[-2:]):
+        lifted.append(
+            pl.pallas_call(
+                functools.partial(lift_kernel, width),
+                out_shape=jax.ShapeDtypeStruct((len(blocks) * width, width * 128), BF16),
+                in_specs=[VMEM] * (1 + len(blocks)),
+                out_specs=VMEM,
+                cost_estimate=cost(1),
+                compiler_params=pltpu.CompilerParams(vmem_limit_bytes=(4 + n_pb) * MIB),
+                name="lift",
+            )(kron, *blocks)
+        )
+    lifted = (lifted, [lax.ppermute(x, "ma", swap) for x in lifted])
     results = []
     for k in range(k_rows):
         results.append(
@@ -314,16 +317,15 @@
                     jax.ShapeDtypeStruct((q_rows, modes, pairs), BF16),
                     jax.ShapeDtypeStruct((1, pairs), F32),
                 ],
-                in_specs=[VMEM] * 7,
+                in_specs=[VMEM] * 5,
                 out_specs=[VMEM, VMEM],
                 scratch_shapes=[
-                    pltpu.VMEM((2 * width, width * 128), BF16),
                     pltpu.VMEM((q_rows * width * (width + 8), 128), F32),
                 ],
                 cost_estimate=cost(40),
                 compiler_params=pltpu.CompilerParams(vmem_limit_bytes=(14 + n_pb) * MIB),
                 name="coupling",
-            )(early[k], *last[k], kron, left, mix, weights)
+            )(*lifted[k], left, mix, weights)
         )
     (first, mean), (second, rest) = results
     core = lax.axis_index("ma")

time: 43.6 us -> 43.4 us (level)
  waiting for transfers between devices: 13.4 us -> 12.5 us
  starting transfers between devices: 15.4 us -> 16.2 us
    ppermute x4, starting transfers between devices: 6.13 us -> 7.33 us  [body(): came = [lax.ppermute(blocks[0], 'pb', flip(n_pb, distance))]]
    ppermute x4, waiting for transfers between devices: 7.92 us -> 7.1 us  [body(): came = [lax.ppermute(blocks[0], 'pb', flip(n_pb, distance))]]
    pallas_call x2, Pallas kernels: 5.28 us -> 4.52 us  [body(): pl.pallas_call(functools.partial(coupling_kernel, k, width, modes, q_rows...]
    ppermute x2, waiting for transfers between devices: 2.97 us -> 3.5 us  [body(): came.append(lax.ppermute(y, 'pb', flip(n_pb, distance)))]
    pallas_call x1 -> x2, Pallas kernels: 1.02 us -> 1.5 us  [body(): pl.pallas_call(functools.partial(lift_kernel, width), out_shape=jax.Shape...]
    ppermute x1, waiting for transfers between devices: 2.22 us -> 1.74 us  [body(): mine.append(lax.ppermute(parts[s * k_rows], 'ea', shift(n_ea, s)))]
  transfers between devices with their start and end apart: 16 -> 15, of which waited for: 7 -> 6; matrix products, arithmetic and copies ran while one was open for 0% -> 0% of each run, Pallas kernels for 20% -> 20%
where the time goes in v5:
time: 43.4 us; the launch traced here: 43.2 us
  starting transfers between devices  16.2 us (37%)
  waiting for transfers between devices  12.5 us (29%)
  Pallas kernels  12 us (28%)
  other arithmetic  1.4 us (3%)
  between operations  0.82 us (2%)
    ppermute x4, starting transfers between devices, body(): came = [lax.ppermute(blocks[0], 'pb', flip(n_pb, distance))]  7.33 us
    ppermute x4, waiting for transfers between devices, body(): came = [lax.ppermute(blocks[0], 'pb', flip(n_pb, distance))]  7.1 us
    pallas_call x2, Pallas kernels, body(): pl.pallas_call(functools.partial(coupling_kernel, k, width, modes, q_rows...  4.52 us
    ppermute x2, waiting for transfers between devices, body(): came.append(lax.ppermute(y, 'pb', flip(n_pb, distance)))  3.5 us
    ppermute x1, starting transfers between devices, body(): mean = mean + lax.ppermute(mean, 'pb', flip(n_pb, distance))  3.07 us
    ppermute x1, starting transfers between devices, body(): mine.append(lax.ppermute(parts[s * k_rows], 'ea', shift(n_ea, s)))  3 us
    pallas_call x2, Pallas kernels, body(): pl.pallas_call(order_kernel, grid=(1,), out_shape=jax.ShapeDtypeStruct((q...  2.97 us
    ppermute x1, waiting for transfers between devices, body(): mine.append(lax.ppermute(parts[s * k_rows], 'ea', shift(n_ea, s)))  1.74 us
  transfers between devices with their start and end apart: 15, of which 6 were waited for; matrix products, arithmetic and copies ran while one was open for 0% of the time, Pallas kernels for 20%

profile of v5, /device:TPU:0, one launch (start us, length us, event | category | flops | bytes accessed | tf_op | source)
XLA Modules:
  0.0 43.2 jit_solution(16313903627492000189)
XLA Ops:
  0.6 0.7 %pad_add_fusion.coords_ref = s32[6,3]{1,0:T(8,128)S(1)} fusion(s32[2,3]{1,0:T(2,128)} %param.10, s32[4,3]{1,0:T(4,128)} %param.12), kind=kLoop, calls=%fused_computation.4 | loop fusion | flops 18 | bytes 144 | tf_op jit(solution)/shard_map/concatenate | solution.py:225
  1.3 0.0 copy-start.1
  1.3 0.7 %electron_phases.1.factor_ref = bf16[256,120]{1,0:T(8,128)(2,1)S(1)} custom-call(s32[6,3]{1,0:T(8,128)S(1)} %pad_add_fusion.coords_ref), custom_call_target="tpu_custom_call" | custom-call | flops 2000000000 | bytes 6000000 | tf_op jit(solution)/shard_map/electron_phases/pallas_call | solution.py:217
  2.1 0.2 copy-done.1
  2.3 0.0 copy-start
  2.3 0.0 copy-start.2
  2.3 0.0 copy-start.4
  2.3 0.0 copy-start.5
  2.3 0.3 electron_sum.1
  2.6 3.0 %collective-permute-start = (bf16[120,512]{1,0:T(8,128)(2,1)S(1)}, bf16[120,512]{1,0:T(8,128)(2,1)S(1)}, u32[]{:S(2)}, u32[]{:S(2)}) collective-permute-start(bf16[120,512]{1,0:T(8,128)(2,1)S(1)} %get-tuple-element.24), channel_id=1, source_target_pairs={{0,2},{2,0},{1,3},{3,1},{4,6},{6,4},{5,7},{7,5},{8,10},{10,8},{9,1... | collective-permute-start | bytes 368648 | tf_op jit(solution)/shard_map/ppermute | solution.py:275
  5.6 0.0 collective-permute-start.1
  5.6 0.0 copy-done
  5.6 0.0 copy-done.2
  5.6 0.0 copy-done.4
  5.6 0.0 copy-done.5
  5.6 0.0 copy-start.6
  5.6 1.3 %rotations.1 = (bf16[2,384,256]{2,1,0:T(8,128)(2,1)S(1)}, bf16[2,256,512]{2,1,0:T(8,128)(2,1)S(1)}) custom-call(s32[4,3]{1,0:T(4,128)S(1)} %copy-done.4, s32[3,24]{1,0:T(4,128)S(1)} %bitcast.4, bf16[2,2,32,32]{3,2,1,0:T(8,128)(2,1)S(1)} %copy-done.2, bf16[2,12,2,32,32]{4,3,2,1,0:T(8,128)(2,1)S(1)} %copy-done), custom_call_target="tpu_custom_call" | custom-call | flops 2000000000 | bytes 6000000 | tf_op jit(solution)/shard_map/rotations/pallas_call | solution.py:244
  6.9 0.0 copy-start.3
  6.9 0.2 collective-permute-start.2
  7.2 1.7 %collective-permute-done = bf16[120,512]{1,0:T(8,128)(2,1)S(1)} collective-permute-done((bf16[120,512]{1,0:T(8,128)(2,1)S(1)}, bf16[120,512]{1,0:T(8,128)(2,1)S(1)}, u32[]{:S(2)}, u32[]{:S(2)}) %collective-permute-start) | collective-permute-done | bytes 122912 | tf_op jit(solution)/shard_map/ppermute | solution.py:275
  8.9 1.9 %collective-permute-start.5 = (bf16[120,512]{1,0:T(8,128)(2,1)S(1)}, bf16[120,512]{1,0:T(8,128)(2,1)S(1)}, u32[]{:S(2)}, u32[]{:S(2)}) collective-permute-start(bf16[120,512]{1,0:T(8,128)(2,1)S(1)} %add_convert_fusion.1.refs_0_), channel_id=1, source_target_pairs={{0,4},{4,0},{8,12},{12,8},{1,5},{5,1},{9,13},{13,9},{2,6},{6,2},{1... | collective-permute-start | bytes 368648 | tf_op jit(solution)/shard_map/ppermute | solution.py:287
  10.8 2.6 %collective-permute-start.3 = (bf16[120,512]{1,0:T(8,128)(2,1)S(1)}, bf16[120,512]{1,0:T(8,128)(2,1)S(1)}, u32[]{:S(2)}, u32[]{:S(2)}) collective-permute-start(bf16[120,512]{1,0:T(8,128)(2,1)S(1)} %add_convert_fusion.1.refs_0_), channel_id=1, source_target_pairs={{0,8},{4,12},{8,0},{12,4},{1,9},{5,13},{9,1},{13,5},{2,10},{6,14},... | collective-permute-start | bytes 368648 | tf_op jit(solution)/shard_map/ppermute | solution.py:287
  13.4 0.0 collective-permute-done.2
  13.4 0.0 collective-permute-done.1
  13.5 1.2 %collective-permute-start.4 = (bf16[120,512]{1,0:T(8,128)(2,1)S(1)}, bf16[120,512]{1,0:T(8,128)(2,1)S(1)}, u32[]{:S(2)}, u32[]{:S(2)}) collective-permute-start(bf16[120,512]{1,0:T(8,128)(2,1)S(1)} %add_convert_fusion.refs_1_), channel_id=1, source_target_pairs={{0,8},{4,12},{8,0},{12,4},{1,9},{5,13},{9,1},{13,5},{2,10},{6,14},... | collective-permute-start | bytes 368648 | tf_op jit(solution)/shard_map/ppermute | solution.py:287
  14.7 0.0 copy-done.6
  14.7 0.1 copy.12.modes_ref
  14.8 1.6 %collective-permute-start.6 = (bf16[120,512]{1,0:T(8,128)(2,1)S(1)}, bf16[120,512]{1,0:T(8,128)(2,1)S(1)}, u32[]{:S(2)}, u32[]{:S(2)}) collective-permute-start(bf16[120,512]{1,0:T(8,128)(2,1)S(1)} %add_convert_fusion.refs_1_), channel_id=1, source_target_pairs={{0,4},{4,0},{8,12},{12,8},{1,5},{5,1},{9,13},{13,9},{2,6},{6,2},{1... | collective-permute-start | bytes 368648 | tf_op jit(solution)/shard_map/ppermute | solution.py:287
  16.4 0.0 collective-permute-done.5.refs_4_
  16.4 5.1 %collective-permute-done.3.refs_2_ = bf16[120,512]{1,0:T(8,128)(2,1)S(1)} collective-permute-done((bf16[120,512]{1,0:T(8,128)(2,1)S(1)}, bf16[120,512]{1,0:T(8,128)(2,1)S(1)}, u32[]{:S(2)}, u32[]{:S(2)}) %collective-permute-start.3) | collective-permute-done | bytes 122912 | tf_op jit(solution)/shard_map/ppermute | solution.py:287
  21.5 0.2 collective-permute-start.7
  21.7 2.0 %collective-permute-done.4.refs_3_ = bf16[120,512]{1,0:T(8,128)(2,1)S(1)} collective-permute-done((bf16[120,512]{1,0:T(8,128)(2,1)S(1)}, bf16[120,512]{1,0:T(8,128)(2,1)S(1)}, u32[]{:S(2)}, u32[]{:S(2)}) %collective-permute-start.4) | collective-permute-done | bytes 122912 | tf_op jit(solution)/shard_map/ppermute | solution.py:287
  23.7 0.0 collective-permute-start.8
  23.7 0.0 copy-done.3
  23.7 0.7 %mode_rotation.1 = (bf16[2,12,128,128]{3,2,1,0:T(8,128)(2,1)S(1)}, f32[12,64,1]{2,1,0:T(8,128)S(1)}) custom-call(bf16[2,12,60,60]{3,2,1,0:T(8,128)(2,1)S(1)} %copy.12.modes_ref, f32[12,60]{1,0:T(8,128)S(1)} %copy-done.3), custom_call_target="tpu_custom_call" | custom-call | flops 2000000000 | bytes 6000000 | tf_op jit(solution)/shard_map/mode_rotation/pallas_call | solution.py:257
  24.4 0.0 collective-permute-done.6.refs_5_
  24.4 1.0 %lift.2.early_ref = bf16[192,4096]{1,0:T(8,128)(2,1)S(1)} custom-call(bf16[2,256,512]{2,1,0:T(8,128)(2,1)S(1)} %get-tuple-element.22.a_ref, bf16[120,512]{1,0:T(8,128)(2,1)S(1)} %add_convert_fusion.1.refs_0_, bf16[120,512]{1,0:T(8,128)(2,1)S(1)} %add_convert_fusion.refs_1_, bf16[120,512]{1,0:T(8,128)(2,1)S(1)} %collective-permute-done.3.refs_2_, ...), custom_call_target="tpu_custom_call" | custom-call | flops 1000000000 | bytes 3000000 | tf_op jit(solution)/shard_map/lift/pallas_call | solution.py:298
  25.4 0.1 collective-permute-start.9
  25.5 1.6 %collective-permute-done.7.refs_0_ = bf16[120,512]{1,0:T(8,128)(2,1)S(1)} collective-permute-done((bf16[120,512]{1,0:T(8,128)(2,1)S(1)}, bf16[120,512]{1,0:T(8,128)(2,1)S(1)}, u32[]{:S(2)}, u32[]{:S(2)}) %collective-permute-start.7) | collective-permute-done | bytes 122912 | tf_op jit(solution)/shard_map/ppermute | solution.py:291
  27.1 1.9 %collective-permute-done.8.refs_1_ = bf16[120,512]{1,0:T(8,128)(2,1)S(1)} collective-permute-done((bf16[120,512]{1,0:T(8,128)(2,1)S(1)}, bf16[120,512]{1,0:T(8,128)(2,1)S(1)}, u32[]{:S(2)}, u32[]{:S(2)}) %collective-permute-start.8) | collective-permute-done | bytes 122912 | tf_op jit(solution)/shard_map/ppermute | solution.py:291
  29.0 0.5 %lift.3.late_ref = bf16[64,4096]{1,0:T(8,128)(2,1)S(1)} custom-call(bf16[2,256,512]{2,1,0:T(8,128)(2,1)S(1)} %get-tuple-element.22.a_ref, bf16[120,512]{1,0:T(8,128)(2,1)S(1)} %collective-permute-done.7.refs_0_, bf16[120,512]{1,0:T(8,128)(2,1)S(1)} %collective-permute-done.8.refs_1_), custom_call_target="tpu_custom_call" | custom-call | flops 1000000000 | bytes 3000000 | tf_op jit(solution)/shard_map/lift/pallas_call | solution.py:298
  29.5 0.1 collective-permute-start.10
  29.6 2.3 %coupling.2 = (bf16[12,60,1024]{2,1,0:T(8,128)(2,1)S(1)}, f32[1,1024]{1,0:T(1,128)S(1)}) custom-call(bf16[192,4096]{1,0:T(8,128)(2,1)S(1)} %lift.2.early_ref, bf16[64,4096]{1,0:T(8,128)(2,1)S(1)} %lift.3.late_ref, bf16[2,384,256]{2,1,0:T(8,128)(2,1)S(1)} %get-tuple-element.29.l_ref, bf16[2,12,128,128]{3,2,1,0:T(8,128)(2,1)S(1)} %get-tuple-element.30.d_ref, ...), custom_call_target="tpu_custom_call" | custom-call | flops 40000000000 | bytes 120000000 | tf_op jit(solution)/shard_map/coupling/pallas_call | solution.py:312
  31.8 0.0 collective-permute-done.10.late_ref
  31.8 0.0 collective-permute-done.9.early_ref
  31.9 2.3 %coupling.3 = (bf16[12,60,1024]{2,1,0:T(8,128)(2,1)S(1)}, f32[1,1024]{1,0:T(1,128)S(1)}) custom-call(bf16[192,4096]{1,0:T(8,128)(2,1)S(1)} %collective-permute-done.9.early_ref, bf16[64,4096]{1,0:T(8,128)(2,1)S(1)} %collective-permute-done.10.late_ref, bf16[2,384,256]{2,1,0:T(8,128)(2,1)S(1)} %get-tuple-element.29.l_ref, ...), custom_call_target="tpu_custom_call" | custom-call | flops 40000000000 | bytes 120000000 | tf_op jit(solution)/shard_map/coupling/pallas_call | solution.py:312
  34.1 0.3 collective-permute-start.12
  34.4 1.6 %collective-permute-start.13 = (f32[2,1024]{1,0:T(2,128)S(1)}, f32[2,1024]{1,0:T(2,128)S(1)}, u32[]{:S(2)}, u32[]{:S(2)}) collective-permute-start(f32[2,1024]{1,0:T(2,128)S(1)} %maximum_select_fusion), channel_id=1, source_target_pairs={{0,5},{1,4},{4,1},{5,0},{8,13},{9,12},{12,9},{13,8},{2,7},{3,6},{6... | collective-permute-start | bytes 24584 | tf_op jit(solution)/shard_map/ppermute | solution.py:357
  36.1 0.3 collective-permute-start.11
  36.4 1.5 %order.2.refs_0_ = bf16[12,60,2,1024]{3,2,1,0:T(2,128)(2,1)} custom-call(bf16[12,60,1024]{2,1,0:T(8,128)(2,1)S(1)} %get-tuple-element.32.first_ref, bf16[12,60,1024]{2,1,0:T(8,128)(2,1)S(1)} %get-tuple-element.33.second_ref), custom_call_target="tpu_custom_call" | custom-call | flops 2000000000 | bytes 6000000 | tf_op jit(solution)/shard_map/order/pallas_call | solution.py:340
  37.8 0.0 collective-permute-done.12
  37.9 0.0 collective-permute-done.13
  37.9 0.0 collective-permute-done.11
  37.9 3.1 %collective-permute-start.14 = (f32[2,1024]{1,0:T(2,128)S(1)}, f32[2,1024]{1,0:T(2,128)S(1)}, u32[]{:S(2)}, u32[]{:S(2)}) collective-permute-start(f32[2,1024]{1,0:T(2,128)S(1)} %add_add_fusion), channel_id=1, source_target_pairs={{0,8},{4,12},{8,0},{12,4},{1,9},{5,13},{9,1},{13,5},{2,10},{6,14},... | collective-permute-start | bytes 24584 | tf_op jit(solution)/shard_map/ppermute | solution.py:362
  41.0 1.5 %order.3 = bf16[12,60,2,1024]{3,2,1,0:T(2,128)(2,1)} custom-call(bf16[12,60,1024]{2,1,0:T(8,128)(2,1)S(1)} %get-tuple-element.32.first_ref, bf16[12,60,1024]{2,1,0:T(8,128)(2,1)S(1)} %get-tuple-element.33.second_ref, bf16[12,60,2,1024]{3,2,1,0:T(2,128)(2,1)} %order.2.refs_0_), custom_call_target="tpu_custom_call", output_to_operand_aliasing={{}: (2, {})} | custom-call | flops 2000000000 | bytes 6000000 | tf_op jit(solution)/shard_map/order/pallas_call | solution.py:340
  42.5 0.2 collective-permute-done.14
  42.6 0.6 %add.23 = f32[2,1024]{1,0:T(2,128)} add(f32[2,1024]{1,0:T(2,128)S(1)} %add_add_fusion, f32[2,1024]{1,0:T(2,128)S(1)} %collective-permute-done.14) | non-fusion elementwise | flops 2048 | bytes 24576 | tf_op jit(solution)/shard_map/add | solution.py:362
  (4 shorter events, 0.1 us)
Async XLA Ops:
  1.3 0.9 %copy-start.1 = (bf16[2,1,2,30,1024]{4,2,3,1,0:T(2,128)(2,1)S(1)}, bf16[2,1,2,30,1024]{4,2,3,1,0:T(2,128)(2,1)}, u32[]{:S(2)}) copy-start(bf16[2,1,2,30,1024]{4,2,3,1,0:T(2,128)(2,1)} %param.9) | copy-start | bytes 737284
  2.3 3.3 %copy-start = (bf16[2,12,2,32,32]{4,3,2,1,0:T(8,128)(2,1)S(1)}, bf16[2,12,2,32,32]{4,3,2,1,0:T(8,128)(2,1)}, u32[]{:S(2)}) copy-start(bf16[2,12,2,32,32]{4,3,2,1,0:T(8,128)(2,1)} %u_kq_ref.1) | copy-start | bytes 294916
  2.3 3.3 %copy-start.2 = (bf16[2,2,32,32]{3,2,1,0:T(8,128)(2,1)S(1)}, bf16[2,2,32,32]{3,2,1,0:T(8,128)(2,1)}, u32[]{:S(2)}) copy-start(bf16[2,2,32,32]{3,2,1,0:T(8,128)(2,1)} %u_k_ref.1) | copy-start | bytes 24580
  2.3 3.3 %copy-start.4 = (s32[4,3]{1,0:T(4,128)S(1)}, s32[4,3]{1,0:T(4,128)}, u32[]{:S(2)}) copy-start(s32[4,3]{1,0:T(4,128)} %r_ref.1) | copy-start | bytes 148
  2.3 3.3 %copy-start.5 = (s32[24,3]{0,1:T(4,128)S(1)}, s32[24,3]{0,1:T(4,128)}, u32[]{:S(2)}) copy-start(s32[24,3]{0,1:T(4,128)} %param.13) | copy-start | bytes 868
  2.6 6.3 %collective-permute-start = (bf16[120,512]{1,0:T(8,128)(2,1)S(1)}, bf16[120,512]{1,0:T(8,128)(2,1)S(1)}, u32[]{:S(2)}, u32[]{:S(2)}) collective-permute-start(bf16[120,512]{1,0:T(8,128)(2,1)S(1)} %get-tuple-element.24), channel_id=1, source_target_pairs={{0,2},{2,0},{1,3},{3,1},{4,6},{6,4},{5,7},{7,5},{8,10},{10,8},{9,1... | collective-permute-start | bytes 368648 | tf_op jit(solution)/shard_map/ppermute | solution.py:275
  5.6 7.8 %collective-permute-start.1 = (f32[120,512]{1,0:T(8,128)S(1)}, f32[120,512]{1,0:T(8,128)S(1)}, u32[]{:S(2)}, u32[]{:S(2)}) collective-permute-start(f32[120,512]{1,0:T(8,128)S(1)} %get-tuple-element.25), channel_id=1, source_target_pairs={{0,1},{1,0},{2,3},{3,2},{4,5},{5,4},{6,7},{7,6},{8,9},{9,8},{10,11... | collective-permute-start | bytes 737288 | tf_op jit(solution)/shard_map/ppermute | solution.py:270
  5.6 9.0 %copy-start.6 = (bf16[2,12,60,60]{3,0,2,1:T(2,128)(2,1)S(1)}, bf16[2,12,60,60]{3,0,2,1:T(2,128)(2,1)}, u32[]{:S(2)}) copy-start(bf16[2,12,60,60]{3,0,2,1:T(2,128)(2,1)} %param.16) | copy-start | bytes 518404
  6.9 16.8 %copy-start.3 = (f32[12,60]{1,0:T(8,128)S(1)}, f32[12,60]{1,0:T(8,128)}, u32[]{:S(2)}) copy-start(f32[12,60]{1,0:T(8,128)} %weights_ref.1) | copy-start | bytes 8644
  6.9 6.5 %collective-permute-start.2 = (bf16[120,512]{1,0:T(8,128)(2,1)S(1)}, bf16[120,512]{1,0:T(8,128)(2,1)S(1)}, u32[]{:S(2)}, u32[]{:S(2)}) collective-permute-start(bf16[120,512]{1,0:T(8,128)(2,1)S(1)} %get-tuple-element.27), channel_id=1, source_target_pairs={{0,3},{1,2},{2,1},{3,0},{4,7},{5,6},{6,5},{7,4},{8,11},{9,10},{10,... | collective-permute-start | bytes 368648 | tf_op jit(solution)/shard_map/ppermute | solution.py:277
  8.9 7.5 %collective-permute-start.5 = (bf16[120,512]{1,0:T(8,128)(2,1)S(1)}, bf16[120,512]{1,0:T(8,128)(2,1)S(1)}, u32[]{:S(2)}, u32[]{:S(2)}) collective-permute-start(bf16[120,512]{1,0:T(8,128)(2,1)S(1)} %add_convert_fusion.1.refs_0_), channel_id=1, source_target_pairs={{0,4},{4,0},{8,12},{12,8},{1,5},{5,1},{9,13},{13,9},{2,6},{6,2},{1... | collective-permute-start | bytes 368648 | tf_op jit(solution)/shard_map/ppermute | solution.py:287
  10.8 10.7 %collective-permute-start.3 = (bf16[120,512]{1,0:T(8,128)(2,1)S(1)}, bf16[120,512]{1,0:T(8,128)(2,1)S(1)}, u32[]{:S(2)}, u32[]{:S(2)}) collective-permute-start(bf16[120,512]{1,0:T(8,128)(2,1)S(1)} %add_convert_fusion.1.refs_0_), channel_id=1, source_target_pairs={{0,8},{4,12},{8,0},{12,4},{1,9},{5,13},{9,1},{13,5},{2,10},{6,14},... | collective-permute-start | bytes 368648 | tf_op jit(solution)/shard_map/ppermute | solution.py:287
  13.5 10.2 %collective-permute-start.4 = (bf16[120,512]{1,0:T(8,128)(2,1)S(1)}, bf16[120,512]{1,0:T(8,128)(2,1)S(1)}, u32[]{:S(2)}, u32[]{:S(2)}) collective-permute-start(bf16[120,512]{1,0:T(8,128)(2,1)S(1)} %add_convert_fusion.refs_1_), channel_id=1, source_target_pairs={{0,8},{4,12},{8,0},{12,4},{1,9},{5,13},{9,1},{13,5},{2,10},{6,14},... | collective-permute-start | bytes 368648 | tf_op jit(solution)/shard_map/ppermute | solution.py:287
  14.8 9.6 %collective-permute-start.6 = (bf16[120,512]{1,0:T(8,128)(2,1)S(1)}, bf16[120,512]{1,0:T(8,128)(2,1)S(1)}, u32[]{:S(2)}, u32[]{:S(2)}) collective-permute-start(bf16[120,512]{1,0:T(8,128)(2,1)S(1)} %add_convert_fusion.refs_1_), channel_id=1, source_target_pairs={{0,4},{4,0},{8,12},{12,8},{1,5},{5,1},{9,13},{13,9},{2,6},{6,2},{1... | collective-permute-start | bytes 368648 | tf_op jit(solution)/shard_map/ppermute | solution.py:287
  21.5 5.6 %collective-permute-start.7 = (bf16[120,512]{1,0:T(8,128)(2,1)S(1)}, bf16[120,512]{1,0:T(8,128)(2,1)S(1)}, u32[]{:S(2)}, u32[]{:S(2)}) collective-permute-start(bf16[120,512]{1,0:T(8,128)(2,1)S(1)} %collective-permute-done.3.refs_2_), channel_id=1, source_target_pairs={{0,4},{4,0},{8,12},{12,8},{1,5},{5,1},{9,13},{13,9},{2,6},{6,2},{1... | collective-permute-start | bytes 368648 | tf_op jit(solution)/shard_map/ppermute | solution.py:291
  23.7 5.3 %collective-permute-start.8 = (bf16[120,512]{1,0:T(8,128)(2,1)S(1)}, bf16[120,512]{1,0:T(8,128)(2,1)S(1)}, u32[]{:S(2)}, u32[]{:S(2)}) collective-permute-start(bf16[120,512]{1,0:T(8,128)(2,1)S(1)} %collective-permute-done.4.refs_3_), channel_id=1, source_target_pairs={{0,4},{4,0},{8,12},{12,8},{1,5},{5,1},{9,13},{13,9},{2,6},{6,2},{1... | collective-permute-start | bytes 368648 | tf_op jit(solution)/shard_map/ppermute | solution.py:291
  25.4 6.4 %collective-permute-start.9 = (bf16[192,4096]{1,0:T(8,128)(2,1)S(1)}, bf16[192,4096]{1,0:T(8,128)(2,1)S(1)}, u32[]{:S(2)}, u32[]{:S(2)}) collective-permute-start(bf16[192,4096]{1,0:T(8,128)(2,1)S(1)} %lift.2.early_ref), channel_id=1, source_target_pairs={{0,1},{1,0},{2,3},{3,2},{4,5},{5,4},{6,7},{7,6},{8,9},{9,8},{10,11... | collective-permute-start | bytes 4718600 | tf_op jit(solution)/shard_map/ppermute | solution.py:308
  29.5 2.3 %collective-permute-start.10 = (bf16[64,4096]{1,0:T(8,128)(2,1)S(1)}, bf16[64,4096]{1,0:T(8,128)(2,1)S(1)}, u32[]{:S(2)}, u32[]{:S(2)}) collective-permute-start(bf16[64,4096]{1,0:T(8,128)(2,1)S(1)} %lift.3.late_ref), channel_id=1, source_target_pairs={{0,1},{1,0},{2,3},{3,2},{4,5},{5,4},{6,7},{7,6},{8,9},{9,8},{10,11... | collective-permute-start | bytes 1572872 | tf_op jit(solution)/shard_map/ppermute | solution.py:308
  34.1 3.7 %collective-permute-start.12 = (f32[2,1024]{1,0:T(2,128)S(1)}, f32[2,1024]{1,0:T(2,128)S(1)}, u32[]{:S(2)}, u32[]{:S(2)}) collective-permute-start(f32[2,1024]{1,0:T(2,128)S(1)} %maximum_select_fusion), channel_id=1, source_target_pairs={{0,4},{4,0},{8,12},{12,8},{1,5},{5,1},{9,13},{13,9},{2,6},{6,2},{1... | collective-permute-start | bytes 24584 | tf_op jit(solution)/shard_map/ppermute | solution.py:356
  34.4 3.5 %collective-permute-start.13 = (f32[2,1024]{1,0:T(2,128)S(1)}, f32[2,1024]{1,0:T(2,128)S(1)}, u32[]{:S(2)}, u32[]{:S(2)}) collective-permute-start(f32[2,1024]{1,0:T(2,128)S(1)} %maximum_select_fusion), channel_id=1, source_target_pairs={{0,5},{1,4},{4,1},{5,0},{8,13},{9,12},{12,9},{13,8},{2,7},{3,6},{6... | collective-permute-start | bytes 24584 | tf_op jit(solution)/shard_map/ppermute | solution.py:357
  36.1 1.8 %collective-permute-start.11 = (f32[2,1024]{1,0:T(2,128)S(1)}, f32[2,1024]{1,0:T(2,128)S(1)}, u32[]{:S(2)}, u32[]{:S(2)}) collective-permute-start(f32[2,1024]{1,0:T(2,128)S(1)} %maximum_select_fusion), channel_id=1, source_target_pairs={{0,1},{1,0},{2,3},{3,2},{4,5},{5,4},{6,7},{7,6},{8,9},{9,8},{10,11... | collective-permute-start | bytes 24584 | tf_op jit(solution)/shard_map/ppermute | solution.py:358
  37.9 4.7 %collective-permute-start.14 = (f32[2,1024]{1,0:T(2,128)S(1)}, f32[2,1024]{1,0:T(2,128)S(1)}, u32[]{:S(2)}, u32[]{:S(2)}) collective-permute-start(f32[2,1024]{1,0:T(2,128)S(1)} %add_add_fusion), channel_id=1, source_target_pairs={{0,8},{4,12},{8,0},{12,4},{1,9},{5,13},{9,1},{13,5},{2,10},{6,14},... | collective-permute-start | bytes 24584 | tf_op jit(solution)/shard_map/ppermute | solution.py:362

commit v6 on v5

--- a/solution.py
+++ b/solution.py
@@ -331,20 +331,23 @@
     core = lax.axis_index("ma")
     mean = jnp.where(core == 0, jnp.concatenate([mean, rest]), jnp.concatenate([rest, mean]))
 
-    pieces = 2 if q_rows % 2 == 0 else 1
+    pieces = 3 if q_rows % 3 == 0 else 1
+    ahead = max(pieces - 1, 1)
+    block = (q_rows // pieces, modes, pairs)
     out = None
-    for i in range(pieces):
-        block = (q_rows // pieces, modes, pairs)
-        at = functools.partial(lambda i, j: (i, 0, 0), i)
+    for i, steps in ((0, ahead), (ahead, pieces - ahead)):
+        if not steps:
+            continue
         operands = [first, second] + ([] if out is None else [out])
         out = pl.pallas_call(
             order_kernel,
-            grid=(1,),
+            grid=(steps,),
             out_shape=jax.ShapeDtypeStruct((q_rows, modes, k_rows, pairs), BF16),
-            in_specs=[pl.BlockSpec(block, at)] * 2 + [pl.BlockSpec(memory_space=pl.ANY)] * (i > 0),
+            in_specs=[pl.BlockSpec(block, functools.partial(lambda i, j: (i + j, 0, 0), i))] * 2
+            + [pl.BlockSpec(memory_space=pl.ANY)] * (i > 0),
             out_specs=pl.BlockSpec(
                 (q_rows // pieces, modes, k_rows, pairs),
-                functools.partial(lambda i, j: (i, 0, 0, 0), i),
+                functools.partial(lambda i, j: (i + j, 0, 0, 0), i),
             ),
             input_output_aliases={2: 0} if i else {},
             cost_estimate=cost(2),

time: 43.4 us -> 43.4 us (level)
  transfers between devices with their start and end apart: 15 -> 15, of which waited for: 6 -> 6; matrix products, arithmetic and copies ran while one was open for 0% -> 0% of each run, Pallas kernels for 20% -> 19%
where the time goes in v6:
time: 43.4 us; the launch traced here: 43.2 us
  starting transfers between devices  16.2 us (37%)
  waiting for transfers between devices  12.8 us (29%)
  Pallas kernels  11.7 us (27%)
  other arithmetic  1.41 us (3%)
  between operations  0.82 us (2%)
    ppermute x4, starting transfers between devices, body(): came = [lax.ppermute(blocks[0], 'pb', flip(n_pb, distance))]  7.33 us
    ppermute x4, waiting for transfers between devices, body(): came = [lax.ppermute(blocks[0], 'pb', flip(n_pb, distance))]  7.1 us
    pallas_call x2, Pallas kernels, body(): pl.pallas_call(functools.partial(coupling_kernel, k, width, modes, q_rows...  4.52 us
    ppermute x2, waiting for transfers between devices, body(): came.append(lax.ppermute(y, 'pb', flip(n_pb, distance)))  3.5 us
    ppermute x1, starting transfers between devices, body(): mean = mean + lax.ppermute(mean, 'pb', flip(n_pb, distance))  3.04 us
    ppermute x1, starting transfers between devices, body(): mine.append(lax.ppermute(parts[s * k_rows], 'ea', shift(n_ea, s)))  3 us
    pallas_call x2, Pallas kernels, body(): pl.pallas_call(order_kernel, grid=(steps,), out_shape=jax.ShapeDtypeStruc...  2.72 us
    ppermute x1, waiting for transfers between devices, body(): mine.append(lax.ppermute(parts[s * k_rows], 'ea', shift(n_ea, s)))  1.74 us
  transfers between devices with their start and end apart: 15, of which 6 were waited for; matrix products, arithmetic and copies ran while one was open for 0% of the time, Pallas kernels for 19%

profile of v6, /device:TPU:0, one launch (start us, length us, event | category | flops | bytes accessed | tf_op | source)
XLA Modules:
  0.0 43.2 jit_solution(7318684298473107214)
XLA Ops:
  0.6 0.7 %pad_add_fusion.coords_ref = s32[6,3]{1,0:T(8,128)S(1)} fusion(s32[2,3]{1,0:T(2,128)} %param.10, s32[4,3]{1,0:T(4,128)} %param.12), kind=kLoop, calls=%fused_computation.4 | loop fusion | flops 18 | bytes 144 | tf_op jit(solution)/shard_map/concatenate | solution.py:225
  1.3 0.0 copy-start.1
  1.3 0.7 %electron_phases.1.factor_ref = bf16[256,120]{1,0:T(8,128)(2,1)S(1)} custom-call(s32[6,3]{1,0:T(8,128)S(1)} %pad_add_fusion.coords_ref), custom_call_target="tpu_custom_call" | custom-call | flops 2000000000 | bytes 6000000 | tf_op jit(solution)/shard_map/electron_phases/pallas_call | solution.py:217
  2.1 0.2 copy-done.1
  2.3 0.0 copy-start
  2.3 0.0 copy-start.2
  2.3 0.0 copy-start.4
  2.3 0.0 copy-start.5
  2.3 0.3 electron_sum.1
  2.6 3.0 %collective-permute-start = (bf16[120,512]{1,0:T(8,128)(2,1)S(1)}, bf16[120,512]{1,0:T(8,128)(2,1)S(1)}, u32[]{:S(2)}, u32[]{:S(2)}) collective-permute-start(bf16[120,512]{1,0:T(8,128)(2,1)S(1)} %get-tuple-element.24), channel_id=1, source_target_pairs={{0,2},{2,0},{1,3},{3,1},{4,6},{6,4},{5,7},{7,5},{8,10},{10,8},{9,1... | collective-permute-start | bytes 368648 | tf_op jit(solution)/shard_map/ppermute | solution.py:275
  5.6 0.0 collective-permute-start.1
  5.6 0.0 copy-done
  5.6 0.0 copy-done.2
  5.6 0.0 copy-done.4
  5.6 0.0 copy-done.5
  5.6 0.0 copy-start.6
  5.6 1.3 %rotations.1 = (bf16[2,384,256]{2,1,0:T(8,128)(2,1)S(1)}, bf16[2,256,512]{2,1,0:T(8,128)(2,1)S(1)}) custom-call(s32[4,3]{1,0:T(4,128)S(1)} %copy-done.4, s32[3,24]{1,0:T(4,128)S(1)} %bitcast.4, bf16[2,2,32,32]{3,2,1,0:T(8,128)(2,1)S(1)} %copy-done.2, bf16[2,12,2,32,32]{4,3,2,1,0:T(8,128)(2,1)S(1)} %copy-done), custom_call_target="tpu_custom_call" | custom-call | flops 2000000000 | bytes 6000000 | tf_op jit(solution)/shard_map/rotations/pallas_call | solution.py:244
  6.9 0.0 copy-start.3
  6.9 0.2 collective-permute-start.2
  7.2 1.7 %collective-permute-done = bf16[120,512]{1,0:T(8,128)(2,1)S(1)} collective-permute-done((bf16[120,512]{1,0:T(8,128)(2,1)S(1)}, bf16[120,512]{1,0:T(8,128)(2,1)S(1)}, u32[]{:S(2)}, u32[]{:S(2)}) %collective-permute-start) | collective-permute-done | bytes 122912 | tf_op jit(solution)/shard_map/ppermute | solution.py:275
  8.9 1.9 %collective-permute-start.5 = (bf16[120,512]{1,0:T(8,128)(2,1)S(1)}, bf16[120,512]{1,0:T(8,128)(2,1)S(1)}, u32[]{:S(2)}, u32[]{:S(2)}) collective-permute-start(bf16[120,512]{1,0:T(8,128)(2,1)S(1)} %add_convert_fusion.1.refs_0_), channel_id=1, source_target_pairs={{0,4},{4,0},{8,12},{12,8},{1,5},{5,1},{9,13},{13,9},{2,6},{6,2},{1... | collective-permute-start | bytes 368648 | tf_op jit(solution)/shard_map/ppermute | solution.py:287
  10.8 2.6 %collective-permute-start.3 = (bf16[120,512]{1,0:T(8,128)(2,1)S(1)}, bf16[120,512]{1,0:T(8,128)(2,1)S(1)}, u32[]{:S(2)}, u32[]{:S(2)}) collective-permute-start(bf16[120,512]{1,0:T(8,128)(2,1)S(1)} %add_convert_fusion.1.refs_0_), channel_id=1, source_target_pairs={{0,8},{4,12},{8,0},{12,4},{1,9},{5,13},{9,1},{13,5},{2,10},{6,14},... | collective-permute-start | bytes 368648 | tf_op jit(solution)/shard_map/ppermute | solution.py:287
  13.4 0.0 collective-permute-done.2
  13.4 0.0 collective-permute-done.1
  13.5 1.2 %collective-permute-start.4 = (bf16[120,512]{1,0:T(8,128)(2,1)S(1)}, bf16[120,512]{1,0:T(8,128)(2,1)S(1)}, u32[]{:S(2)}, u32[]{:S(2)}) collective-permute-start(bf16[120,512]{1,0:T(8,128)(2,1)S(1)} %add_convert_fusion.refs_1_), channel_id=1, source_target_pairs={{0,8},{4,12},{8,0},{12,4},{1,9},{5,13},{9,1},{13,5},{2,10},{6,14},... | collective-permute-start | bytes 368648 | tf_op jit(solution)/shard_map/ppermute | solution.py:287
  14.7 0.0 copy-done.6
  14.7 0.1 copy.12.modes_ref
  14.8 1.6 %collective-permute-start.6 = (bf16[120,512]{1,0:T(8,128)(2,1)S(1)}, bf16[120,512]{1,0:T(8,128)(2,1)S(1)}, u32[]{:S(2)}, u32[]{:S(2)}) collective-permute-start(bf16[120,512]{1,0:T(8,128)(2,1)S(1)} %add_convert_fusion.refs_1_), channel_id=1, source_target_pairs={{0,4},{4,0},{8,12},{12,8},{1,5},{5,1},{9,13},{13,9},{2,6},{6,2},{1... | collective-permute-start | bytes 368648 | tf_op jit(solution)/shard_map/ppermute | solution.py:287
  16.4 0.0 collective-permute-done.5.refs_4_
  16.4 5.1 %collective-permute-done.3.refs_2_ = bf16[120,512]{1,0:T(8,128)(2,1)S(1)} collective-permute-done((bf16[120,512]{1,0:T(8,128)(2,1)S(1)}, bf16[120,512]{1,0:T(8,128)(2,1)S(1)}, u32[]{:S(2)}, u32[]{:S(2)}) %collective-permute-start.3) | collective-permute-done | bytes 122912 | tf_op jit(solution)/shard_map/ppermute | solution.py:287
  21.5 0.2 collective-permute-start.7
  21.7 2.0 %collective-permute-done.4.refs_3_ = bf16[120,512]{1,0:T(8,128)(2,1)S(1)} collective-permute-done((bf16[120,512]{1,0:T(8,128)(2,1)S(1)}, bf16[120,512]{1,0:T(8,128)(2,1)S(1)}, u32[]{:S(2)}, u32[]{:S(2)}) %collective-permute-start.4) | collective-permute-done | bytes 122912 | tf_op jit(solution)/shard_map/ppermute | solution.py:287
  23.7 0.0 collective-permute-start.8
  23.7 0.0 copy-done.3
  23.7 0.7 %mode_rotation.1 = (bf16[2,12,128,128]{3,2,1,0:T(8,128)(2,1)S(1)}, f32[12,64,1]{2,1,0:T(8,128)S(1)}) custom-call(bf16[2,12,60,60]{3,2,1,0:T(8,128)(2,1)S(1)} %copy.12.modes_ref, f32[12,60]{1,0:T(8,128)S(1)} %copy-done.3), custom_call_target="tpu_custom_call" | custom-call | flops 2000000000 | bytes 6000000 | tf_op jit(solution)/shard_map/mode_rotation/pallas_call | solution.py:257
  24.4 0.0 collective-permute-done.6.refs_5_
  24.4 1.0 %lift.2.early_ref = bf16[192,4096]{1,0:T(8,128)(2,1)S(1)} custom-call(bf16[2,256,512]{2,1,0:T(8,128)(2,1)S(1)} %get-tuple-element.22.a_ref, bf16[120,512]{1,0:T(8,128)(2,1)S(1)} %add_convert_fusion.1.refs_0_, bf16[120,512]{1,0:T(8,128)(2,1)S(1)} %add_convert_fusion.refs_1_, bf16[120,512]{1,0:T(8,128)(2,1)S(1)} %collective-permute-done.3.refs_2_, ...), custom_call_target="tpu_custom_call" | custom-call | flops 1000000000 | bytes 3000000 | tf_op jit(solution)/shard_map/lift/pallas_call | solution.py:298
  25.4 0.1 collective-permute-start.9
  25.5 1.6 %collective-permute-done.7.refs_0_ = bf16[120,512]{1,0:T(8,128)(2,1)S(1)} collective-permute-done((bf16[120,512]{1,0:T(8,128)(2,1)S(1)}, bf16[120,512]{1,0:T(8,128)(2,1)S(1)}, u32[]{:S(2)}, u32[]{:S(2)}) %collective-permute-start.7) | collective-permute-done | bytes 122912 | tf_op jit(solution)/shard_map/ppermute | solution.py:291
  27.1 1.9 %collective-permute-done.8.refs_1_ = bf16[120,512]{1,0:T(8,128)(2,1)S(1)} collective-permute-done((bf16[120,512]{1,0:T(8,128)(2,1)S(1)}, bf16[120,512]{1,0:T(8,128)(2,1)S(1)}, u32[]{:S(2)}, u32[]{:S(2)}) %collective-permute-start.8) | collective-permute-done | bytes 122912 | tf_op jit(solution)/shard_map/ppermute | solution.py:291
  29.0 0.5 %lift.3.late_ref = bf16[64,4096]{1,0:T(8,128)(2,1)S(1)} custom-call(bf16[2,256,512]{2,1,0:T(8,128)(2,1)S(1)} %get-tuple-element.22.a_ref, bf16[120,512]{1,0:T(8,128)(2,1)S(1)} %collective-permute-done.7.refs_0_, bf16[120,512]{1,0:T(8,128)(2,1)S(1)} %collective-permute-done.8.refs_1_), custom_call_target="tpu_custom_call" | custom-call | flops 1000000000 | bytes 3000000 | tf_op jit(solution)/shard_map/lift/pallas_call | solution.py:298
  29.5 0.1 collective-permute-start.10
  29.6 2.3 %coupling.2 = (bf16[12,60,1024]{2,1,0:T(8,128)(2,1)S(1)}, f32[1,1024]{1,0:T(1,128)S(1)}) custom-call(bf16[192,4096]{1,0:T(8,128)(2,1)S(1)} %lift.2.early_ref, bf16[64,4096]{1,0:T(8,128)(2,1)S(1)} %lift.3.late_ref, bf16[2,384,256]{2,1,0:T(8,128)(2,1)S(1)} %get-tuple-element.29.l_ref, bf16[2,12,128,128]{3,2,1,0:T(8,128)(2,1)S(1)} %get-tuple-element.30.d_ref, ...), custom_call_target="tpu_custom_call" | custom-call | flops 40000000000 | bytes 120000000 | tf_op jit(solution)/shard_map/coupling/pallas_call | solution.py:312
  31.8 0.0 collective-permute-done.10.late_ref
  31.8 0.0 collective-permute-done.9.early_ref
  31.9 2.3 %coupling.3 = (bf16[12,60,1024]{2,1,0:T(8,128)(2,1)S(1)}, f32[1,1024]{1,0:T(1,128)S(1)}) custom-call(bf16[192,4096]{1,0:T(8,128)(2,1)S(1)} %collective-permute-done.9.early_ref, bf16[64,4096]{1,0:T(8,128)(2,1)S(1)} %collective-permute-done.10.late_ref, bf16[2,384,256]{2,1,0:T(8,128)(2,1)S(1)} %get-tuple-element.29.l_ref, ...), custom_call_target="tpu_custom_call" | custom-call | flops 40000000000 | bytes 120000000 | tf_op jit(solution)/shard_map/coupling/pallas_call | solution.py:312
  34.1 0.3 collective-permute-start.12
  34.4 1.6 %collective-permute-start.13 = (f32[2,1024]{1,0:T(2,128)S(1)}, f32[2,1024]{1,0:T(2,128)S(1)}, u32[]{:S(2)}, u32[]{:S(2)}) collective-permute-start(f32[2,1024]{1,0:T(2,128)S(1)} %maximum_select_fusion), channel_id=1, source_target_pairs={{0,5},{1,4},{4,1},{5,0},{8,13},{9,12},{12,9},{13,8},{2,7},{3,6},{6... | collective-permute-start | bytes 24584 | tf_op jit(solution)/shard_map/ppermute | solution.py:360
  36.1 0.3 collective-permute-start.11
  36.4 1.5 %order.2.refs_0_ = bf16[12,60,2,1024]{3,2,1,0:T(2,128)(2,1)} custom-call(bf16[12,60,1024]{2,1,0:T(8,128)(2,1)S(1)} %get-tuple-element.32.first_ref, bf16[12,60,1024]{2,1,0:T(8,128)(2,1)S(1)} %get-tuple-element.33.second_ref), custom_call_target="tpu_custom_call" | custom-call | flops 2000000000 | bytes 6000000 | tf_op jit(solution)/shard_map/order/pallas_call | solution.py:342
  37.9 0.0 collective-permute-done.12
  37.9 0.0 collective-permute-done.13
  37.9 0.0 collective-permute-done.11
  37.9 3.0 %collective-permute-start.14 = (f32[2,1024]{1,0:T(2,128)S(1)}, f32[2,1024]{1,0:T(2,128)S(1)}, u32[]{:S(2)}, u32[]{:S(2)}) collective-permute-start(f32[2,1024]{1,0:T(2,128)S(1)} %add_add_fusion), channel_id=1, source_target_pairs={{0,8},{4,12},{8,0},{12,4},{1,9},{5,13},{9,1},{13,5},{2,10},{6,14},... | collective-permute-start | bytes 24584 | tf_op jit(solution)/shard_map/ppermute | solution.py:365
  41.0 1.2 %order.3 = bf16[12,60,2,1024]{3,2,1,0:T(2,128)(2,1)} custom-call(bf16[12,60,1024]{2,1,0:T(8,128)(2,1)S(1)} %get-tuple-element.32.first_ref, bf16[12,60,1024]{2,1,0:T(8,128)(2,1)S(1)} %get-tuple-element.33.second_ref, bf16[12,60,2,1024]{3,2,1,0:T(2,128)(2,1)} %order.2.refs_0_), custom_call_target="tpu_custom_call", output_to_operand_aliasing={{}: (2, {})} | custom-call | flops 2000000000 | bytes 6000000 | tf_op jit(solution)/shard_map/order/pallas_call | solution.py:342
  42.2 0.4 %collective-permute-done.14 = f32[2,1024]{1,0:T(2,128)S(1)} collective-permute-done((f32[2,1024]{1,0:T(2,128)S(1)}, f32[2,1024]{1,0:T(2,128)S(1)}, u32[]{:S(2)}, u32[]{:S(2)}) %collective-permute-start.14) | collective-permute-done | bytes 8224 | tf_op jit(solution)/shard_map/ppermute | solution.py:365
  42.6 0.6 %add.23 = f32[2,1024]{1,0:T(2,128)} add(f32[2,1024]{1,0:T(2,128)S(1)} %add_add_fusion, f32[2,1024]{1,0:T(2,128)S(1)} %collective-permute-done.14) | non-fusion elementwise | flops 2048 | bytes 24576 | tf_op jit(solution)/shard_map/add | solution.py:365
  (4 shorter events, 0.1 us)
Async XLA Ops:
  1.3 0.9 %copy-start.1 = (bf16[2,1,2,30,1024]{4,2,3,1,0:T(2,128)(2,1)S(1)}, bf16[2,1,2,30,1024]{4,2,3,1,0:T(2,128)(2,1)}, u32[]{:S(2)}) copy-start(bf16[2,1,2,30,1024]{4,2,3,1,0:T(2,128)(2,1)} %param.9) | copy-start | bytes 737284
  2.3 3.3 %copy-start = (bf16[2,12,2,32,32]{4,3,2,1,0:T(8,128)(2,1)S(1)}, bf16[2,12,2,32,32]{4,3,2,1,0:T(8,128)(2,1)}, u32[]{:S(2)}) copy-start(bf16[2,12,2,32,32]{4,3,2,1,0:T(8,128)(2,1)} %u_kq_ref.1) | copy-start | bytes 294916
  2.3 3.3 %copy-start.2 = (bf16[2,2,32,32]{3,2,1,0:T(8,128)(2,1)S(1)}, bf16[2,2,32,32]{3,2,1,0:T(8,128)(2,1)}, u32[]{:S(2)}) copy-start(bf16[2,2,32,32]{3,2,1,0:T(8,128)(2,1)} %u_k_ref.1) | copy-start | bytes 24580
  2.3 3.3 %copy-start.4 = (s32[4,3]{1,0:T(4,128)S(1)}, s32[4,3]{1,0:T(4,128)}, u32[]{:S(2)}) copy-start(s32[4,3]{1,0:T(4,128)} %r_ref.1) | copy-start | bytes 148
  2.3 3.3 %copy-start.5 = (s32[24,3]{0,1:T(4,128)S(1)}, s32[24,3]{0,1:T(4,128)}, u32[]{:S(2)}) copy-start(s32[24,3]{0,1:T(4,128)} %param.13) | copy-start | bytes 868
  2.6 6.3 %collective-permute-start = (bf16[120,512]{1,0:T(8,128)(2,1)S(1)}, bf16[120,512]{1,0:T(8,128)(2,1)S(1)}, u32[]{:S(2)}, u32[]{:S(2)}) collective-permute-start(bf16[120,512]{1,0:T(8,128)(2,1)S(1)} %get-tuple-element.24), channel_id=1, source_target_pairs={{0,2},{2,0},{1,3},{3,1},{4,6},{6,4},{5,7},{7,5},{8,10},{10,8},{9,1... | collective-permute-start | bytes 368648 | tf_op jit(solution)/shard_map/ppermute | solution.py:275
  5.6 7.8 %collective-permute-start.1 = (f32[120,512]{1,0:T(8,128)S(1)}, f32[120,512]{1,0:T(8,128)S(1)}, u32[]{:S(2)}, u32[]{:S(2)}) collective-permute-start(f32[120,512]{1,0:T(8,128)S(1)} %get-tuple-element.25), channel_id=1, source_target_pairs={{0,1},{1,0},{2,3},{3,2},{4,5},{5,4},{6,7},{7,6},{8,9},{9,8},{10,11... | collective-permute-start | bytes 737288 | tf_op jit(solution)/shard_map/ppermute | solution.py:270
  5.6 9.0 %copy-start.6 = (bf16[2,12,60,60]{3,0,2,1:T(2,128)(2,1)S(1)}, bf16[2,12,60,60]{3,0,2,1:T(2,128)(2,1)}, u32[]{:S(2)}) copy-start(bf16[2,12,60,60]{3,0,2,1:T(2,128)(2,1)} %param.16) | copy-start | bytes 518404
  6.9 16.8 %copy-start.3 = (f32[12,60]{1,0:T(8,128)S(1)}, f32[12,60]{1,0:T(8,128)}, u32[]{:S(2)}) copy-start(f32[12,60]{1,0:T(8,128)} %weights_ref.1) | copy-start | bytes 8644
  6.9 6.5 %collective-permute-start.2 = (bf16[120,512]{1,0:T(8,128)(2,1)S(1)}, bf16[120,512]{1,0:T(8,128)(2,1)S(1)}, u32[]{:S(2)}, u32[]{:S(2)}) collective-permute-start(bf16[120,512]{1,0:T(8,128)(2,1)S(1)} %get-tuple-element.27), channel_id=1, source_target_pairs={{0,3},{1,2},{2,1},{3,0},{4,7},{5,6},{6,5},{7,4},{8,11},{9,10},{10,... | collective-permute-start | bytes 368648 | tf_op jit(solution)/shard_map/ppermute | solution.py:277
  8.9 7.5 %collective-permute-start.5 = (bf16[120,512]{1,0:T(8,128)(2,1)S(1)}, bf16[120,512]{1,0:T(8,128)(2,1)S(1)}, u32[]{:S(2)}, u32[]{:S(2)}) collective-permute-start(bf16[120,512]{1,0:T(8,128)(2,1)S(1)} %add_convert_fusion.1.refs_0_), channel_id=1, source_target_pairs={{0,4},{4,0},{8,12},{12,8},{1,5},{5,1},{9,13},{13,9},{2,6},{6,2},{1... | collective-permute-start | bytes 368648 | tf_op jit(solution)/shard_map/ppermute | solution.py:287
  10.8 10.7 %collective-permute-start.3 = (bf16[120,512]{1,0:T(8,128)(2,1)S(1)}, bf16[120,512]{1,0:T(8,128)(2,1)S(1)}, u32[]{:S(2)}, u32[]{:S(2)}) collective-permute-start(bf16[120,512]{1,0:T(8,128)(2,1)S(1)} %add_convert_fusion.1.refs_0_), channel_id=1, source_target_pairs={{0,8},{4,12},{8,0},{12,4},{1,9},{5,13},{9,1},{13,5},{2,10},{6,14},... | collective-permute-start | bytes 368648 | tf_op jit(solution)/shard_map/ppermute | solution.py:287
  13.5 10.2 %collective-permute-start.4 = (bf16[120,512]{1,0:T(8,128)(2,1)S(1)}, bf16[120,512]{1,0:T(8,128)(2,1)S(1)}, u32[]{:S(2)}, u32[]{:S(2)}) collective-permute-start(bf16[120,512]{1,0:T(8,128)(2,1)S(1)} %add_convert_fusion.refs_1_), channel_id=1, source_target_pairs={{0,8},{4,12},{8,0},{12,4},{1,9},{5,13},{9,1},{13,5},{2,10},{6,14},... | collective-permute-start | bytes 368648 | tf_op jit(solution)/shard_map/ppermute | solution.py:287
  14.8 9.6 %collective-permute-start.6 = (bf16[120,512]{1,0:T(8,128)(2,1)S(1)}, bf16[120,512]{1,0:T(8,128)(2,1)S(1)}, u32[]{:S(2)}, u32[]{:S(2)}) collective-permute-start(bf16[120,512]{1,0:T(8,128)(2,1)S(1)} %add_convert_fusion.refs_1_), channel_id=1, source_target_pairs={{0,4},{4,0},{8,12},{12,8},{1,5},{5,1},{9,13},{13,9},{2,6},{6,2},{1... | collective-permute-start | bytes 368648 | tf_op jit(solution)/shard_map/ppermute | solution.py:287
  21.5 5.6 %collective-permute-start.7 = (bf16[120,512]{1,0:T(8,128)(2,1)S(1)}, bf16[120,512]{1,0:T(8,128)(2,1)S(1)}, u32[]{:S(2)}, u32[]{:S(2)}) collective-permute-start(bf16[120,512]{1,0:T(8,128)(2,1)S(1)} %collective-permute-done.3.refs_2_), channel_id=1, source_target_pairs={{0,4},{4,0},{8,12},{12,8},{1,5},{5,1},{9,13},{13,9},{2,6},{6,2},{1... | collective-permute-start | bytes 368648 | tf_op jit(solution)/shard_map/ppermute | solution.py:291
  23.7 5.3 %collective-permute-start.8 = (bf16[120,512]{1,0:T(8,128)(2,1)S(1)}, bf16[120,512]{1,0:T(8,128)(2,1)S(1)}, u32[]{:S(2)}, u32[]{:S(2)}) collective-permute-start(bf16[120,512]{1,0:T(8,128)(2,1)S(1)} %collective-permute-done.4.refs_3_), channel_id=1, source_target_pairs={{0,4},{4,0},{8,12},{12,8},{1,5},{5,1},{9,13},{13,9},{2,6},{6,2},{1... | collective-permute-start | bytes 368648 | tf_op jit(solution)/shard_map/ppermute | solution.py:291
  25.4 6.4 %collective-permute-start.9 = (bf16[192,4096]{1,0:T(8,128)(2,1)S(1)}, bf16[192,4096]{1,0:T(8,128)(2,1)S(1)}, u32[]{:S(2)}, u32[]{:S(2)}) collective-permute-start(bf16[192,4096]{1,0:T(8,128)(2,1)S(1)} %lift.2.early_ref), channel_id=1, source_target_pairs={{0,1},{1,0},{2,3},{3,2},{4,5},{5,4},{6,7},{7,6},{8,9},{9,8},{10,11... | collective-permute-start | bytes 4718600 | tf_op jit(solution)/shard_map/ppermute | solution.py:308
  29.5 2.3 %collective-permute-start.10 = (bf16[64,4096]{1,0:T(8,128)(2,1)S(1)}, bf16[64,4096]{1,0:T(8,128)(2,1)S(1)}, u32[]{:S(2)}, u32[]{:S(2)}) collective-permute-start(bf16[64,4096]{1,0:T(8,128)(2,1)S(1)} %lift.3.late_ref), channel_id=1, source_target_pairs={{0,1},{1,0},{2,3},{3,2},{4,5},{5,4},{6,7},{7,6},{8,9},{9,8},{10,11... | collective-permute-start | bytes 1572872 | tf_op jit(solution)/shard_map/ppermute | solution.py:308
  34.1 3.7 %collective-permute-start.12 = (f32[2,1024]{1,0:T(2,128)S(1)}, f32[2,1024]{1,0:T(2,128)S(1)}, u32[]{:S(2)}, u32[]{:S(2)}) collective-permute-start(f32[2,1024]{1,0:T(2,128)S(1)} %maximum_select_fusion), channel_id=1, source_target_pairs={{0,4},{4,0},{8,12},{12,8},{1,5},{5,1},{9,13},{13,9},{2,6},{6,2},{1... | collective-permute-start | bytes 24584 | tf_op jit(solution)/shard_map/ppermute | solution.py:359
  34.4 3.5 %collective-permute-start.13 = (f32[2,1024]{1,0:T(2,128)S(1)}, f32[2,1024]{1,0:T(2,128)S(1)}, u32[]{:S(2)}, u32[]{:S(2)}) collective-permute-start(f32[2,1024]{1,0:T(2,128)S(1)} %maximum_select_fusion), channel_id=1, source_target_pairs={{0,5},{1,4},{4,1},{5,0},{8,13},{9,12},{12,9},{13,8},{2,7},{3,6},{6... | collective-permute-start | bytes 24584 | tf_op jit(solution)/shard_map/ppermute | solution.py:360
  36.1 1.8 %collective-permute-start.11 = (f32[2,1024]{1,0:T(2,128)S(1)}, f32[2,1024]{1,0:T(2,128)S(1)}, u32[]{:S(2)}, u32[]{:S(2)}) collective-permute-start(f32[2,1024]{1,0:T(2,128)S(1)} %maximum_select_fusion), channel_id=1, source_target_pairs={{0,1},{1,0},{2,3},{3,2},{4,5},{5,4},{6,7},{7,6},{8,9},{9,8},{10,11... | collective-permute-start | bytes 24584 | tf_op jit(solution)/shard_map/ppermute | solution.py:361
  37.9 4.7 %collective-permute-start.14 = (f32[2,1024]{1,0:T(2,128)S(1)}, f32[2,1024]{1,0:T(2,128)S(1)}, u32[]{:S(2)}, u32[]{:S(2)}) collective-permute-start(f32[2,1024]{1,0:T(2,128)S(1)} %add_add_fusion), channel_id=1, source_target_pairs={{0,8},{4,12},{8,0},{12,4},{1,9},{5,13},{9,1},{13,5},{2,10},{6,14},... | collective-permute-start | bytes 24584 | tf_op jit(solution)/shard_map/ppermute | solution.py:365
